TPU v7x, 32 devices: a whole 2x2x4 slice. The times are simulated.
32 devices in a mesh: groups: 2 (over y), tm: 8 (over z, x), height: 2 (over core).
Axes of the slice: x: 2, y: 2, z: 4, core: 2. Of those that a mesh axis runs over, the one named last changes fastest.
Arguments:
- video: bfloat16 [32, 8, 64, 256], P(('groups', 'tm'), 'height'), parts along dimension 0, may hold values from -6 to 6
- block_ids: int32 [32], P('groups'), parts along dimension 0, may hold values from 0 to 4, never falling along the last dimension, each value on 1 to 4 neighbouring positions
- conv_weight: bfloat16 [3, 3, 3, 256, 256], replicated, may hold values from -0.078125 to 0.078125
- w_query: bfloat16 [256, 256], replicated, may hold values from -4 to 4
- w_key: bfloat16 [256, 256], replicated, may hold values from -4 to 4
- w_value: bfloat16 [256, 256], replicated, may hold values from -0.375 to 0.375
- w_output: bfloat16 [256, 256], replicated, may hold values from -0.375 to 0.375
Outputs:
- encoded: bfloat16 [32, 8, 64, 256], P(('groups', 'tm'), 'height'), parts along dimension 0
There are 2 independent parts, one for each index of `groups`. A program takes and returns all parts, laid end to end along the dimension named above; an argument that names none is the same for every part. Nothing has to cross between parts.
Inputs may be any that keep to these rules, and one draw needn't show every extreme that they name: `block_ids`: block ids never fall along the frames and start at 0; each block has 1 to 4 frames, and some block has exactly 4.
All inputs are finite; a program needn't handle non-finite values.
Results may differ from a plain program's by a relative error of at most 0.012.
Values may be sent and summed in bfloat16 or wider, within the bound.
No kernel may reach another device: no remote copies, remote signals or barrier semaphores. Data moves between devices by JAX's collectives and lax.ppermute only.
A program may use at most 64 MiB of HBM per device.

v0:
```python
import jax
import jax.numpy as jnp
from jax import lax
from jax.sharding import PartitionSpec as P

HD = 64


def passed_along(value, axis, by):
    count = lax.axis_size(axis)
    pairs = [(i, i + by) for i in range(count) if 0 <= i + by < count]
    return lax.ppermute(value, axis, pairs)


def with_halo(value, sides, width):
    for axis, dim in sides:
        count, length = (lax.axis_size(axis), value.shape[dim])
        up = [(i, (i + 1) % count) for i in range(count - 1)]
        down = [(j, i) for i, j in up]
        last = lax.slice_in_dim(value, length - width, length, axis=dim)
        first = lax.slice_in_dim(value, 0, width, axis=dim)
        before = lax.ppermute(last, axis, up)
        after = lax.ppermute(first, axis, down)
        value = jnp.concatenate([before, value, after], axis=dim)
    return value


def normalize(values):
    wide = values.astype(jnp.float32)
    return wide * lax.rsqrt(jnp.mean(wide * wide, axis=-1, keepdims=True) + 1e-06)


def project(flat, weight):
    return jnp.dot(flat, weight, preferred_element_type=jnp.float32).astype(jnp.bfloat16)


def per_device(video, block_ids, conv_weight, w_query, w_key, w_value, w_output):
    count, rows, cols, chans = video.shape
    heads = chans // HD
    activated = jax.nn.silu(normalize(video)).astype(jnp.bfloat16)
    cached = passed_along(activated, "tm", 1)
    extended = jnp.concatenate([cached, activated], axis=0)
    rimmed = with_halo(extended, (("height", 1),), 1)
    padded = jnp.pad(rimmed, ((0, 0), (0, 0), (1, 1), (0, 0)))
    total = jnp.zeros((count * rows * cols, chans), jnp.float32)
    for tap_t in range(3):
        for tap_r in range(3):
            for tap_w in range(3):
                window = padded[
                    tap_t : tap_t + count, tap_r : tap_r + rows, tap_w : tap_w + cols
                ].reshape(-1, chans)
                total = total + jnp.dot(
                    window, conv_weight[tap_t, tap_r, tap_w], preferred_element_type=jnp.float32
                )
    hidden = (video.astype(jnp.float32) + total.reshape(video.shape)).astype(jnp.bfloat16)
    normed = normalize(hidden).astype(jnp.bfloat16).reshape(-1, chans)
    pixels = rows * cols
    tm_count = lax.axis_size("tm")
    per_dev = -(-pixels // tm_count)
    padded_pix = per_dev * tm_count
    grid = normed.reshape(count, pixels, chans)
    grid = grid.reshape(count, tm_count, per_dev, chans)
    piece = lax.all_to_all(grid, "tm", split_axis=1, concat_axis=0, tiled=True)
    frames_all = piece.shape[0]
    several = piece.shape[2]
    flat = piece.reshape(-1, chans)
    query_p = project(flat, w_query).reshape(frames_all, several, heads, HD)
    keys_p = project(flat, w_key).reshape(frames_all, several, heads, HD)
    vals_p = project(flat, w_value).reshape(frames_all, several, heads, HD)
    order = jnp.arange(frames_all, dtype=jnp.int32)
    permit = (order[None, :] <= order[:, None]) & (block_ids[None, :] >= block_ids[:, None] - 1)
    scores_p = jnp.einsum(
        "fphd,kphd->phfk", query_p, keys_p, preferred_element_type=jnp.float32
    ) * HD ** (-0.5)
    scores_p = jnp.where(permit[None, None], scores_p, -1e30)
    top_p = jnp.max(scores_p, axis=-1, keepdims=True)
    expo_p = jnp.exp(scores_p - top_p)
    weights_p = (expo_p / jnp.sum(expo_p, axis=-1, keepdims=True)).astype(jnp.bfloat16)
    result = jnp.einsum("phfk,kphd->fphd", weights_p, vals_p, preferred_element_type=jnp.float32)
    gone = result.astype(jnp.bfloat16).reshape(frames_all, 1, several, chans)
    back = lax.all_to_all(gone, "tm", split_axis=0, concat_axis=1, tiled=True)
    attended = back.reshape(count, padded_pix, chans).reshape(-1, chans)
    mixed = hidden.astype(jnp.float32).reshape(-1, chans) + jnp.dot(
        attended, w_output, preferred_element_type=jnp.float32
    )
    return mixed.astype(jnp.bfloat16).reshape(video.shape)


def solution(mesh):
    placed = (P(("groups", "tm"), "height", None, None), P("groups"), P(), P(), P(), P(), P())
    return jax.shard_map(
        per_device,
        mesh=mesh,
        in_specs=placed,
        out_specs=P(("groups", "tm"), "height", None, None),
        check_vma=False,
    )
```

profile of v0, /device:TPU:0, one launch (start us, length us, event | category | flops | bytes accessed | tf_op | source)
XLA Modules:
  0.0 62.3 jit_solution(18016009349427102440)
XLA Ops:
  0.0 1.1 %fusion.18 = f32[2,4,64]{2,1,0:T(4,128)S(1)} fusion(bf16[2,4,64,256]{3,2,1,0:T(8,128)(2,1)} %param.7), kind=kLoop, calls=%fused_computation.58 | loop fusion | flops 392704 | bytes 264192 | tf_op jit(solution)/shard_map/reduce_sum | solution.py:30
  1.1 1.2 %fusion.17 = bf16[2,4,64,256]{3,2,1,0:T(8,128)(2,1)S(1)} fusion(bf16[2,4,64,256]{3,2,1,0:T(8,128)(2,1)} %param.7, f32[2,4,64]{2,1,0:T(4,128)S(1)} %add_rsqrt_fusion.1), kind=kLoop, calls=%fused_computation.57 | loop fusion | flops 917504 | bytes 526336 | tf_op jit(solution)/shard_map/convert_element_type | solution.py:40
  2.3 4.9 %collective-permute-start = (bf16[2,4,64,256]{3,2,1,0:T(8,128)(2,1)S(1)}, bf16[2,4,64,256]{3,2,1,0:T(8,128)(2,1)S(1)}, u32[]{:S(2)}, u32[]{:S(2)}) collective-permute-start(bf16[2,4,64,256]{3,2,1,0:T(8,128)(2,1)S(1)} %fusion.17), channel_id=1, source_target_pairs={{0,2},{2,4},{4,6},{6,8},{8,10},{10,12},{12,14},{1,3},{3,5},{5,7},{... | collective-permute-start | bytes 786440 | tf_op jit(solution)/shard_map/ppermute | solution.py:12
  7.2 5.5 %collective-permute-done = bf16[2,4,64,256]{3,2,1,0:T(8,128)(2,1)S(1)} collective-permute-done((bf16[2,4,64,256]{3,2,1,0:T(8,128)(2,1)S(1)}, bf16[2,4,64,256]{3,2,1,0:T(8,128)(2,1)S(1)}, u32[]{:S(2)}, u32[]{:S(2)}) %collective-permute-start) | collective-permute-done | bytes 262176 | tf_op jit(solution)/shard_map/ppermute | solution.py:12
  12.7 1.3 %collective-permute-start.1 = (bf16[4,1,64,256]{3,2,1,0:T(8,128)(2,1)S(1)}, bf16[4,1,64,256]{3,2,1,0:T(8,128)(2,1)S(1)}, u32[]{:S(2)}, u32[]{:S(2)}) collective-permute-start(bf16[4,1,64,256]{3,2,1,0:T(8,128)(2,1)S(1)} %get-tuple-element.33), channel_id=1, source_target_pairs={{0,1},{2,3},{4,5},{6,7},{8,9},{10,11},{12,13},{14,15},{16,17},{18,... | collective-permute-start | bytes 393224 | tf_op jit(solution)/shard_map/ppermute | solution.py:22
  14.1 1.3 %collective-permute-start.2 = (bf16[4,1,64,256]{3,2,1,0:T(8,128)(2,1)S(1)}, bf16[4,1,64,256]{3,2,1,0:T(8,128)(2,1)S(1)}, u32[]{:S(2)}, u32[]{:S(2)}) collective-permute-start(bf16[4,1,64,256]{3,2,1,0:T(8,128)(2,1)S(1)} %get-tuple-element.34), channel_id=1, source_target_pairs={{1,0},{3,2},{5,4},{7,6},{9,8},{11,10},{13,12},{15,14},{17,16},{19,... | collective-permute-start | bytes 393224 | tf_op jit(solution)/shard_map/ppermute | solution.py:23
  15.4 0.0 collective-permute-done.1
  15.4 1.9 %collective-permute-done.2 = bf16[4,1,64,256]{3,2,1,0:T(8,128)(2,1)S(1)} collective-permute-done((bf16[4,1,64,256]{3,2,1,0:T(8,128)(2,1)S(1)}, bf16[4,1,64,256]{3,2,1,0:T(8,128)(2,1)S(1)}, u32[]{:S(2)}, u32[]{:S(2)}) %collective-permute-start.2) | collective-permute-done | bytes 131104 | tf_op jit(solution)/shard_map/ppermute | solution.py:23
  17.3 0.5 select_maximum_fusion
  17.8 0.0 copy-start.1
  17.8 0.8 %fusion.84 = (bf16[2,4,64,256]{3,2,1,0:T(8,128)(2,1)S(1)}, bf16[2,4,64,256]{3,2,1,0:T(8,128)(2,1)S(1)}, bf16[2,4,64,256]{3,2,1,0:T(8,128)(2,1)S(1)}, bf16[2,4,64...) fusion(bf16[4,6,66,256]{3,2,1,0:T(8,128)(2,1)S(1)} %select_maxi, ...), kind=kLoop, calls=%fused_computation.132 | loop fusion | bytes 9437184 | tf_op jit(solution)/shard_map/slice | solution.py:49
  18.6 1.2 %copy-done.1 = bf16[3,3,3,256,256]{4,3,2,1,0:T(8,128)(2,1)S(1)} copy-done((bf16[3,3,3,256,256]{4,3,2,1,0:T(8,128)(2,1)S(1)}, bf16[3,3,3,256,256]{4,3,2,1,0:T(8,128)(2,1)}, u32[]{:S(2)}) %copy-start.1) | copy-done | bytes 3538968
  19.8 0.2 fusion.53
  20.0 0.2 fusion.47
  20.2 0.2 fusion.37
  20.5 0.1 pad_maximum_fusion
  20.6 0.2 fusion.85
  20.8 0.2 convolution_add_fusion.24
  21.0 0.2 convolution_add_fusion.23
  21.2 0.2 convolution_add_fusion.22
  21.4 0.2 fusion.7
  21.7 0.2 convolution_add_fusion.20
  21.9 0.2 convolution_add_fusion.19
  22.2 0.2 convolution_add_fusion.18
  22.4 0.2 convolution_add_fusion.17
  22.6 0.2 convolution_add_fusion.16
  22.9 0.2 convolution_add_fusion.15
  23.1 0.2 convolution_add_fusion.14
  23.3 0.2 fusion.6
  23.6 0.2 convolution_add_fusion.12
  23.8 0.2 convolution_add_fusion.11
  24.1 0.2 convolution_add_fusion.10
  24.3 0.2 convolution_add_fusion.9
  24.5 0.2 convolution_add_fusion.8
  24.8 0.2 convolution_add_fusion.7
  25.0 0.2 convolution_add_fusion.6
  25.2 0.0 copy-start.2
  25.2 0.2 convolution_add_fusion.5
  25.5 0.2 convolution_add_fusion.4
  25.7 0.0 copy-start.6
  25.7 0.2 convolution_add_fusion.3
  25.9 0.0 copy-start.3
  26.0 0.2 convolution_add_fusion.2
  26.2 0.0 copy-start.4
  26.2 0.2 convolution_add_fusion.1
  26.4 0.2 multiply_reduce_fusion
  26.6 0.1 multiply_convert_fusion
  26.8 0.7 %copy.32 = bf16[2,8,32,256]{3,2,0,1:T(8,128)(2,1)} copy(bf16[2,8,32,256]{3,2,1,0:T(8,128)(2,1)S(1)} %bitcast.170) | data formatting | bytes 524288 | tf_op jit(solution)/shard_map/reshape;reshape;reshape | solution.py:62
  27.5 6.8 %all-to-all-start = ((bf16[2,8,32,256]{3,2,0,1:T(8,128)(2,1)}), bf16[2,8,32,256]{3,2,0,1:T(8,128)(2,1)S(1)}, u32[]{:S(2)}, u32[]{:S(2)}) async-start(bf16[2,8,32,256]{3,2,0,1:T(8,128)(2,1)} %copy.32), calls=%async_computation | async-start | bytes 524288 | tf_op jit(solution)/shard_map/all_to_all | solution.py:63
  34.3 0.1 fusion.82
  34.3 9.1 %all-to-all-done = bf16[2,8,32,256]{3,2,0,1:T(8,128)(2,1)S(1)} async-done(((bf16[2,8,32,256]{3,2,0,1:T(8,128)(2,1)}), bf16[2,8,32,256]{3,2,0,1:T(8,128)(2,1)S(1)}, u32[]{:S(2)}, u32[]{:S(2)}) %all-to-all-start) | async-done | bytes 262176 | tf_op jit(solution)/shard_map/all_to_all | solution.py:63
  43.5 0.2 convolution_convert_fusion.2
  43.7 0.2 reshape.197
  44.0 0.2 convolution_convert_fusion.1
  44.2 0.2 reshape.198
  44.5 0.2 convolution_convert_fusion.3
  44.7 0.2 reshape.196
  44.9 2.0 %fusion.87 = (f32[32,4,16]{2,1,0:T(4,128)S(1)}, f32[32,4,16,16]{2,3,1,0:T(8,128)}) fusion(bf16[16,32,4,64]{3,2,1,0:T(4,128)(2,1)S(1)} %reshape.198, bf16[16,32,4,64]{3,2,1,0:T(4,128)(2,1)S(1)} %reshape.197, pred[16,16]{0,1:T(8,128)(4,1)S(1)} %fusion.82), kind=kOutput, calls=%fused_computation.135 | convolution fusion | flops 4325391 | bytes 663808 | tf_op jit(solution)/shard_map/sub | solution.py:77
  47.0 0.0 copy-start.5
  47.0 1.8 %fusion.5 = bf16[16,32,4,64]{3,0,2,1:T(8,128)(2,1)S(1)} fusion(f32[32,4,16,16]{2,3,1,0:T(8,128)} %get-tuple-element.36, bf16[16,32,4,64]{3,2,1,0:T(4,128)(2,1)S(1)} %reshape.196, f32[32,4,16]{2,1,0:T(4,128)S(1)} %get-tuple-element.35), kind=kOutput, calls=%fused_computation.9 | convolution fusion | flops 4390912 | bytes 663552 | tf_op jit(solution)/shard_map/phfk,kphd->fphd/dot_general | solution.py:79
  48.7 0.3 copy.37
  49.0 0.3 reshape.199
  49.3 11.9 %all_to_all.30 = bf16[16,1,32,256]{3,2,1,0:T(8,128)(2,1)S(1)} all-to-all(bf16[16,1,32,256]{3,2,1,0:T(8,128)(2,1)S(1)} %bitcast.171), channel_id=1, replica_groups=mesh['groups'=2,'tm'=8,'height'=2] {'tm'}, dimensions={0} | all-to-all | bytes 524288 | tf_op jit(solution)/shard_map/all_to_all | solution.py:81
  61.3 0.9 %fusion.8 = bf16[512,256]{1,0:T(8,128)(2,1)} fusion(f32[512,256]{1,0:T(8,128)S(1)} %bitcast.161, bf16[512,256]{1,0:T(8,128)(2,1)S(1)} %bitcast.194, bf16[256,256]{1,0:T(8,128)(2,1)S(1)} %copy-done.5), kind=kOutput, calls=%fused_computation.40 | convolution fusion | flops 67371008 | bytes 1179648 | tf_op jit(solution)/shard_map/dot_general | solution.py:83
  (13 shorter events, 0.1 us)
Async XLA Ops:
  0.0 43.5 %copy-start = (bf16[256,256]{1,0:T(8,128)(2,1)S(1)}, bf16[256,256]{1,0:T(8,128)(2,1)}, u32[]{:S(2)}) copy-start(bf16[256,256]{1,0:T(8,128)(2,1)} %param.10) | copy-start | bytes 393220
  2.3 10.4 %collective-permute-start = (bf16[2,4,64,256]{3,2,1,0:T(8,128)(2,1)S(1)}, bf16[2,4,64,256]{3,2,1,0:T(8,128)(2,1)S(1)}, u32[]{:S(2)}, u32[]{:S(2)}) collective-permute-start(bf16[2,4,64,256]{3,2,1,0:T(8,128)(2,1)S(1)} %fusion.17), channel_id=1, source_target_pairs={{0,2},{2,4},{4,6},{6,8},{8,10},{10,12},{12,14},{1,3},{3,5},{5,7},{... | collective-permute-start | bytes 786440 | tf_op jit(solution)/shard_map/ppermute | solution.py:12
  12.7 2.6 %collective-permute-start.1 = (bf16[4,1,64,256]{3,2,1,0:T(8,128)(2,1)S(1)}, bf16[4,1,64,256]{3,2,1,0:T(8,128)(2,1)S(1)}, u32[]{:S(2)}, u32[]{:S(2)}) collective-permute-start(bf16[4,1,64,256]{3,2,1,0:T(8,128)(2,1)S(1)} %get-tuple-element.33), channel_id=1, source_target_pairs={{0,1},{2,3},{4,5},{6,7},{8,9},{10,11},{12,13},{14,15},{16,17},{18,... | collective-permute-start | bytes 393224 | tf_op jit(solution)/shard_map/ppermute | solution.py:22
  14.1 3.2 %collective-permute-start.2 = (bf16[4,1,64,256]{3,2,1,0:T(8,128)(2,1)S(1)}, bf16[4,1,64,256]{3,2,1,0:T(8,128)(2,1)S(1)}, u32[]{:S(2)}, u32[]{:S(2)}) collective-permute-start(bf16[4,1,64,256]{3,2,1,0:T(8,128)(2,1)S(1)} %get-tuple-element.34), channel_id=1, source_target_pairs={{1,0},{3,2},{5,4},{7,6},{9,8},{11,10},{13,12},{15,14},{17,16},{19,... | collective-permute-start | bytes 393224 | tf_op jit(solution)/shard_map/ppermute | solution.py:23
  17.8 2.0 %copy-start.1 = (bf16[3,3,3,256,256]{4,3,2,1,0:T(8,128)(2,1)S(1)}, bf16[3,3,3,256,256]{4,3,2,1,0:T(8,128)(2,1)}, u32[]{:S(2)}) copy-start(bf16[3,3,3,256,256]{4,3,2,1,0:T(8,128)(2,1)} %param.9) | copy-start | bytes 10616836
  25.2 1.2 %copy-start.2 = (bf16[2,4,64,256]{3,2,1,0:T(8,128)(2,1)S(1)}, bf16[2,4,64,256]{3,2,1,0:T(8,128)(2,1)}, u32[]{:S(2)}) copy-start(bf16[2,4,64,256]{3,2,1,0:T(8,128)(2,1)} %param.7) | copy-start | bytes 786436
  25.7 8.6 %copy-start.6 = (s32[16]{0:T(128)S(1)}, s32[16]{0:T(128)}, u32[]{:S(2)}) copy-start(s32[16]{0:T(128)} %param.8) | copy-start | bytes 196
  25.9 18.0 %copy-start.3 = (bf16[256,256]{1,0:T(8,128)(2,1)S(1)}, bf16[256,256]{1,0:T(8,128)(2,1)}, u32[]{:S(2)}) copy-start(bf16[256,256]{1,0:T(8,128)(2,1)} %param.11) | copy-start | bytes 393220
  26.2 18.3 %copy-start.4 = (bf16[256,256]{1,0:T(8,128)(2,1)S(1)}, bf16[256,256]{1,0:T(8,128)(2,1)}, u32[]{:S(2)}) copy-start(bf16[256,256]{1,0:T(8,128)(2,1)} %param.12) | copy-start | bytes 393220
  27.5 16.0 %all-to-all-start = ((bf16[2,8,32,256]{3,2,0,1:T(8,128)(2,1)}), bf16[2,8,32,256]{3,2,0,1:T(8,128)(2,1)S(1)}, u32[]{:S(2)}, u32[]{:S(2)}) async-start(bf16[2,8,32,256]{3,2,0,1:T(8,128)(2,1)} %copy.32), calls=%async_computation | async-start | bytes 524288 | tf_op jit(solution)/shard_map/all_to_all | solution.py:63
  47.0 14.4 %copy-start.5 = (bf16[256,256]{1,0:T(8,128)(2,1)S(1)}, bf16[256,256]{1,0:T(8,128)(2,1)}, u32[]{:S(2)}) copy-start(bf16[256,256]{1,0:T(8,128)(2,1)} %param.13) | copy-start | bytes 393220
where the time goes:
time: 62.7 us; the launch traced here: 62.3 us
  waiting for transfers between devices  16.6 us (26%)
  starting transfers between devices  14.2 us (23%)
  blocking collectives  11.9 us (19%)
  matrix products  11.5 us (18%)
  local copies, waits for them, and re-layouts  4.25 us (7%)
  other arithmetic  3.32 us (5%)
    all_to_all x1, blocking collectives, per_device(): back = lax.all_to_all(gone, 'tm', split_axis=0, concat_axis=1, tiled=True)  11.9 us
    all_to_all x1, waiting for transfers between devices, per_device(): piece = lax.all_to_all(grid, 'tm', split_axis=1, concat_axis=0, tiled=True)  9.14 us
    all_to_all x1, starting transfers between devices, per_device(): piece = lax.all_to_all(grid, 'tm', split_axis=1, concat_axis=0, tiled=True)  6.77 us
    dot_general x27, matrix products, per_device(): jnp.dot(window, conv_weight[tap_t, tap_r, tap_w], preferred_element_type=...  6.16 us
    ppermute x1, waiting for transfers between devices, passed_along(): return lax.ppermute(value, axis, pairs)  5.53 us
    ppermute x1, starting transfers between devices, passed_along(): return lax.ppermute(value, axis, pairs)  4.86 us
    sub x1, matrix products, per_device(): expo_p = jnp.exp(scores_p - top_p)  2 us
    ppermute x1, waiting for transfers between devices, with_halo(): after = lax.ppermute(first, axis, down)  1.9 us
  transfers between devices with their start and end apart: 4, of which 3 were waited for; matrix products, arithmetic and copies ran while one was open for 0% of the time, Pallas kernels for 0%

commit v1 on v0

v1 whole, which is shorter than its diff:
```python
import functools

import jax
import jax.numpy as jnp
import numpy as np
from jax import lax
from jax.experimental import pallas as pl
from jax.experimental.pallas import tpu as pltpu
from jax.sharding import Mesh, PartitionSpec as P

HD = 64
BLOCK = 4
TAPS = 3
REACH = 2 * BLOCK - 1 + TAPS - 1
LANES = 128
VMEM = 40 * 2**20

bf16, f32 = jnp.bfloat16, jnp.float32


def get(ref, start, size, stride):
    return jnp.concatenate([ref[i, pl.ds(start, size, stride=stride), :] for i in range(ref.shape[0])], axis=1)


def put(ref, start, size, stride, value):
    for i in range(ref.shape[0]):
        ref[i, pl.ds(start, size, stride=stride), :] = value[:, i * LANES : (i + 1) * LANES]


def fill(ref, value):
    for i in range(ref.shape[0]):
        ref[i] = value[:, i * LANES : (i + 1) * LANES]


def scratch(rows, chans):
    return pltpu.VMEM((chans // LANES, rows, LANES), f32)


def pack_kernel(video, out, wide):
    count, rows, cols, chans = video.shape
    lines = count * rows
    fill(wide, video[...].reshape(lines * cols, chans).astype(f32))
    chunks = out.shape[0]
    span = out.shape[1] // lines
    own = span - 2
    pieces = 16 // lines

    def column(w):
        if 0 <= w < cols:
            return get(wide, w, lines, cols)
        return jnp.zeros((lines, chans), f32)

    for d in range(chunks):
        for k in range(0, span, pieces):
            tile = jnp.concatenate([column(d * own - 1 + k + i) for i in range(pieces)], axis=0)
            out[d, pl.ds(k * lines, 16), :] = tile.astype(bf16)


def unpack_kernel(packed, out, wide):
    count, rows, cols, chans = out.shape
    lines = count * rows
    fill(wide, packed[...].reshape(lines * cols, chans).astype(f32))
    for t in range(count):
        for r in range(rows):
            out[t, r] = get(wide, t * rows + r, cols, lines).astype(bf16)


def rms(wide):
    return wide * lax.rsqrt(jnp.mean(wide * wide, axis=-1, keepdims=True) + 1e-06)


def main_kernel(
    count, rows, ids, video, conv_weight, w_query, w_key, w_value, w_output, out,
    vid, act, grid, res,
):
    sources, halves, _, chans = video.shape
    owners = out.shape[0]
    lines = count * rows
    span = video.shape[2] // lines
    own = span - 2
    high = halves * rows
    frames = sources * count
    heads = chans // HD
    step = halves * span * lines
    back = halves * own * lines

    xs = video[...].reshape(-1, chans).astype(f32)
    fill(vid, xs)
    normal = rms(xs)
    fill(act, normal / (1.0 + jnp.exp(-normal)))

    def pixel(ref, w, r):
        half, line = divmod(r, rows)
        return [
            get(ref, (half * span + w) * lines + t * rows + line, sources, step)
            for t in range(count)
        ]

    first = lax.broadcasted_iota(jnp.int32, (sources, chans), 0) == 0

    def earlier(x):
        return jnp.where(first, 0.0, pltpu.roll(x, 1, 0))

    zero = jnp.zeros((frames, TAPS * chans), bf16)
    for w in range(span):
        grid[w, 0] = zero
        grid[w, high + 1] = zero
        for r in range(high):
            now = pixel(act, w, r)
            past = [earlier(x) for x in now]
            ordered = past + now
            for a in range(TAPS):
                shift = TAPS - 1 - a
                picked = [ordered[count + t - shift] for t in range(count)]
                grid[w, r + 1, :, a * chans : (a + 1) * chans] = jnp.concatenate(picked, 0).astype(bf16)

    area = high * frames
    row_at = lax.broadcasted_iota(jnp.int32, (area, area), 0)
    col_at = lax.broadcasted_iota(jnp.int32, (area, area), 1)

    def frame_of(at):
        place = at % frames
        return (place % sources) * count + place // sources

    row_t, col_t = frame_of(row_at), frame_of(col_at)

    def block_of(t):
        found = jnp.zeros(t.shape, jnp.int32)
        for s in range(frames):
            found = jnp.where(t == s, ids[s], found)
        return found

    row_b, col_b = block_of(row_t), block_of(col_t)
    permit = (row_at // frames == col_at // frames) & (col_t <= row_t) & (col_b >= row_b - 1)
    head_of = lax.broadcasted_iota(jnp.int32, (area, chans), 1) // HD

    for w in range(own):
        total = jnp.zeros((area, chans), f32)
        for e in range(TAPS):
            for b in range(TAPS):
                window = grid[w + e, b : b + high].reshape(area, TAPS * chans)
                weight = jnp.concatenate([conv_weight[a, b, e] for a in range(TAPS)], axis=0)
                total = total + jnp.dot(window, weight, preferred_element_type=f32)
        shown = jnp.concatenate([x for r in range(high) for x in pixel(vid, w + 1, r)], axis=0)
        hidden = (shown + total).astype(bf16).astype(f32)
        normed = rms(hidden).astype(bf16)
        query = jnp.dot(normed, w_query[...], preferred_element_type=f32).astype(bf16)
        keys = jnp.dot(normed, w_key[...], preferred_element_type=f32).astype(bf16)
        values = jnp.dot(normed, w_value[...], preferred_element_type=f32).astype(bf16)
        attended = jnp.zeros((area, chans), f32)
        for h in range(heads):
            single = jnp.where(head_of == h, query, jnp.zeros((), bf16))
            scores = lax.dot_general(single, keys, (((1,), (1,)), ((), ())), preferred_element_type=f32)
            scores = jnp.where(permit, scores * HD ** (-0.5), -1e30)
            expo = jnp.exp(scores - jnp.max(scores, axis=-1, keepdims=True))
            weights = (expo / jnp.sum(expo, axis=-1, keepdims=True)).astype(bf16)
            mixed = jnp.dot(weights, values, preferred_element_type=f32)
            attended = jnp.where(head_of == h, mixed, attended)
        encoded = hidden + jnp.dot(attended.astype(bf16), w_output[...], preferred_element_type=f32)
        for r in range(high):
            half, line = divmod(r, rows)
            for t in range(count):
                start = (r * count + t + 1) * sources - owners
                place = (half * own + w) * lines + t * rows + line
                put(res, place, owners, back, encoded[start : start + owners])
    done = jnp.concatenate([res[i] for i in range(res.shape[0])], axis=1)
    out[...] = done.astype(bf16).reshape(out.shape)


def per_device(outer, video, block_ids, conv_weight, w_query, w_key, w_value, w_output):
    count, rows, cols, chans = video.shape
    group, halves = lax.axis_size("tm"), lax.axis_size("height")
    chunks = group * halves
    own = cols // chunks
    span = own + 2
    lines = count * rows
    whole = pl.BlockSpec(memory_space=pltpu.VMEM)
    params = pltpu.CompilerParams(vmem_limit_bytes=VMEM)

    packed = pl.pallas_call(
        pack_kernel,
        out_shape=jax.ShapeDtypeStruct((chunks, span * lines, chans), bf16),
        in_specs=[whole],
        out_specs=whole,
        scratch_shapes=[scratch(lines * cols, chans)],
        compiler_params=params,
    )(video)
    piece = lax.all_to_all(packed, ("tm", "height"), split_axis=0, concat_axis=0, tiled=True)
    piece = piece.reshape(group, halves, span * lines, chans)
    ids = block_ids
    if outer > 1:
        before = lax.ppermute(piece, "outer", [(i, i + 1) for i in range(outer - 1)])
        piece = jnp.concatenate([before, piece], axis=0)
        ids = jnp.concatenate([jnp.full((group * count,), -2, jnp.int32), ids])
        ids = lax.dynamic_slice(ids, (lax.axis_index("outer") * group * count,), (2 * group * count,))
    sources = piece.shape[0]
    frames = sources * count
    done = pl.pallas_call(
        functools.partial(main_kernel, count, rows),
        out_shape=jax.ShapeDtypeStruct((group, halves, own * lines, chans), bf16),
        in_specs=[pl.BlockSpec(memory_space=pltpu.SMEM)] + [whole] * 6,
        out_specs=whole,
        scratch_shapes=[
            scratch(sources * halves * span * lines, chans),
            scratch(sources * halves * span * lines, chans),
            pltpu.VMEM((span, halves * rows + 2, frames, TAPS * chans), bf16),
            scratch(chunks * own * lines, chans),
        ],
        compiler_params=params,
    )(ids, piece, conv_weight, w_query, w_key, w_value, w_output)
    done = done.reshape(chunks, own * lines, chans)
    returned = lax.all_to_all(done, ("tm", "height"), split_axis=0, concat_axis=0, tiled=True)
    return pl.pallas_call(
        unpack_kernel,
        out_shape=jax.ShapeDtypeStruct(video.shape, bf16),
        in_specs=[whole],
        out_specs=whole,
        scratch_shapes=[scratch(lines * cols, chans)],
        compiler_params=params,
    )(returned)


def solution(mesh):
    parts, along, halves = (mesh.shape[a] for a in ("groups", "tm", "height"))

    def run(video, *rest):
        count = video.shape[0] // (parts * along)
        group = min(g for g in range(1, along + 1) if along % g == 0 and (g * count >= REACH or g == along))
        outer = along // group
        split = Mesh(
            np.asarray(mesh.devices).reshape(parts, outer, group, halves),
            ("groups", "outer", "tm", "height"),
        )
        spec = P(("groups", "outer", "tm"), "height", None, None)
        placed = (spec, P("groups"), P(), P(), P(), P(), P())
        return jax.shard_map(
            functools.partial(per_device, outer),
            mesh=split,
            in_specs=placed,
            out_specs=spec,
            check_vma=False,
        )(video, *rest)

    return run
```

time: 62.7 us -> 53.5 us (0.85)
  blocking collectives: 11.9 us -> 32.7 us
  waiting for transfers between devices: 16.6 us -> 0 us
  starting transfers between devices: 14.2 us -> 0 us
  Pallas kernels: 0 us -> 13.2 us
  matrix products: 11.5 us -> 0 us
  other arithmetic: 3.32 us -> 0 us
  local copies, waits for them, and re-layouts: 4.25 us -> 7.22 us
    all_to_all x1 -> x2, blocking collectives: 11.9 us -> 32.7 us  [the longest x1 19.4 us: per_device(): lax.all_to_all(packed, ('tm', 'height'), split_axis=0, concat_axis=0, til...]
    pallas_call x0 -> x3, Pallas kernels: none -> 13.2 us  [the longest x1 12.1 us: per_device(): pl.pallas_call(functools.partial(main_kernel, count, rows), out_shape=jax...]
    dot_general x32 -> x0, matrix products: 9.52 us -> none  [the longest x27 6.16 us: per_device(): jnp.dot(window, conv_weight[tap_t, tap_r, tap_w], preferred_element_type=...]
    all_to_all x1 -> x0, waiting for transfers between devices: 9.14 us -> none  [per_device(): piece = lax.all_to_all(grid, 'tm', split_axis=1, concat_axis=0, tiled=True)]
    ppermute x3 -> x0, starting transfers between devices: 7.45 us -> none  [the longest x1 4.86 us: passed_along(): return lax.ppermute(value, axis, pairs)]
    ppermute x3 -> x0, waiting for transfers between devices: 7.43 us -> none  [the longest x1 5.53 us: passed_along(): return lax.ppermute(value, axis, pairs)]
    all_to_all x1 -> x0, starting transfers between devices: 6.77 us -> none  [per_device(): piece = lax.all_to_all(grid, 'tm', split_axis=1, concat_axis=0, tiled=True)]
    unnamed x14, local copies, waits for them, and re-layouts: 1.2 us -> 7.22 us
  transfers between devices with their start and end apart: 4 -> 0, of which waited for: 3 -> 0; matrix products, arithmetic and copies ran while one was open for 0% -> 0% of each run, Pallas kernels for 0% -> 0%
where the time goes in v1:
time: 53.5 us; the launch traced here: 53.2 us
  blocking collectives  32.7 us (61%)
  Pallas kernels  13.2 us (25%)
  local copies, waits for them, and re-layouts  7.22 us (13%)
    all_to_all x1, blocking collectives, per_device(): lax.all_to_all(packed, ('tm', 'height'), split_axis=0, concat_axis=0, til...  19.4 us
    all_to_all x1, blocking collectives, per_device(): lax.all_to_all(done, ('tm', 'height'), split_axis=0, concat_axis=0, tiled...  13.4 us
    pallas_call x1, Pallas kernels, per_device(): pl.pallas_call(functools.partial(main_kernel, count, rows), out_shape=jax...  12.1 us
    unnamed x14, local copies, waits for them, and re-layouts  7.22 us

profile of v1, /device:TPU:0, one launch (start us, length us, event | category | flops | bytes accessed | tf_op | source)
XLA Modules:
  0.0 53.2 jit_solution(18038197345879419185)
XLA Ops:
  0.0 0.0 copy-start.1
  0.0 0.9 %copy-done.1 = bf16[2,4,64,256]{3,2,1,0:T(8,128)(2,1)S(1)} copy-done((bf16[2,4,64,256]{3,2,1,0:T(8,128)(2,1)S(1)}, bf16[2,4,64,256]{3,2,1,0:T(8,128)(2,1)}, u32[]{:S(2)}) %copy-start.1) | copy-done | bytes 262168
  1.0 0.3 shard_map.73
  1.3 19.4 %all_to_all.10 = bf16[16,48,256]{2,1,0:T(8,128)(2,1)S(1)} all-to-all(bf16[16,48,256]{2,1,0:T(8,128)(2,1)S(1)} %shard_map.73), channel_id=1, replica_groups=mesh['groups'=2,'tm'=8,'height'=2] {'tm','height'}, dimensions={0} | all-to-all | bytes 786432 | tf_op jit(solution)/shard_map/all_to_all | solution.py:188
  20.6 0.0 copy-start
  20.6 2.0 %copy-done = bf16[3,3,3,256,256]{4,3,2,1,0:T(8,128)(2,1)S(1)} copy-done((bf16[3,3,3,256,256]{4,3,2,1,0:T(8,128)(2,1)S(1)}, bf16[3,3,3,256,256]{4,3,2,1,0:T(8,128)(2,1)}, u32[]{:S(2)}) %copy-start) | copy-done | bytes 3538968
  22.6 0.0 copy-start.2
  22.6 0.9 %copy-done.2 = bf16[256,256]{1,0:T(8,128)(2,1)S(1)} copy-done((bf16[256,256]{1,0:T(8,128)(2,1)S(1)}, bf16[256,256]{1,0:T(8,128)(2,1)}, u32[]{:S(2)}) %copy-start.2) | copy-done | bytes 131096
  23.5 0.0 copy-start.3
  23.5 0.9 %copy-done.3 = bf16[256,256]{1,0:T(8,128)(2,1)S(1)} copy-done((bf16[256,256]{1,0:T(8,128)(2,1)S(1)}, bf16[256,256]{1,0:T(8,128)(2,1)}, u32[]{:S(2)}) %copy-start.3) | copy-done | bytes 131096
  24.4 0.0 copy-start.4
  24.4 0.9 %copy-done.4 = bf16[256,256]{1,0:T(8,128)(2,1)S(1)} copy-done((bf16[256,256]{1,0:T(8,128)(2,1)S(1)}, bf16[256,256]{1,0:T(8,128)(2,1)}, u32[]{:S(2)}) %copy-start.4) | copy-done | bytes 131096
  25.3 0.0 copy-start.5
  25.3 0.9 %copy-done.5 = bf16[256,256]{1,0:T(8,128)(2,1)S(1)} copy-done((bf16[256,256]{1,0:T(8,128)(2,1)S(1)}, bf16[256,256]{1,0:T(8,128)(2,1)}, u32[]{:S(2)}) %copy-start.5) | copy-done | bytes 131096
  26.3 0.0 copy-start.6
  26.3 0.7 %copy-done.6 = s32[16]{0:T(128)S(1)} copy-done((s32[16]{0:T(128)S(1)}, s32[16]{0:T(128)}, u32[]{:S(2)}) %copy-start.6) | copy-done | bytes 88
  26.9 12.1 %shard_map.74 = bf16[8,2,32,256]{3,2,1,0:T(8,128)(2,1)S(1)} custom-call(s32[16]{0:T(128)S(1)} %copy-done.6, bf16[8,2,48,256]{3,2,1,0:T(8,128)(2,1)S(1)} %bitcast.2, bf16[3,3,3,256,256]{4,3,2,1,0:T(8,128)(2,1)S(1)} %copy-done, bf16[256,256]{1,0:T(8,128)(2,1)S(1)} %copy-done.2, bf16[256,256]{1,0:T(8,128)(2,1)S(1)} %copy-done.3, ...), custom_call_target="tpu_custom_call" | custom-call | tf_op jit(solution)/shard_map/pallas_call | solution.py:198
  39.0 13.4 %all_to_all.11.packed = bf16[16,32,256]{2,1,0:T(8,128)(2,1)S(1)} all-to-all(bf16[16,32,256]{2,1,0:T(8,128)(2,1)S(1)} %bitcast.3), channel_id=1, replica_groups=mesh['groups'=2,'tm'=8,'height'=2] {'tm','height'}, dimensions={0} | all-to-all | bytes 524288 | tf_op jit(solution)/shard_map/all_to_all | solution.py:212
  52.3 0.8 %shard_map.75 = bf16[2,4,64,256]{3,2,1,0:T(8,128)(2,1)} custom-call(bf16[16,32,256]{2,1,0:T(8,128)(2,1)S(1)} %all_to_all.11.packed), custom_call_target="tpu_custom_call" | custom-call | tf_op jit(solution)/shard_map/pallas_call | solution.py:213
Async XLA Ops:
  0.0 0.9 %copy-start.1 = (bf16[2,4,64,256]{3,2,1,0:T(8,128)(2,1)S(1)}, bf16[2,4,64,256]{3,2,1,0:T(8,128)(2,1)}, u32[]{:S(2)}) copy-start(bf16[2,4,64,256]{3,2,1,0:T(8,128)(2,1)} %video.1) | copy-start | bytes 786436
  20.6 2.0 %copy-start = (bf16[3,3,3,256,256]{4,3,2,1,0:T(8,128)(2,1)S(1)}, bf16[3,3,3,256,256]{4,3,2,1,0:T(8,128)(2,1)}, u32[]{:S(2)}) copy-start(bf16[3,3,3,256,256]{4,3,2,1,0:T(8,128)(2,1)} %conv_weight.1) | copy-start | bytes 10616836
  22.6 0.9 %copy-start.2 = (bf16[256,256]{1,0:T(8,128)(2,1)S(1)}, bf16[256,256]{1,0:T(8,128)(2,1)}, u32[]{:S(2)}) copy-start(bf16[256,256]{1,0:T(8,128)(2,1)} %w_query.1) | copy-start | bytes 393220
  23.5 0.9 %copy-start.3 = (bf16[256,256]{1,0:T(8,128)(2,1)S(1)}, bf16[256,256]{1,0:T(8,128)(2,1)}, u32[]{:S(2)}) copy-start(bf16[256,256]{1,0:T(8,128)(2,1)} %w_key.1) | copy-start | bytes 393220
  24.4 0.9 %copy-start.4 = (bf16[256,256]{1,0:T(8,128)(2,1)S(1)}, bf16[256,256]{1,0:T(8,128)(2,1)}, u32[]{:S(2)}) copy-start(bf16[256,256]{1,0:T(8,128)(2,1)} %w_value.1) | copy-start | bytes 393220
  25.3 0.9 %copy-start.5 = (bf16[256,256]{1,0:T(8,128)(2,1)S(1)}, bf16[256,256]{1,0:T(8,128)(2,1)}, u32[]{:S(2)}) copy-start(bf16[256,256]{1,0:T(8,128)(2,1)} %w_output.1) | copy-start | bytes 393220
  26.3 0.7 %copy-start.6 = (s32[16]{0:T(128)S(1)}, s32[16]{0:T(128)}, u32[]{:S(2)}) copy-start(s32[16]{0:T(128)} %ids.1) | copy-start | bytes 196

commit v2 on v1

--- a/solution.py
+++ b/solution.py
@@ -36,10 +36,19 @@
     return pltpu.VMEM((chans // LANES, rows, LANES), f32)
 
 
-def pack_kernel(video, out, wide):
+def pack_kernel(video, out, local, wide, sems):
     count, rows, cols, chans = video.shape
     lines = count * rows
-    fill(wide, video[...].reshape(lines * cols, chans).astype(f32))
+    copies = []
+    for t in range(count):
+        for r in range(rows):
+            copy = pltpu.make_async_copy(video.at[t, r], local.at[t, r], sems.at[t * rows + r])
+            copy.start()
+            copies.append(copy)
+    for at, copy in enumerate(copies):
+        copy.wait()
+        for i in range(wide.shape[0]):
+            wide[i, pl.ds(at * cols, cols), :] = local[at // rows, at % rows, :, i * LANES : (i + 1) * LANES].astype(f32)
     chunks = out.shape[0]
     span = out.shape[1] // lines
     own = span - 2
@@ -56,23 +65,43 @@
             out[d, pl.ds(k * lines, 16), :] = tile.astype(bf16)
 
 
-def unpack_kernel(packed, out, wide):
+def unpack_kernel(packed, out, local, wide, sems):
     count, rows, cols, chans = out.shape
     lines = count * rows
     fill(wide, packed[...].reshape(lines * cols, chans).astype(f32))
+    copies = []
     for t in range(count):
         for r in range(rows):
-            out[t, r] = get(wide, t * rows + r, cols, lines).astype(bf16)
+            local[t, r] = get(wide, t * rows + r, cols, lines).astype(bf16)
+            copy = pltpu.make_async_copy(local.at[t, r], out.at[t, r], sems.at[t * rows + r])
+            copy.start()
+            copies.append(copy)
+    for copy in copies:
+        copy.wait()
 
 
 def rms(wide):
     return wide * lax.rsqrt(jnp.mean(wide * wide, axis=-1, keepdims=True) + 1e-06)
 
 
+def divided(at, by):
+    if by & (by - 1) == 0:
+        bits = by.bit_length() - 1
+        return at >> bits, at & (by - 1)
+    return lax.div(at, jnp.int32(by)), lax.rem(at, jnp.int32(by))
+
+
 def main_kernel(
-    count, rows, ids, video, conv_weight, w_query, w_key, w_value, w_output, out,
-    vid, act, grid, res,
+    count, rows, ids_far, video, conv_far, query_far, key_far, value_far, output_far, out,
+    ids, conv_weight, w_query, w_key, w_value, w_output, vid, act, grid, total, shown, res, conv_sems, sems,
 ):
+    taps = [pltpu.make_async_copy(conv_far.at[:, b], conv_weight.at[:, b], conv_sems.at[b]) for b in range(TAPS)]
+    near = (ids, w_query, w_key, w_value, w_output)
+    far = (ids_far, query_far, key_far, value_far, output_far)
+    others = [pltpu.make_async_copy(src, dst, sems.at[i]) for i, (src, dst) in enumerate(zip(far, near))]
+    for copy in taps + others:
+        copy.start()
+
     sources, halves, _, chans = video.shape
     owners = out.shape[0]
     lines = count * rows
@@ -83,6 +112,7 @@
     heads = chans // HD
     step = halves * span * lines
     back = halves * own * lines
+    area = high * frames
 
     xs = video[...].reshape(-1, chans).astype(f32)
     fill(vid, xs)
@@ -92,8 +122,7 @@
     def pixel(ref, w, r):
         half, line = divmod(r, rows)
         return [
-            get(ref, (half * span + w) * lines + t * rows + line, sources, step)
-            for t in range(count)
+            get(ref, (half * span + w) * lines + t * rows + line, sources, step) for t in range(count)
         ]
 
     first = lax.broadcasted_iota(jnp.int32, (sources, chans), 0) == 0
@@ -113,54 +142,71 @@
                 shift = TAPS - 1 - a
                 picked = [ordered[count + t - shift] for t in range(count)]
                 grid[w, r + 1, :, a * chans : (a + 1) * chans] = jnp.concatenate(picked, 0).astype(bf16)
-
-    area = high * frames
-    row_at = lax.broadcasted_iota(jnp.int32, (area, area), 0)
-    col_at = lax.broadcasted_iota(jnp.int32, (area, area), 1)
-
-    def frame_of(at):
-        place = at % frames
-        return (place % sources) * count + place // sources
-
-    row_t, col_t = frame_of(row_at), frame_of(col_at)
-
-    def block_of(t):
-        found = jnp.zeros(t.shape, jnp.int32)
+            if 1 <= w <= own:
+                place = ((w - 1) * high + r) * frames
+                shown[pl.ds(place, frames), :] = jnp.concatenate(pixel(vid, w, r), 0)
+
+    others[0].wait()
+
+    def frame_and_block(shape, dim):
+        inner, source = divided(lax.broadcasted_iota(jnp.int32, shape, dim), sources)
+        frame = source * count + inner
+        block = jnp.zeros(shape, jnp.int32)
         for s in range(frames):
-            found = jnp.where(t == s, ids[s], found)
-        return found
-
-    row_b, col_b = block_of(row_t), block_of(col_t)
-    permit = (row_at // frames == col_at // frames) & (col_t <= row_t) & (col_b >= row_b - 1)
+            block = jnp.where(frame == s, ids[s], block)
+        return frame, block
+
+    row_t, row_b = (jnp.concatenate([x] * high, 0) for x in frame_and_block((frames, area), 0))
+    wrap = divided(lax.broadcasted_iota(jnp.int32, (1, area), 1), frames)[1]
+    col_inner, col_source = divided(wrap, sources)
+    col_t = col_source * count + col_inner
+    col_b = jnp.zeros((1, area), jnp.int32)
+    for s in range(frames):
+        col_b = jnp.where(col_t == s, ids[s], col_b)
+    row_p = divided(lax.broadcasted_iota(jnp.int32, (area, area), 0), frames)[0]
+    col_p = divided(lax.broadcasted_iota(jnp.int32, (area, area), 1), frames)[0]
+    permit = (row_p == col_p) & (col_t <= row_t) & (col_b >= row_b - 1)
+    bias = jnp.where(permit, 0.0, -1e30)
     head_of = lax.broadcasted_iota(jnp.int32, (area, chans), 1) // HD
 
+    for b in range(TAPS):
+        taps[b].wait()
+        for e in range(TAPS):
+            window = grid[e : e + own, b : b + high].reshape(own * area, TAPS * chans)
+            weight = jnp.concatenate([conv_weight[a, b, e] for a in range(TAPS)], axis=0)
+            part = jnp.dot(window, weight, preferred_element_type=f32)
+            total[...] = part if b == e == 0 else total[...] + part
+
+    hidden = (shown[...] + total[...]).astype(bf16).astype(f32)
+    shown[...] = hidden
+    normed = rms(hidden).astype(bf16)
+    for copy in others[1:]:
+        copy.wait()
+    query, keys, values = (
+        jnp.dot(normed, weight[...], preferred_element_type=f32).astype(bf16) for weight in (w_query, w_key, w_value)
+    )
+    gone = []
     for w in range(own):
-        total = jnp.zeros((area, chans), f32)
-        for e in range(TAPS):
-            for b in range(TAPS):
-                window = grid[w + e, b : b + high].reshape(area, TAPS * chans)
-                weight = jnp.concatenate([conv_weight[a, b, e] for a in range(TAPS)], axis=0)
-                total = total + jnp.dot(window, weight, preferred_element_type=f32)
-        shown = jnp.concatenate([x for r in range(high) for x in pixel(vid, w + 1, r)], axis=0)
-        hidden = (shown + total).astype(bf16).astype(f32)
-        normed = rms(hidden).astype(bf16)
-        query = jnp.dot(normed, w_query[...], preferred_element_type=f32).astype(bf16)
-        keys = jnp.dot(normed, w_key[...], preferred_element_type=f32).astype(bf16)
-        values = jnp.dot(normed, w_value[...], preferred_element_type=f32).astype(bf16)
-        attended = jnp.zeros((area, chans), f32)
-        for h in range(heads):
-            single = jnp.where(head_of == h, query, jnp.zeros((), bf16))
-            scores = lax.dot_general(single, keys, (((1,), (1,)), ((), ())), preferred_element_type=f32)
-            scores = jnp.where(permit, scores * HD ** (-0.5), -1e30)
-            expo = jnp.exp(scores - jnp.max(scores, axis=-1, keepdims=True))
-            weights = (expo / jnp.sum(expo, axis=-1, keepdims=True)).astype(bf16)
-            mixed = jnp.dot(weights, values, preferred_element_type=f32)
-            attended = jnp.where(head_of == h, mixed, attended)
-        encoded = hidden + jnp.dot(attended.astype(bf16), w_output[...], preferred_element_type=f32)
+        part = slice(w * area, (w + 1) * area)
+        single = jnp.concatenate(
+            [jnp.where(head_of == h, query[part], jnp.zeros((), bf16)) for h in range(heads)], axis=0
+        )
+        scores = lax.dot_general(single, keys[part], (((1,), (1,)), ((), ())), preferred_element_type=f32)
+        scores = scores * HD ** (-0.5) + jnp.concatenate([bias] * heads, axis=0)
+        expo = jnp.exp(scores - jnp.max(scores, axis=-1, keepdims=True))
+        weights = (expo * (1.0 / jnp.sum(expo, axis=-1, keepdims=True))).astype(bf16)
+        mixed = jnp.dot(weights, values[part], preferred_element_type=f32)
+        attended = mixed[:area]
+        for h in range(1, heads):
+            attended = jnp.where(head_of == h, mixed[h * area : (h + 1) * area], attended)
+        gone.append(attended.astype(bf16))
+    attended = jnp.concatenate(gone, axis=0)
+    encoded = shown[...] + jnp.dot(attended, w_output[...], preferred_element_type=f32)
+    for w in range(own):
         for r in range(high):
             half, line = divmod(r, rows)
             for t in range(count):
-                start = (r * count + t + 1) * sources - owners
+                start = ((w * high + r) * count + t + 1) * sources - owners
                 place = (half * own + w) * lines + t * rows + line
                 put(res, place, owners, back, encoded[start : start + owners])
     done = jnp.concatenate([res[i] for i in range(res.shape[0])], axis=1)
@@ -175,14 +221,19 @@
     span = own + 2
     lines = count * rows
     whole = pl.BlockSpec(memory_space=pltpu.VMEM)
+    far = pl.BlockSpec(memory_space=pl.ANY)
     params = pltpu.CompilerParams(vmem_limit_bytes=VMEM)
 
     packed = pl.pallas_call(
         pack_kernel,
         out_shape=jax.ShapeDtypeStruct((chunks, span * lines, chans), bf16),
-        in_specs=[whole],
+        in_specs=[far],
         out_specs=whole,
-        scratch_shapes=[scratch(lines * cols, chans)],
+        scratch_shapes=[
+            pltpu.VMEM(video.shape, bf16),
+            scratch(lines * cols, chans),
+            pltpu.SemaphoreType.DMA((lines,)),
+        ],
         compiler_params=params,
     )(video)
     piece = lax.all_to_all(packed, ("tm", "height"), split_axis=0, concat_axis=0, tiled=True)
@@ -198,13 +249,21 @@
     done = pl.pallas_call(
         functools.partial(main_kernel, count, rows),
         out_shape=jax.ShapeDtypeStruct((group, halves, own * lines, chans), bf16),
-        in_specs=[pl.BlockSpec(memory_space=pltpu.SMEM)] + [whole] * 6,
+        in_specs=[far, whole] + [far] * 5,
         out_specs=whole,
         scratch_shapes=[
-            scratch(sources * halves * span * lines, chans),
-            scratch(sources * halves * span * lines, chans),
+            pltpu.SMEM((frames,), jnp.int32),
+            pltpu.VMEM(conv_weight.shape, bf16),
+        ]
+        + [pltpu.VMEM((chans, chans), bf16)] * 4
+        + [scratch(sources * halves * span * lines, chans)] * 2
+        + [
             pltpu.VMEM((span, halves * rows + 2, frames, TAPS * chans), bf16),
+            pltpu.VMEM((own * halves * rows * frames, chans), f32),
+            pltpu.VMEM((own * halves * rows * frames, chans), f32),
             scratch(chunks * own * lines, chans),
+            pltpu.SemaphoreType.DMA((TAPS,)),
+            pltpu.SemaphoreType.DMA((5,)),
         ],
         compiler_params=params,
     )(ids, piece, conv_weight, w_query, w_key, w_value, w_output)
@@ -214,8 +273,12 @@
         unpack_kernel,
         out_shape=jax.ShapeDtypeStruct(video.shape, bf16),
         in_specs=[whole],
-        out_specs=whole,
-        scratch_shapes=[scratch(lines * cols, chans)],
+        out_specs=far,
+        scratch_shapes=[
+            pltpu.VMEM(video.shape, bf16),
+            scratch(lines * cols, chans),
+            pltpu.SemaphoreType.DMA((lines,)),
+        ],
         compiler_params=params,
     )(returned)
 

time: 53.5 us -> 51.1 us (0.955)
  Pallas kernels: 13.2 us -> 10.8 us
    pallas_call x1, Pallas kernels: 12.1 us -> 9.27 us  [per_device(): pl.pallas_call(functools.partial(main_kernel, count, rows), out_shape=jax...]
where the time goes in v2:
time: 51.1 us; the launch traced here: 50.8 us
  blocking collectives  32.7 us (64%)
  Pallas kernels  10.8 us (21%)
  local copies, waits for them, and re-layouts  7.22 us (14%)
    all_to_all x1, blocking collectives, per_device(): lax.all_to_all(packed, ('tm', 'height'), split_axis=0, concat_axis=0, til...  19.4 us
    all_to_all x1, blocking collectives, per_device(): lax.all_to_all(done, ('tm', 'height'), split_axis=0, concat_axis=0, tiled...  13.4 us
    pallas_call x1, Pallas kernels, per_device(): pl.pallas_call(functools.partial(main_kernel, count, rows), out_shape=jax...  9.27 us
    unnamed x14, local copies, waits for them, and re-layouts  7.22 us

profile of v2, /device:TPU:0, one launch (start us, length us, event | category | flops | bytes accessed | tf_op | source)
XLA Modules:
  0.0 50.8 jit_solution(2614067283580452220)
XLA Ops:
  0.0 0.0 copy-start.1
  0.0 0.9 %copy-done.1 = bf16[2,4,64,256]{3,2,1,0:T(8,128)(2,1)S(1)} copy-done((bf16[2,4,64,256]{3,2,1,0:T(8,128)(2,1)S(1)}, bf16[2,4,64,256]{3,2,1,0:T(8,128)(2,1)}, u32[]{:S(2)}) %copy-start.1) | copy-done | bytes 262168
  1.0 0.7 %shard_map.73 = bf16[16,48,256]{2,1,0:T(8,128)(2,1)S(1)} custom-call(bf16[2,4,64,256]{3,2,1,0:T(8,128)(2,1)S(1)} %copy-done.1), custom_call_target="tpu_custom_call" | custom-call | tf_op jit(solution)/shard_map/pallas_call | solution.py:227
  1.7 19.4 %all_to_all.10 = bf16[16,48,256]{2,1,0:T(8,128)(2,1)S(1)} all-to-all(bf16[16,48,256]{2,1,0:T(8,128)(2,1)S(1)} %shard_map.73), channel_id=1, replica_groups=mesh['groups'=2,'tm'=8,'height'=2] {'tm','height'}, dimensions={0} | all-to-all | bytes 786432 | tf_op jit(solution)/shard_map/all_to_all | solution.py:239
  21.0 0.0 copy-start
  21.0 2.0 %copy-done = bf16[3,3,3,256,256]{4,3,2,1,0:T(8,128)(2,1)S(1)} copy-done((bf16[3,3,3,256,256]{4,3,2,1,0:T(8,128)(2,1)S(1)}, bf16[3,3,3,256,256]{4,3,2,1,0:T(8,128)(2,1)}, u32[]{:S(2)}) %copy-start) | copy-done | bytes 3538968
  23.0 0.0 copy-start.2
  23.0 0.9 %copy-done.2 = bf16[256,256]{1,0:T(8,128)(2,1)S(1)} copy-done((bf16[256,256]{1,0:T(8,128)(2,1)S(1)}, bf16[256,256]{1,0:T(8,128)(2,1)}, u32[]{:S(2)}) %copy-start.2) | copy-done | bytes 131096
  23.9 0.0 copy-start.3
  23.9 0.9 %copy-done.3 = bf16[256,256]{1,0:T(8,128)(2,1)S(1)} copy-done((bf16[256,256]{1,0:T(8,128)(2,1)S(1)}, bf16[256,256]{1,0:T(8,128)(2,1)}, u32[]{:S(2)}) %copy-start.3) | copy-done | bytes 131096
  24.9 0.0 copy-start.4
  24.9 0.9 %copy-done.4 = bf16[256,256]{1,0:T(8,128)(2,1)S(1)} copy-done((bf16[256,256]{1,0:T(8,128)(2,1)S(1)}, bf16[256,256]{1,0:T(8,128)(2,1)}, u32[]{:S(2)}) %copy-start.4) | copy-done | bytes 131096
  25.8 0.0 copy-start.5
  25.8 0.9 %copy-done.5 = bf16[256,256]{1,0:T(8,128)(2,1)S(1)} copy-done((bf16[256,256]{1,0:T(8,128)(2,1)S(1)}, bf16[256,256]{1,0:T(8,128)(2,1)}, u32[]{:S(2)}) %copy-start.5) | copy-done | bytes 131096
  26.7 0.0 copy-start.6
  26.7 0.7 %copy-done.6 = s32[16]{0:T(128)S(1)} copy-done((s32[16]{0:T(128)S(1)}, s32[16]{0:T(128)}, u32[]{:S(2)}) %copy-start.6) | copy-done | bytes 88
  27.3 9.3 %shard_map.74 = bf16[8,2,32,256]{3,2,1,0:T(8,128)(2,1)S(1)} custom-call(s32[16]{0:T(128)S(1)} %copy-done.6, bf16[8,2,48,256]{3,2,1,0:T(8,128)(2,1)S(1)} %bitcast.2, bf16[3,3,3,256,256]{4,3,2,1,0:T(8,128)(2,1)S(1)} %copy-done, bf16[256,256]{1,0:T(8,128)(2,1)S(1)} %copy-done.2, bf16[256,256]{1,0:T(8,128)(2,1)S(1)} %copy-done.3, ...), custom_call_target="tpu_custom_call" | custom-call | tf_op jit(solution)/shard_map/pallas_call | solution.py:249
  36.6 13.4 %all_to_all.11.packed = bf16[16,32,256]{2,1,0:T(8,128)(2,1)S(1)} all-to-all(bf16[16,32,256]{2,1,0:T(8,128)(2,1)S(1)} %bitcast.3), channel_id=1, replica_groups=mesh['groups'=2,'tm'=8,'height'=2] {'tm','height'}, dimensions={0} | all-to-all | bytes 524288 | tf_op jit(solution)/shard_map/all_to_all | solution.py:271
  50.0 0.8 %shard_map.75 = bf16[2,4,64,256]{3,2,1,0:T(8,128)(2,1)} custom-call(bf16[16,32,256]{2,1,0:T(8,128)(2,1)S(1)} %all_to_all.11.packed), custom_call_target="tpu_custom_call" | custom-call | tf_op jit(solution)/shard_map/pallas_call | solution.py:272
Async XLA Ops:
  0.0 0.9 %copy-start.1 = (bf16[2,4,64,256]{3,2,1,0:T(8,128)(2,1)S(1)}, bf16[2,4,64,256]{3,2,1,0:T(8,128)(2,1)}, u32[]{:S(2)}) copy-start(bf16[2,4,64,256]{3,2,1,0:T(8,128)(2,1)} %video.1) | copy-start | bytes 786436
  21.0 2.0 %copy-start = (bf16[3,3,3,256,256]{4,3,2,1,0:T(8,128)(2,1)S(1)}, bf16[3,3,3,256,256]{4,3,2,1,0:T(8,128)(2,1)}, u32[]{:S(2)}) copy-start(bf16[3,3,3,256,256]{4,3,2,1,0:T(8,128)(2,1)} %conv_far.1) | copy-start | bytes 10616836
  23.0 0.9 %copy-start.2 = (bf16[256,256]{1,0:T(8,128)(2,1)S(1)}, bf16[256,256]{1,0:T(8,128)(2,1)}, u32[]{:S(2)}) copy-start(bf16[256,256]{1,0:T(8,128)(2,1)} %query_far.1) | copy-start | bytes 393220
  23.9 0.9 %copy-start.3 = (bf16[256,256]{1,0:T(8,128)(2,1)S(1)}, bf16[256,256]{1,0:T(8,128)(2,1)}, u32[]{:S(2)}) copy-start(bf16[256,256]{1,0:T(8,128)(2,1)} %key_far.1) | copy-start | bytes 393220
  24.9 0.9 %copy-start.4 = (bf16[256,256]{1,0:T(8,128)(2,1)S(1)}, bf16[256,256]{1,0:T(8,128)(2,1)}, u32[]{:S(2)}) copy-start(bf16[256,256]{1,0:T(8,128)(2,1)} %value_far.1) | copy-start | bytes 393220
  25.8 0.9 %copy-start.5 = (bf16[256,256]{1,0:T(8,128)(2,1)S(1)}, bf16[256,256]{1,0:T(8,128)(2,1)}, u32[]{:S(2)}) copy-start(bf16[256,256]{1,0:T(8,128)(2,1)} %output_far.1) | copy-start | bytes 393220
  26.7 0.7 %copy-start.6 = (s32[16]{0:T(128)S(1)}, s32[16]{0:T(128)}, u32[]{:S(2)}) copy-start(s32[16]{0:T(128)} %ids_far.1) | copy-start | bytes 196

commit v3 on v2

--- a/solution.py
+++ b/solution.py
@@ -221,8 +221,12 @@
     span = own + 2
     lines = count * rows
     whole = pl.BlockSpec(memory_space=pltpu.VMEM)
-    far = pl.BlockSpec(memory_space=pl.ANY)
+    far = pl.BlockSpec(memory_space=pltpu.HBM)
     params = pltpu.CompilerParams(vmem_limit_bytes=VMEM)
+    video, conv_weight, w_query, w_key, w_value, w_output = (
+        pltpu.with_memory_space_constraint(x, pltpu.HBM)
+        for x in (video, conv_weight, w_query, w_key, w_value, w_output)
+    )
 
     packed = pl.pallas_call(
         pack_kernel,
@@ -244,6 +248,7 @@
         piece = jnp.concatenate([before, piece], axis=0)
         ids = jnp.concatenate([jnp.full((group * count,), -2, jnp.int32), ids])
         ids = lax.dynamic_slice(ids, (lax.axis_index("outer") * group * count,), (2 * group * count,))
+    ids = pltpu.with_memory_space_constraint(ids, pltpu.HBM)
     sources = piece.shape[0]
     frames = sources * count
     done = pl.pallas_call(

time: 51.1 us -> 43.8 us (0.86)
  local copies, waits for them, and re-layouts: 7.22 us -> 0 us
    unnamed x14 -> x0, local copies, waits for them, and re-layouts: 7.22 us -> none
    pallas_call x1, Pallas kernels: 0.72 us -> 1.24 us  [per_device(): pl.pallas_call(pack_kernel, out_shape=jax.ShapeDtypeStruct((chunks, span...]
where the time goes in v3:
time: 43.8 us; the launch traced here: 43.6 us
  blocking collectives  32.7 us (75%)
  Pallas kernels  10.8 us (25%)
    all_to_all x1, blocking collectives, per_device(): lax.all_to_all(packed, ('tm', 'height'), split_axis=0, concat_axis=0, til...  19.4 us
    all_to_all x1, blocking collectives, per_device(): lax.all_to_all(done, ('tm', 'height'), split_axis=0, concat_axis=0, tiled...  13.4 us
    pallas_call x1, Pallas kernels, per_device(): pl.pallas_call(functools.partial(main_kernel, count, rows), out_shape=jax...  8.78 us
    pallas_call x1, Pallas kernels, per_device(): pl.pallas_call(pack_kernel, out_shape=jax.ShapeDtypeStruct((chunks, span...  1.24 us

profile of v3, /device:TPU:0, one launch (start us, length us, event | category | flops | bytes accessed | tf_op | source)
XLA Modules:
  0.0 43.6 jit_solution(13104576221179466161)
XLA Ops:
  0.0 1.2 %shard_map.73 = bf16[16,48,256]{2,1,0:T(8,128)(2,1)S(1)} custom-call(bf16[2,4,64,256]{3,2,1,0:T(8,128)(2,1)} %video.1), custom_call_target="tpu_custom_call" | custom-call | tf_op jit(solution)/shard_map/pallas_call | solution.py:231
  1.2 19.4 %all_to_all.10 = bf16[16,48,256]{2,1,0:T(8,128)(2,1)S(1)} all-to-all(bf16[16,48,256]{2,1,0:T(8,128)(2,1)S(1)} %shard_map.73), channel_id=1, replica_groups=mesh['groups'=2,'tm'=8,'height'=2] {'tm','height'}, dimensions={0} | all-to-all | bytes 786432 | tf_op jit(solution)/shard_map/all_to_all | solution.py:243
  20.6 8.8 %shard_map.74 = bf16[8,2,32,256]{3,2,1,0:T(8,128)(2,1)S(1)} custom-call(s32[16]{0:T(128)} %ids_far.1, bf16[8,2,48,256]{3,2,1,0:T(8,128)(2,1)S(1)} %bitcast.2, bf16[3,3,3,256,256]{4,3,2,1,0:T(8,128)(2,1)} %conv_far.1, bf16[256,256]{1,0:T(8,128)(2,1)} %query_far.1, bf16[256,256]{1,0:T(8,128)(2,1)} %key_far.1, bf16[256,256]{1,0:T(8,128)(2,1)} %value_far.1, ...), custom_call_target="tpu_custom_call" | custom-call | tf_op jit(solution)/shard_map/pallas_call | solution.py:254
  29.4 13.4 %all_to_all.11.packed = bf16[16,32,256]{2,1,0:T(8,128)(2,1)S(1)} all-to-all(bf16[16,32,256]{2,1,0:T(8,128)(2,1)S(1)} %bitcast.3), channel_id=1, replica_groups=mesh['groups'=2,'tm'=8,'height'=2] {'tm','height'}, dimensions={0} | all-to-all | bytes 524288 | tf_op jit(solution)/shard_map/all_to_all | solution.py:276
  42.8 0.8 %shard_map.75 = bf16[2,4,64,256]{3,2,1,0:T(8,128)(2,1)} custom-call(bf16[16,32,256]{2,1,0:T(8,128)(2,1)S(1)} %all_to_all.11.packed), custom_call_target="tpu_custom_call" | custom-call | tf_op jit(solution)/shard_map/pallas_call | solution.py:277

commit v4 on v2

v4 whole, which is shorter than its diff:
```python
import functools

import jax
import jax.numpy as jnp
import numpy as np
from jax import lax
from jax.experimental import pallas as pl
from jax.experimental.pallas import tpu as pltpu
from jax.sharding import Mesh, PartitionSpec as P

HD = 64
BLOCK = 4
TAPS = 3
REACH = 2 * BLOCK - 1 + TAPS - 1
LANES = 128
EDGE = 8
VMEM = 28 * 2**20

bf16, f32 = jnp.bfloat16, jnp.float32


def get(ref, start, size, stride):
    return jnp.concatenate([ref[i, pl.ds(start, size, stride=stride), :] for i in range(ref.shape[0])], axis=1)


def put(ref, start, size, stride, value):
    for i in range(ref.shape[0]):
        ref[i, pl.ds(start, size, stride=stride), :] = value[:, i * LANES : (i + 1) * LANES]


def fill(ref, start, value):
    for i in range(ref.shape[0]):
        ref[i, pl.ds(start, value.shape[0]), :] = value[:, i * LANES : (i + 1) * LANES]


def scratch(rows, chans):
    return pltpu.VMEM((chans // LANES, rows, LANES), f32)


def partner(me, k, group):
    return me ^ k if group & (group - 1) == 0 else (k - me) % group


def rms(wide):
    return wide * lax.rsqrt(jnp.mean(wide * wide, axis=-1, keepdims=True) + 1e-06)


def divided(at, by):
    if by & (by - 1) == 0:
        bits = by.bit_length() - 1
        return at >> bits, at & (by - 1)
    return lax.div(at, jnp.int32(by)), lax.rem(at, jnp.int32(by))


def pack_kernel(group, video, *refs):
    blocks, (local, wide, sems) = refs[:group], refs[group:]
    count, rows, cols, chans = video.shape
    lines = count * rows
    stride = cols + 2 * EDGE
    own = cols // group
    span = own + 2
    copies = []
    for at in range(lines):
        place = (at // rows, at % rows)
        copy = pltpu.make_async_copy(video.at[place], local.at[place], sems.at[at])
        copy.start()
        copies.append(copy)
    nothing = jnp.zeros((EDGE, chans), f32)
    for at in range(lines):
        fill(wide, at * stride, nothing)
        fill(wide, at * stride + EDGE + cols, nothing)
    for at, copy in enumerate(copies):
        copy.wait()
        fill(wide, at * stride + EDGE, local[at // rows, at % rows].astype(f32))
    me = lax.axis_index("tm")
    together = 16 // lines
    for k in range(group):
        start = partner(me, k, group) * own + EDGE - 1
        for w in range(0, span, together):
            tile = jnp.concatenate([get(wide, start + w + i, lines, stride) for i in range(together)], axis=0)
            blocks[k][pl.ds(w * lines, 16), :] = tile.astype(bf16)


def shift_kernel(count, rows, group, before, *refs):
    blocks, refs = refs[:group], refs[group:]
    past, refs = (refs[0], refs[1:]) if before else (None, refs)
    far, refs = refs[:5], refs[5:]
    grid, edge, shown, refs = refs[0], refs[1], refs[2], refs[3:]
    near, (vid, act, sems) = refs[:5], refs[5:]
    copies = [pltpu.make_async_copy(src, dst, sems.at[i]) for i, (src, dst) in enumerate(zip(far, near))]
    for copy in copies:
        copy.start()
    step, chans = blocks[0].shape
    lines = count * rows
    span = step // lines
    own = span - 2
    frames = grid.shape[2]
    sources = frames // count
    me = lax.axis_index("tm")

    def take(block, source):
        start = pl.multiple_of(source * step, 16)
        wide = block.astype(f32)
        fill(vid, start, wide)
        normal = rms(wide)
        fill(act, start, normal / (1.0 + jnp.exp(-normal)))

    for k in range(group):
        source = partner(me, k, group)
        take(blocks[k][...], source + sources - group)
        if before:
            take(past[k], source)

    def pixel(ref, w, r):
        return [get(ref, w * lines + t * rows + r, sources, step) for t in range(count)]

    first = lax.broadcasted_iota(jnp.int32, (sources, chans), 0) == 0

    def earlier(x):
        return jnp.where(first, 0.0, pltpu.roll(x, 1, 0))

    for w in range(span):
        for r in range(rows):
            now = pixel(act, w, r)
            ordered = [earlier(x) for x in now] + now
            for a in range(TAPS):
                shift = TAPS - 1 - a
                picked = [ordered[count + t - shift] for t in range(count)]
                grid[w, r, :, a * chans : (a + 1) * chans] = jnp.concatenate(picked, 0).astype(bf16)
            if 1 <= w <= own:
                shown[pl.ds(((w - 1) * rows + r) * frames, frames), :] = jnp.concatenate(pixel(vid, w, r), 0)
    lower = lax.axis_index("height")
    edge[...] = grid[:, (rows - 1) * (1 - lower)]
    for copy in copies:
        copy.wait()


def main_kernel(
    count, rows, group, ids_far, grid, edge, given, conv_weight, w_query, w_key, w_value, w_output, *refs
):
    blocks, (ids, border, total, shown, res, sem) = refs[:group], refs[group:]
    ids_copy = pltpu.make_async_copy(ids_far, ids, sem)
    ids_copy.start()
    span, _, frames, _ = grid.shape
    chans = w_query.shape[0]
    own = span - 2
    sources = frames // count
    lines = count * rows
    heads = chans // HD
    back = own * lines
    several = own // 2 if own % 2 == 0 else own
    area = several * rows * frames
    lower = lax.axis_index("height")
    border[1 - lower] = edge[...]
    border[lower] = jnp.zeros(edge.shape, bf16)

    for b in range(TAPS):
        for e in range(TAPS):
            ahead = [border[0, e : e + own][:, None]] if b == 0 else []
            after = [border[1, e : e + own][:, None]] if b == TAPS - 1 else []
            inner = grid[e : e + own, max(b - 1, 0) : min(b - 1 + rows, rows)]
            window = jnp.concatenate(ahead + [inner] + after, axis=1) if ahead or after else inner
            window = window.reshape(own * rows * frames, TAPS * chans)
            weight = jnp.concatenate([conv_weight[a, b, e] for a in range(TAPS)], axis=0)
            part = jnp.dot(window, weight, preferred_element_type=f32)
            total[...] = part if b == e == 0 else total[...] + part

    hidden = (given[...] + total[...]).astype(bf16).astype(f32)
    shown[...] = hidden
    normed = rms(hidden).astype(bf16)
    query, keys, values = (
        jnp.dot(normed, weight[...], preferred_element_type=f32).astype(bf16) for weight in (w_query, w_key, w_value)
    )

    ids_copy.wait()

    def place_of(shape, dim):
        inner, source = divided(lax.broadcasted_iota(jnp.int32, shape, dim) % frames, sources)
        frame = source * count + inner
        block = jnp.zeros(shape, jnp.int32)
        for s in range(frames):
            block = jnp.where(frame == s, ids[s], block)
        return frame, block

    pixels = several * rows
    row_t, row_b = (jnp.concatenate([x] * pixels, 0) for x in place_of((frames, area), 0))
    col_t, col_b = place_of((1, area), 1)
    row_p = divided(lax.broadcasted_iota(jnp.int32, (area, area), 0), frames)[0]
    col_p = divided(lax.broadcasted_iota(jnp.int32, (area, area), 1), frames)[0]
    permit = (row_p == col_p) & (col_t <= row_t) & (col_b >= row_b - 1)
    bias = jnp.where(permit, 0.0, -1e30)
    head_of = lax.broadcasted_iota(jnp.int32, (area, chans), 1) // HD

    gone = []
    for w in range(0, own, several):
        part = slice(w * rows * frames, w * rows * frames + area)
        single = jnp.concatenate(
            [jnp.where(head_of == h, query[part], jnp.zeros((), bf16)) for h in range(heads)], axis=0
        )
        scores = lax.dot_general(single, keys[part], (((1,), (1,)), ((), ())), preferred_element_type=f32)
        scores = scores * HD ** (-0.5) + jnp.concatenate([bias] * heads, axis=0)
        expo = jnp.exp(scores - jnp.max(scores, axis=-1, keepdims=True))
        weights = (expo * (1.0 / jnp.sum(expo, axis=-1, keepdims=True))).astype(bf16)
        mixed = jnp.dot(weights, values[part], preferred_element_type=f32)
        attended = mixed[:area]
        for h in range(1, heads):
            attended = jnp.where(head_of == h, mixed[h * area : (h + 1) * area], attended)
        gone.append(attended.astype(bf16))
    attended = jnp.concatenate(gone, axis=0)
    encoded = shown[...] + jnp.dot(attended, w_output[...], preferred_element_type=f32)
    for w in range(own):
        for r in range(rows):
            for t in range(count):
                start = ((w * rows + r) * count + t + 1) * sources - group
                put(res, w * lines + t * rows + r, group, back, encoded[start : start + group])
    me = lax.axis_index("tm")
    for k in range(group):
        start = pl.multiple_of(partner(me, k, group) * back, 16)
        block = jnp.concatenate([res[i, pl.ds(start, back), :] for i in range(res.shape[0])], axis=1)
        blocks[k][...] = block.astype(bf16)


def unpack_kernel(group, *refs):
    blocks, (out, local, wide, sems) = refs[:group], refs[group:]
    count, rows, cols, chans = out.shape
    lines = count * rows
    me = lax.axis_index("tm")
    for k in range(group):
        start = pl.multiple_of(partner(me, k, group) * blocks[k].shape[0], 16)
        fill(wide, start, blocks[k][...].astype(f32))
    copies = []
    for at in range(lines):
        place = (at // rows, at % rows)
        local[place] = get(wide, at, cols, lines).astype(bf16)
        copy = pltpu.make_async_copy(local.at[place], out.at[place], sems.at[at])
        copy.start()
        copies.append(copy)
    for copy in copies:
        copy.wait()


def exchanged(blocks, group):
    back = [blocks[0]]
    for k in range(1, group):
        back.append(lax.ppermute(blocks[k], "tm", [(i, partner(i, k, group)) for i in range(group)]))
    return back


def per_device(outer, video, block_ids, conv_weight, w_query, w_key, w_value, w_output):
    count, rows, cols, chans = video.shape
    group = lax.axis_size("tm")
    own = cols // group
    span = own + 2
    lines = count * rows
    near = pl.BlockSpec(memory_space=pltpu.VMEM)
    far = pl.BlockSpec(memory_space=pltpu.HBM)
    params = pltpu.CompilerParams(vmem_limit_bytes=VMEM)
    in_far = functools.partial(pltpu.with_memory_space_constraint, memory_space=pltpu.HBM)
    weights = [in_far(x) for x in (conv_weight, w_query, w_key, w_value, w_output)]

    blocks = pl.pallas_call(
        functools.partial(pack_kernel, group),
        out_shape=[jax.ShapeDtypeStruct((span * lines, chans), bf16)] * group,
        in_specs=[far],
        out_specs=[near] * group,
        scratch_shapes=[
            pltpu.VMEM(video.shape, bf16),
            scratch(lines * (cols + 2 * EDGE), chans),
            pltpu.SemaphoreType.DMA((lines,)),
        ],
        compiler_params=params,
    )(in_far(video))
    pieces = exchanged(blocks, group)
    ids = block_ids
    if outer > 1:
        before = lax.ppermute(jnp.stack(pieces), "outer", [(i, i + 1) for i in range(outer - 1)])
        pieces = pieces + [before]
        ids = jnp.concatenate([jnp.full((group * count,), -2, jnp.int32), ids])
        ids = lax.dynamic_slice(ids, (lax.axis_index("outer") * group * count,), (2 * group * count,))
    sources = group * (2 if outer > 1 else 1)
    frames = sources * count
    total = own * rows * frames
    grid, edge, shown, *weights = pl.pallas_call(
        functools.partial(shift_kernel, count, rows, group, outer > 1),
        out_shape=[
            jax.ShapeDtypeStruct((span, rows, frames, TAPS * chans), bf16),
            jax.ShapeDtypeStruct((span, frames, TAPS * chans), bf16),
            jax.ShapeDtypeStruct((total, chans), f32),
        ]
        + [jax.ShapeDtypeStruct(x.shape, bf16) for x in weights],
        in_specs=[near] * len(pieces) + [far] * 5,
        out_specs=[near] * 8,
        scratch_shapes=[scratch(sources * span * lines, chans)] * 2 + [pltpu.SemaphoreType.DMA((5,))],
        compiler_params=params,
    )(*pieces, *weights)
    edge = lax.ppermute(edge, "height", [(0, 1), (1, 0)])
    blocks = pl.pallas_call(
        functools.partial(main_kernel, count, rows, group),
        out_shape=[jax.ShapeDtypeStruct((own * lines, chans), bf16)] * group,
        in_specs=[far] + [near] * 8,
        out_specs=[near] * group,
        scratch_shapes=[
            pltpu.SMEM((frames,), jnp.int32),
            pltpu.VMEM((2,) + edge.shape, bf16),
            pltpu.VMEM((total, chans), f32),
            pltpu.VMEM((total, chans), f32),
            scratch(group * own * lines, chans),
            pltpu.SemaphoreType.DMA(()),
        ],
        compiler_params=params,
    )(in_far(ids), grid, edge, shown, *weights)
    return pl.pallas_call(
        functools.partial(unpack_kernel, group),
        out_shape=jax.ShapeDtypeStruct(video.shape, bf16),
        in_specs=[near] * group,
        out_specs=far,
        scratch_shapes=[
            pltpu.VMEM(video.shape, bf16),
            scratch(lines * cols, chans),
            pltpu.SemaphoreType.DMA((lines,)),
        ],
        compiler_params=params,
    )(*exchanged(blocks, group))


def solution(mesh):
    parts, along, halves = (mesh.shape[a] for a in ("groups", "tm", "height"))

    def run(video, *rest):
        count = video.shape[0] // (parts * along)
        group = min(g for g in range(1, along + 1) if along % g == 0 and (g * count >= REACH or g == along))
        outer = along // group
        split = Mesh(
            np.asarray(mesh.devices).reshape(parts, outer, group, halves),
            ("groups", "outer", "tm", "height"),
        )
        spec = P(("groups", "outer", "tm"), "height", None, None)
        placed = (spec, P("groups"), P(), P(), P(), P(), P())
        return jax.shard_map(
            functools.partial(per_device, outer),
            mesh=split,
            in_specs=placed,
            out_specs=spec,
            check_vma=False,
        )(video, *rest)

    return run
```

time: 51.1 us -> 44.6 us (0.87)
  blocking collectives: 32.7 us -> 0 us
  starting transfers between devices: 0 us -> 23.8 us
  waiting for transfers between devices: 0 us -> 10.5 us
  local copies, waits for them, and re-layouts: 7.22 us -> 0 us
  Pallas kernels: 10.8 us -> 10 us
    all_to_all x2 -> x0, blocking collectives: 32.7 us -> none  [the longest x1 19.4 us: per_device(): lax.all_to_all(packed, ('tm', 'height'), split_axis=0, concat_axis=0, til...]
    ppermute x0 -> x15, starting transfers between devices: none -> 23.8 us  [the longest x14 23.7 us: exchanged(): lax.ppermute(blocks[k], 'tm', [(i, partner(i, k, group)) for i in range(g...]
    ppermute x0 -> x15, waiting for transfers between devices: none -> 10.5 us  [the longest x14 8.99 us: exchanged(): lax.ppermute(blocks[k], 'tm', [(i, partner(i, k, group)) for i in range(g...]
    unnamed x14 -> x0, local copies, waits for them, and re-layouts: 7.22 us -> none
    pallas_call x3 -> x4, Pallas kernels: 10.8 us -> 10 us  [the longest x1 5.84 us: per_device(): pl.pallas_call(functools.partial(main_kernel, count, rows, group), out_sh...]
  transfers between devices with their start and end apart: 0 -> 15, of which waited for: 0 -> 6; matrix products, arithmetic and copies ran while one was open for 0% -> 0% of each run, Pallas kernels for 0% -> 0%
where the time goes in v4:
time: 44.6 us; the launch traced here: 44.4 us
  starting transfers between devices  23.8 us (53%)
  waiting for transfers between devices  10.5 us (24%)
  Pallas kernels  10 us (22%)
    ppermute x14, starting transfers between devices, exchanged(): lax.ppermute(blocks[k], 'tm', [(i, partner(i, k, group)) for i in range(g...  23.7 us
    ppermute x14, waiting for transfers between devices, exchanged(): lax.ppermute(blocks[k], 'tm', [(i, partner(i, k, group)) for i in range(g...  8.99 us
    pallas_call x1, Pallas kernels, per_device(): pl.pallas_call(functools.partial(main_kernel, count, rows, group), out_sh...  5.84 us
    pallas_call x1, Pallas kernels, per_device(): pl.pallas_call(functools.partial(shift_kernel, count, rows, group, outer...  2.25 us
    ppermute x1, waiting for transfers between devices, per_device(): edge = lax.ppermute(edge, 'height', [(0, 1), (1, 0)])  1.5 us
    pallas_call x1, Pallas kernels, per_device(): pl.pallas_call(functools.partial(pack_kernel, group), out_shape=[jax.Shap...  1.14 us
  transfers between devices with their start and end apart: 15, of which 6 were waited for; matrix products, arithmetic and copies ran while one was open for 0% of the time, Pallas kernels for 0%

profile of v4, /device:TPU:0, one launch (start us, length us, event | category | flops | bytes accessed | tf_op | source)
XLA Modules:
  0.0 44.4 jit_solution(15046089628693639567)
XLA Ops:
  0.0 1.1 %shard_map.73 = (bf16[80,256]{1,0:T(8,128)(2,1)S(1)}, bf16[80,256]{1,0:T(8,128)(2,1)S(1)}, bf16[80,256]{1,0:T(8,128)(2,1)S(1)}, bf16[80,256]{1,0:T(8,128)(2,1)S(...) custom-call(bf16[2,4,64,256]{3,2,1,0:T(8,128)(2,1)} %video.1), custom_call_target="tpu_custom_call" | custom-call | tf_op jit(solution)/shard_map/pallas_call | solution.py:261
  1.1 3.0 %collective-permute-start = (bf16[80,256]{1,0:T(8,128)(2,1)S(1)}, bf16[80,256]{1,0:T(8,128)(2,1)S(1)}, u32[]{:S(2)}, u32[]{:S(2)}) collective-permute-start(bf16[80,256]{1,0:T(8,128)(2,1)S(1)} %get-tuple-element.30), channel_id=1, source_target_pairs={{0,2},{2,0},{4,6},{6,4},{8,10},{10,8},{12,14},{14,12},{1,3},{3,1},... | collective-permute-start | bytes 122888 | tf_op jit(solution)/shard_map/ppermute | solution.py:245
  4.2 1.6 %collective-permute-start.1 = (bf16[80,256]{1,0:T(8,128)(2,1)S(1)}, bf16[80,256]{1,0:T(8,128)(2,1)S(1)}, u32[]{:S(2)}, u32[]{:S(2)}) collective-permute-start(bf16[80,256]{1,0:T(8,128)(2,1)S(1)} %get-tuple-element.31), channel_id=1, source_target_pairs={{0,4},{2,6},{4,0},{6,2},{8,12},{10,14},{12,8},{14,10},{1,5},{3,7},... | collective-permute-start | bytes 122888 | tf_op jit(solution)/shard_map/ppermute | solution.py:245
  5.7 0.0 collective-permute-start.2
  5.7 3.0 %collective-permute-start.3 = (bf16[80,256]{1,0:T(8,128)(2,1)S(1)}, bf16[80,256]{1,0:T(8,128)(2,1)S(1)}, u32[]{:S(2)}, u32[]{:S(2)}) collective-permute-start(bf16[80,256]{1,0:T(8,128)(2,1)S(1)} %get-tuple-element.33), channel_id=1, source_target_pairs={{0,8},{2,10},{4,12},{6,14},{8,0},{10,2},{12,4},{14,6},{1,9},{3,11}... | collective-permute-start | bytes 122888 | tf_op jit(solution)/shard_map/ppermute | solution.py:245
  8.7 1.3 %collective-permute-start.4 = (bf16[80,256]{1,0:T(8,128)(2,1)S(1)}, bf16[80,256]{1,0:T(8,128)(2,1)S(1)}, u32[]{:S(2)}, u32[]{:S(2)}) collective-permute-start(bf16[80,256]{1,0:T(8,128)(2,1)S(1)} %get-tuple-element.34), channel_id=1, source_target_pairs={{0,10},{2,8},{4,14},{6,12},{8,2},{10,0},{12,6},{14,4},{1,11},{3,9}... | collective-permute-start | bytes 122888 | tf_op jit(solution)/shard_map/ppermute | solution.py:245
  10.0 0.0 collective-permute-done.refs_1_
  10.0 3.6 %collective-permute-start.5 = (bf16[80,256]{1,0:T(8,128)(2,1)S(1)}, bf16[80,256]{1,0:T(8,128)(2,1)S(1)}, u32[]{:S(2)}, u32[]{:S(2)}) collective-permute-start(bf16[80,256]{1,0:T(8,128)(2,1)S(1)} %get-tuple-element.35), channel_id=1, source_target_pairs={{0,12},{2,14},{4,8},{6,10},{8,4},{10,6},{12,0},{14,2},{1,13},{3,15... | collective-permute-start | bytes 122888 | tf_op jit(solution)/shard_map/ppermute | solution.py:245
  13.6 0.0 collective-permute-done.1.refs_2_
  13.6 0.0 collective-permute-start.6
  13.7 0.0 collective-permute-done.2.refs_3_
  13.7 0.0 collective-permute-done.3.refs_4_
  13.7 1.3 %collective-permute-done.4.refs_5_ = bf16[80,256]{1,0:T(8,128)(2,1)S(1)} collective-permute-done((bf16[80,256]{1,0:T(8,128)(2,1)S(1)}, bf16[80,256]{1,0:T(8,128)(2,1)S(1)}, u32[]{:S(2)}, u32[]{:S(2)}) %collective-permute-start.4) | collective-permute-done | bytes 40992 | tf_op jit(solution)/shard_map/ppermute | solution.py:245
  15.0 1.1 %collective-permute-done.5.refs_6_ = bf16[80,256]{1,0:T(8,128)(2,1)S(1)} collective-permute-done((bf16[80,256]{1,0:T(8,128)(2,1)S(1)}, bf16[80,256]{1,0:T(8,128)(2,1)S(1)}, u32[]{:S(2)}, u32[]{:S(2)}) %collective-permute-start.5) | collective-permute-done | bytes 40992 | tf_op jit(solution)/shard_map/ppermute | solution.py:245
  16.1 4.2 %collective-permute-done.6.refs_7_ = bf16[80,256]{1,0:T(8,128)(2,1)S(1)} collective-permute-done((bf16[80,256]{1,0:T(8,128)(2,1)S(1)}, bf16[80,256]{1,0:T(8,128)(2,1)S(1)}, u32[]{:S(2)}, u32[]{:S(2)}) %collective-permute-start.6) | collective-permute-done | bytes 40992 | tf_op jit(solution)/shard_map/ppermute | solution.py:245
  20.3 2.2 %shard_map.74 = (bf16[10,4,16,768]{3,2,1,0:T(8,128)(2,1)S(1)}, bf16[10,16,768]{2,1,0:T(8,128)(2,1)S(1)}, f32[512,256]{1,0:T(8,128)S(1)}, bf16[3,3,3,256,256]{4,3...) custom-call(bf16[80,256]{1,0:T(8,128)(2,1)S(1)} %get-tuple-element.2, ...), custom_call_target="tpu_custom_call" | custom-call | tf_op jit(solution)/shard_map/pallas_call | solution.py:283
  22.6 0.1 collective-permute-start.7
  22.6 1.5 %collective-permute-done.7.edge = bf16[10,16,768]{2,1,0:T(8,128)(2,1)S(1)} collective-permute-done((bf16[10,16,768]{2,1,0:T(8,128)(2,1)S(1)}, bf16[10,16,768]{2,1,0:T(8,128)(2,1)S(1)}, u32[]{:S(2)}, u32[]{:S(2)}) %collective-permute-start.7) | collective-permute-done | bytes 245792 | tf_op jit(solution)/shard_map/ppermute | solution.py:296
  24.1 5.8 %shard_map.75 = (bf16[64,256]{1,0:T(8,128)(2,1)S(1)}, bf16[64,256]{1,0:T(8,128)(2,1)S(1)}, bf16[64,256]{1,0:T(8,128)(2,1)S(1)}, bf16[64,256]{1,0:T(8,128)(2,1)S(...) custom-call(s32[16]{0:T(128)} %ids_far.1, ...), custom_call_target="tpu_custom_call" | custom-call | tf_op jit(solution)/shard_map/pallas_call | solution.py:297
  30.0 0.6 %collective-permute-start.8 = (bf16[64,256]{1,0:T(8,128)(2,1)S(1)}, bf16[64,256]{1,0:T(8,128)(2,1)S(1)}, u32[]{:S(2)}, u32[]{:S(2)}) collective-permute-start(bf16[64,256]{1,0:T(8,128)(2,1)S(1)} %get-tuple-element.46), channel_id=1, source_target_pairs={{0,2},{2,0},{4,6},{6,4},{8,10},{10,8},{12,14},{14,12},{1,3},{3,1},... | collective-permute-start | bytes 98312 | tf_op jit(solution)/shard_map/ppermute | solution.py:245
  30.6 0.0 collective-permute-start.9
  30.6 2.9 %collective-permute-start.10 = (bf16[64,256]{1,0:T(8,128)(2,1)S(1)}, bf16[64,256]{1,0:T(8,128)(2,1)S(1)}, u32[]{:S(2)}, u32[]{:S(2)}) collective-permute-start(bf16[64,256]{1,0:T(8,128)(2,1)S(1)} %get-tuple-element.48), channel_id=1, source_target_pairs={{0,6},{2,4},{4,2},{6,0},{8,14},{10,12},{12,10},{14,8},{1,7},{3,5},... | collective-permute-start | bytes 98312 | tf_op jit(solution)/shard_map/ppermute | solution.py:245
  33.5 0.0 collective-permute-start.11
  33.5 2.9 %collective-permute-start.12 = (bf16[64,256]{1,0:T(8,128)(2,1)S(1)}, bf16[64,256]{1,0:T(8,128)(2,1)S(1)}, u32[]{:S(2)}, u32[]{:S(2)}) collective-permute-start(bf16[64,256]{1,0:T(8,128)(2,1)S(1)} %get-tuple-element.50), channel_id=1, source_target_pairs={{0,10},{2,8},{4,14},{6,12},{8,2},{10,0},{12,6},{14,4},{1,11},{3,9}... | collective-permute-start | bytes 98312 | tf_op jit(solution)/shard_map/ppermute | solution.py:245
  36.4 0.0 collective-permute-done.8.refs_1_
  36.4 0.5 %collective-permute-start.13 = (bf16[64,256]{1,0:T(8,128)(2,1)S(1)}, bf16[64,256]{1,0:T(8,128)(2,1)S(1)}, u32[]{:S(2)}, u32[]{:S(2)}) collective-permute-start(bf16[64,256]{1,0:T(8,128)(2,1)S(1)} %get-tuple-element.51), channel_id=1, source_target_pairs={{0,12},{2,14},{4,8},{6,10},{8,4},{10,6},{12,0},{14,2},{1,13},{3,15... | collective-permute-start | bytes 98312 | tf_op jit(solution)/shard_map/ppermute | solution.py:245
  36.9 0.0 collective-permute-done.9.refs_2_
  36.9 4.3 %collective-permute-start.14 = (bf16[64,256]{1,0:T(8,128)(2,1)S(1)}, bf16[64,256]{1,0:T(8,128)(2,1)S(1)}, u32[]{:S(2)}, u32[]{:S(2)}) collective-permute-start(bf16[64,256]{1,0:T(8,128)(2,1)S(1)} %get-tuple-element.52), channel_id=1, source_target_pairs={{0,14},{2,12},{4,10},{6,8},{8,6},{10,4},{12,2},{14,0},{1,15},{3,13... | collective-permute-start | bytes 98312 | tf_op jit(solution)/shard_map/ppermute | solution.py:245
  41.2 0.0 collective-permute-done.10.refs_3_
  41.2 0.0 collective-permute-done.11.refs_4_
  41.2 0.0 collective-permute-done.12.refs_5_
  41.2 0.9 %collective-permute-done.13.refs_6_ = bf16[64,256]{1,0:T(8,128)(2,1)S(1)} collective-permute-done((bf16[64,256]{1,0:T(8,128)(2,1)S(1)}, bf16[64,256]{1,0:T(8,128)(2,1)S(1)}, u32[]{:S(2)}, u32[]{:S(2)}) %collective-permute-start.13) | collective-permute-done | bytes 32800 | tf_op jit(solution)/shard_map/ppermute | solution.py:245
  42.2 1.4 %collective-permute-done.14.refs_7_ = bf16[64,256]{1,0:T(8,128)(2,1)S(1)} collective-permute-done((bf16[64,256]{1,0:T(8,128)(2,1)S(1)}, bf16[64,256]{1,0:T(8,128)(2,1)S(1)}, u32[]{:S(2)}, u32[]{:S(2)}) %collective-permute-start.14) | collective-permute-done | bytes 32800 | tf_op jit(solution)/shard_map/ppermute | solution.py:245
  43.5 0.8 %shard_map.76 = bf16[2,4,64,256]{3,2,1,0:T(8,128)(2,1)} custom-call(bf16[64,256]{1,0:T(8,128)(2,1)S(1)} %get-tuple-element.45.refs_0_, bf16[64,256]{1,0:T(8,128)(2,1)S(1)} %collective-permute-done.8.refs_1_, bf16[64,256]{1,0:T(8,128)(2,1)S(1)} %collective-permute-done.9.refs_2_, bf16[64,256]{1,0:T(8,128)(2,1)S(1)} %collective-permute-done.10.refs_3_, ...), custom_call_target="tpu_custom_call" | custom-call | tf_op jit(solution)/shard_map/pallas_call | solution.py:312
Async XLA Ops:
  1.1 8.9 %collective-permute-start = (bf16[80,256]{1,0:T(8,128)(2,1)S(1)}, bf16[80,256]{1,0:T(8,128)(2,1)S(1)}, u32[]{:S(2)}, u32[]{:S(2)}) collective-permute-start(bf16[80,256]{1,0:T(8,128)(2,1)S(1)} %get-tuple-element.30), channel_id=1, source_target_pairs={{0,2},{2,0},{4,6},{6,4},{8,10},{10,8},{12,14},{14,12},{1,3},{3,1},... | collective-permute-start | bytes 122888 | tf_op jit(solution)/shard_map/ppermute | solution.py:245
  4.2 9.5 %collective-permute-start.1 = (bf16[80,256]{1,0:T(8,128)(2,1)S(1)}, bf16[80,256]{1,0:T(8,128)(2,1)S(1)}, u32[]{:S(2)}, u32[]{:S(2)}) collective-permute-start(bf16[80,256]{1,0:T(8,128)(2,1)S(1)} %get-tuple-element.31), channel_id=1, source_target_pairs={{0,4},{2,6},{4,0},{6,2},{8,12},{10,14},{12,8},{14,10},{1,5},{3,7},... | collective-permute-start | bytes 122888 | tf_op jit(solution)/shard_map/ppermute | solution.py:245
  5.7 7.9 %collective-permute-start.2 = (bf16[80,256]{1,0:T(8,128)(2,1)S(1)}, bf16[80,256]{1,0:T(8,128)(2,1)S(1)}, u32[]{:S(2)}, u32[]{:S(2)}) collective-permute-start(bf16[80,256]{1,0:T(8,128)(2,1)S(1)} %get-tuple-element.32), channel_id=1, source_target_pairs={{0,6},{2,4},{4,2},{6,0},{8,14},{10,12},{12,10},{14,8},{1,7},{3,5},... | collective-permute-start | bytes 122888 | tf_op jit(solution)/shard_map/ppermute | solution.py:245
  5.7 7.9 %collective-permute-start.3 = (bf16[80,256]{1,0:T(8,128)(2,1)S(1)}, bf16[80,256]{1,0:T(8,128)(2,1)S(1)}, u32[]{:S(2)}, u32[]{:S(2)}) collective-permute-start(bf16[80,256]{1,0:T(8,128)(2,1)S(1)} %get-tuple-element.33), channel_id=1, source_target_pairs={{0,8},{2,10},{4,12},{6,14},{8,0},{10,2},{12,4},{14,6},{1,9},{3,11}... | collective-permute-start | bytes 122888 | tf_op jit(solution)/shard_map/ppermute | solution.py:245
  8.7 6.2 %collective-permute-start.4 = (bf16[80,256]{1,0:T(8,128)(2,1)S(1)}, bf16[80,256]{1,0:T(8,128)(2,1)S(1)}, u32[]{:S(2)}, u32[]{:S(2)}) collective-permute-start(bf16[80,256]{1,0:T(8,128)(2,1)S(1)} %get-tuple-element.34), channel_id=1, source_target_pairs={{0,10},{2,8},{4,14},{6,12},{8,2},{10,0},{12,6},{14,4},{1,11},{3,9}... | collective-permute-start | bytes 122888 | tf_op jit(solution)/shard_map/ppermute | solution.py:245
  10.0 6.1 %collective-permute-start.5 = (bf16[80,256]{1,0:T(8,128)(2,1)S(1)}, bf16[80,256]{1,0:T(8,128)(2,1)S(1)}, u32[]{:S(2)}, u32[]{:S(2)}) collective-permute-start(bf16[80,256]{1,0:T(8,128)(2,1)S(1)} %get-tuple-element.35), channel_id=1, source_target_pairs={{0,12},{2,14},{4,8},{6,10},{8,4},{10,6},{12,0},{14,2},{1,13},{3,15... | collective-permute-start | bytes 122888 | tf_op jit(solution)/shard_map/ppermute | solution.py:245
  13.6 6.7 %collective-permute-start.6 = (bf16[80,256]{1,0:T(8,128)(2,1)S(1)}, bf16[80,256]{1,0:T(8,128)(2,1)S(1)}, u32[]{:S(2)}, u32[]{:S(2)}) collective-permute-start(bf16[80,256]{1,0:T(8,128)(2,1)S(1)} %get-tuple-element.36), channel_id=1, source_target_pairs={{0,14},{2,12},{4,10},{6,8},{8,6},{10,4},{12,2},{14,0},{1,15},{3,13... | collective-permute-start | bytes 122888 | tf_op jit(solution)/shard_map/ppermute | solution.py:245
  22.6 1.6 %collective-permute-start.7 = (bf16[10,16,768]{2,1,0:T(8,128)(2,1)S(1)}, bf16[10,16,768]{2,1,0:T(8,128)(2,1)S(1)}, u32[]{:S(2)}, u32[]{:S(2)}) collective-permute-start(bf16[10,16,768]{2,1,0:T(8,128)(2,1)S(1)} %get-tuple-element.38), channel_id=1, source_target_pairs={{0,1},{1,0},{2,3},{3,2},{4,5},{5,4},{6,7},{7,6},{8,9},{9,8},{10,11... | collective-permute-start | bytes 737288 | tf_op jit(solution)/shard_map/ppermute | solution.py:296
  30.0 6.5 %collective-permute-start.8 = (bf16[64,256]{1,0:T(8,128)(2,1)S(1)}, bf16[64,256]{1,0:T(8,128)(2,1)S(1)}, u32[]{:S(2)}, u32[]{:S(2)}) collective-permute-start(bf16[64,256]{1,0:T(8,128)(2,1)S(1)} %get-tuple-element.46), channel_id=1, source_target_pairs={{0,2},{2,0},{4,6},{6,4},{8,10},{10,8},{12,14},{14,12},{1,3},{3,1},... | collective-permute-start | bytes 98312 | tf_op jit(solution)/shard_map/ppermute | solution.py:245
  30.6 6.3 %collective-permute-start.9 = (bf16[64,256]{1,0:T(8,128)(2,1)S(1)}, bf16[64,256]{1,0:T(8,128)(2,1)S(1)}, u32[]{:S(2)}, u32[]{:S(2)}) collective-permute-start(bf16[64,256]{1,0:T(8,128)(2,1)S(1)} %get-tuple-element.47), channel_id=1, source_target_pairs={{0,4},{2,6},{4,0},{6,2},{8,12},{10,14},{12,8},{14,10},{1,5},{3,7},... | collective-permute-start | bytes 98312 | tf_op jit(solution)/shard_map/ppermute | solution.py:245
  30.6 10.6 %collective-permute-start.10 = (bf16[64,256]{1,0:T(8,128)(2,1)S(1)}, bf16[64,256]{1,0:T(8,128)(2,1)S(1)}, u32[]{:S(2)}, u32[]{:S(2)}) collective-permute-start(bf16[64,256]{1,0:T(8,128)(2,1)S(1)} %get-tuple-element.48), channel_id=1, source_target_pairs={{0,6},{2,4},{4,2},{6,0},{8,14},{10,12},{12,10},{14,8},{1,7},{3,5},... | collective-permute-start | bytes 98312 | tf_op jit(solution)/shard_map/ppermute | solution.py:245
  33.5 7.7 %collective-permute-start.11 = (bf16[64,256]{1,0:T(8,128)(2,1)S(1)}, bf16[64,256]{1,0:T(8,128)(2,1)S(1)}, u32[]{:S(2)}, u32[]{:S(2)}) collective-permute-start(bf16[64,256]{1,0:T(8,128)(2,1)S(1)} %get-tuple-element.49), channel_id=1, source_target_pairs={{0,8},{2,10},{4,12},{6,14},{8,0},{10,2},{12,4},{14,6},{1,9},{3,11}... | collective-permute-start | bytes 98312 | tf_op jit(solution)/shard_map/ppermute | solution.py:245
  33.5 7.7 %collective-permute-start.12 = (bf16[64,256]{1,0:T(8,128)(2,1)S(1)}, bf16[64,256]{1,0:T(8,128)(2,1)S(1)}, u32[]{:S(2)}, u32[]{:S(2)}) collective-permute-start(bf16[64,256]{1,0:T(8,128)(2,1)S(1)} %get-tuple-element.50), channel_id=1, source_target_pairs={{0,10},{2,8},{4,14},{6,12},{8,2},{10,0},{12,6},{14,4},{1,11},{3,9}... | collective-permute-start | bytes 98312 | tf_op jit(solution)/shard_map/ppermute | solution.py:245
  36.4 5.7 %collective-permute-start.13 = (bf16[64,256]{1,0:T(8,128)(2,1)S(1)}, bf16[64,256]{1,0:T(8,128)(2,1)S(1)}, u32[]{:S(2)}, u32[]{:S(2)}) collective-permute-start(bf16[64,256]{1,0:T(8,128)(2,1)S(1)} %get-tuple-element.51), channel_id=1, source_target_pairs={{0,12},{2,14},{4,8},{6,10},{8,4},{10,6},{12,0},{14,2},{1,13},{3,15... | collective-permute-start | bytes 98312 | tf_op jit(solution)/shard_map/ppermute | solution.py:245
  36.9 6.6 %collective-permute-start.14 = (bf16[64,256]{1,0:T(8,128)(2,1)S(1)}, bf16[64,256]{1,0:T(8,128)(2,1)S(1)}, u32[]{:S(2)}, u32[]{:S(2)}) collective-permute-start(bf16[64,256]{1,0:T(8,128)(2,1)S(1)} %get-tuple-element.52), channel_id=1, source_target_pairs={{0,14},{2,12},{4,10},{6,8},{8,6},{10,4},{12,2},{14,0},{1,15},{3,13... | collective-permute-start | bytes 98312 | tf_op jit(solution)/shard_map/ppermute | solution.py:245

commit v5 on v4

--- a/solution.py
+++ b/solution.py
@@ -37,10 +37,6 @@
     return pltpu.VMEM((chans // LANES, rows, LANES), f32)
 
 
-def partner(me, k, group):
-    return me ^ k if group & (group - 1) == 0 else (k - me) % group
-
-
 def rms(wide):
     return wide * lax.rsqrt(jnp.mean(wide * wide, axis=-1, keepdims=True) + 1e-06)
 
@@ -53,7 +49,7 @@
 
 
 def pack_kernel(group, video, *refs):
-    blocks, (local, wide, sems) = refs[:group], refs[group:]
+    out, local, wide, sems = refs
     count, rows, cols, chans = video.shape
     lines = count * rows
     stride = cols + 2 * EDGE
@@ -72,44 +68,30 @@
     for at, copy in enumerate(copies):
         copy.wait()
         fill(wide, at * stride + EDGE, local[at // rows, at % rows].astype(f32))
-    me = lax.axis_index("tm")
     together = 16 // lines
     for k in range(group):
-        start = partner(me, k, group) * own + EDGE - 1
+        start = k * own + EDGE - 1
         for w in range(0, span, together):
             tile = jnp.concatenate([get(wide, start + w + i, lines, stride) for i in range(together)], axis=0)
-            blocks[k][pl.ds(w * lines, 16), :] = tile.astype(bf16)
-
-
-def shift_kernel(count, rows, group, before, *refs):
-    blocks, refs = refs[:group], refs[group:]
-    past, refs = (refs[0], refs[1:]) if before else (None, refs)
-    far, refs = refs[:5], refs[5:]
+            out[k, pl.ds(w * lines, 16), :] = tile.astype(bf16)
+
+
+def shift_kernel(count, rows, *refs):
+    video, far, refs = refs[0], refs[1:6], refs[6:]
     grid, edge, shown, refs = refs[0], refs[1], refs[2], refs[3:]
     near, (vid, act, sems) = refs[:5], refs[5:]
     copies = [pltpu.make_async_copy(src, dst, sems.at[i]) for i, (src, dst) in enumerate(zip(far, near))]
     for copy in copies:
         copy.start()
-    step, chans = blocks[0].shape
+    sources, step, chans = video.shape
     lines = count * rows
     span = step // lines
     own = span - 2
-    frames = grid.shape[2]
-    sources = frames // count
-    me = lax.axis_index("tm")
-
-    def take(block, source):
-        start = pl.multiple_of(source * step, 16)
-        wide = block.astype(f32)
-        fill(vid, start, wide)
-        normal = rms(wide)
-        fill(act, start, normal / (1.0 + jnp.exp(-normal)))
-
-    for k in range(group):
-        source = partner(me, k, group)
-        take(blocks[k][...], source + sources - group)
-        if before:
-            take(past[k], source)
+    frames = sources * count
+    xs = video[...].reshape(sources * step, chans).astype(f32)
+    fill(vid, 0, xs)
+    normal = rms(xs)
+    fill(act, 0, normal / (1.0 + jnp.exp(-normal)))
 
     def pixel(ref, w, r):
         return [get(ref, w * lines + t * rows + r, sources, step) for t in range(count)]
@@ -138,7 +120,7 @@
 def main_kernel(
     count, rows, group, ids_far, grid, edge, given, conv_weight, w_query, w_key, w_value, w_output, *refs
 ):
-    blocks, (ids, border, total, shown, res, sem) = refs[:group], refs[group:]
+    out, ids, border, total, shown, res, sem = refs
     ids_copy = pltpu.make_async_copy(ids_far, ids, sem)
     ids_copy.start()
     span, _, frames, _ = grid.shape
@@ -213,21 +195,14 @@
             for t in range(count):
                 start = ((w * rows + r) * count + t + 1) * sources - group
                 put(res, w * lines + t * rows + r, group, back, encoded[start : start + group])
-    me = lax.axis_index("tm")
-    for k in range(group):
-        start = pl.multiple_of(partner(me, k, group) * back, 16)
-        block = jnp.concatenate([res[i, pl.ds(start, back), :] for i in range(res.shape[0])], axis=1)
-        blocks[k][...] = block.astype(bf16)
-
-
-def unpack_kernel(group, *refs):
-    blocks, (out, local, wide, sems) = refs[:group], refs[group:]
+    done = jnp.concatenate([res[i] for i in range(res.shape[0])], axis=1)
+    out[...] = done.astype(bf16).reshape(out.shape)
+
+
+def unpack_kernel(packed, out, local, wide, sems):
     count, rows, cols, chans = out.shape
     lines = count * rows
-    me = lax.axis_index("tm")
-    for k in range(group):
-        start = pl.multiple_of(partner(me, k, group) * blocks[k].shape[0], 16)
-        fill(wide, start, blocks[k][...].astype(f32))
+    fill(wide, 0, packed[...].reshape(lines * cols, chans).astype(f32))
     copies = []
     for at in range(lines):
         place = (at // rows, at % rows)
@@ -239,11 +214,8 @@
         copy.wait()
 
 
-def exchanged(blocks, group):
-    back = [blocks[0]]
-    for k in range(1, group):
-        back.append(lax.ppermute(blocks[k], "tm", [(i, partner(i, k, group)) for i in range(group)]))
-    return back
+def exchanged(blocks):
+    return lax.all_to_all(blocks, "tm", split_axis=0, concat_axis=0, tiled=True)
 
 
 def per_device(outer, video, block_ids, conv_weight, w_query, w_key, w_value, w_output):
@@ -260,9 +232,9 @@
 
     blocks = pl.pallas_call(
         functools.partial(pack_kernel, group),
-        out_shape=[jax.ShapeDtypeStruct((span * lines, chans), bf16)] * group,
+        out_shape=jax.ShapeDtypeStruct((group, span * lines, chans), bf16),
         in_specs=[far],
-        out_specs=[near] * group,
+        out_specs=near,
         scratch_shapes=[
             pltpu.VMEM(video.shape, bf16),
             scratch(lines * (cols + 2 * EDGE), chans),
@@ -270,35 +242,35 @@
         ],
         compiler_params=params,
     )(in_far(video))
-    pieces = exchanged(blocks, group)
+    piece = exchanged(blocks)
     ids = block_ids
     if outer > 1:
-        before = lax.ppermute(jnp.stack(pieces), "outer", [(i, i + 1) for i in range(outer - 1)])
-        pieces = pieces + [before]
+        before = lax.ppermute(piece, "outer", [(i, i + 1) for i in range(outer - 1)])
+        piece = jnp.concatenate([before, piece], axis=0)
         ids = jnp.concatenate([jnp.full((group * count,), -2, jnp.int32), ids])
         ids = lax.dynamic_slice(ids, (lax.axis_index("outer") * group * count,), (2 * group * count,))
-    sources = group * (2 if outer > 1 else 1)
+    sources = piece.shape[0]
     frames = sources * count
     total = own * rows * frames
     grid, edge, shown, *weights = pl.pallas_call(
-        functools.partial(shift_kernel, count, rows, group, outer > 1),
+        functools.partial(shift_kernel, count, rows),
         out_shape=[
             jax.ShapeDtypeStruct((span, rows, frames, TAPS * chans), bf16),
             jax.ShapeDtypeStruct((span, frames, TAPS * chans), bf16),
             jax.ShapeDtypeStruct((total, chans), f32),
         ]
         + [jax.ShapeDtypeStruct(x.shape, bf16) for x in weights],
-        in_specs=[near] * len(pieces) + [far] * 5,
+        in_specs=[near] + [far] * 5,
         out_specs=[near] * 8,
         scratch_shapes=[scratch(sources * span * lines, chans)] * 2 + [pltpu.SemaphoreType.DMA((5,))],
         compiler_params=params,
-    )(*pieces, *weights)
+    )(piece, *weights)
     edge = lax.ppermute(edge, "height", [(0, 1), (1, 0)])
     blocks = pl.pallas_call(
         functools.partial(main_kernel, count, rows, group),
-        out_shape=[jax.ShapeDtypeStruct((own * lines, chans), bf16)] * group,
+        out_shape=jax.ShapeDtypeStruct((group, own * lines, chans), bf16),
         in_specs=[far] + [near] * 8,
-        out_specs=[near] * group,
+        out_specs=near,
         scratch_shapes=[
             pltpu.SMEM((frames,), jnp.int32),
             pltpu.VMEM((2,) + edge.shape, bf16),
@@ -310,9 +282,9 @@
         compiler_params=params,
     )(in_far(ids), grid, edge, shown, *weights)
     return pl.pallas_call(
-        functools.partial(unpack_kernel, group),
+        unpack_kernel,
         out_shape=jax.ShapeDtypeStruct(video.shape, bf16),
-        in_specs=[near] * group,
+        in_specs=[near],
         out_specs=far,
         scratch_shapes=[
             pltpu.VMEM(video.shape, bf16),
@@ -320,7 +292,7 @@
             pltpu.SemaphoreType.DMA((lines,)),
         ],
         compiler_params=params,
-    )(*exchanged(blocks, group))
+    )(exchanged(blocks))
 
 
 def solution(mesh):

time: 44.6 us -> 41.9 us (0.939)
  blocking collectives: 0 us -> 30 us
  starting transfers between devices: 23.8 us -> 0.07 us
  waiting for transfers between devices: 10.5 us -> 1.5 us
    all_to_all x0 -> x2, blocking collectives: none -> 30 us  [exchanged(): return lax.all_to_all(blocks, 'tm', split_axis=0, concat_axis=0, tiled=True)]
    ppermute x14 -> x0, starting transfers between devices: 23.7 us -> none  [exchanged(): lax.ppermute(blocks[k], 'tm', [(i, partner(i, k, group)) for i in range(g...]
    ppermute x14 -> x0, waiting for transfers between devices: 8.99 us -> none  [exchanged(): lax.ppermute(blocks[k], 'tm', [(i, partner(i, k, group)) for i in range(g...]
  transfers between devices with their start and end apart: 15 -> 1, of which waited for: 6 -> 1; matrix products, arithmetic and copies ran while one was open for 0% -> 0% of each run, Pallas kernels for 0% -> 0%
where the time goes in v5:
time: 41.9 us; the launch traced here: 41.7 us
  blocking collectives  30 us (72%)
  Pallas kernels  10.1 us (24%)
  waiting for transfers between devices  1.5 us (4%)
    all_to_all x2, blocking collectives, exchanged(): return lax.all_to_all(blocks, 'tm', split_axis=0, concat_axis=0, tiled=True)  30 us
    pallas_call x1, Pallas kernels, per_device(): pl.pallas_call(functools.partial(main_kernel, count, rows, group), out_sh...  5.79 us
    pallas_call x1, Pallas kernels, per_device(): pl.pallas_call(functools.partial(shift_kernel, count, rows), out_shape=[j...  2.39 us
    ppermute x1, waiting for transfers between devices, per_device(): edge = lax.ppermute(edge, 'height', [(0, 1), (1, 0)])  1.5 us
    pallas_call x1, Pallas kernels, per_device(): pl.pallas_call(functools.partial(pack_kernel, group), out_shape=jax.Shape...  1.11 us
  transfers between devices with their start and end apart: 1, of which 1 were waited for; matrix products, arithmetic and copies ran while one was open for 0% of the time, Pallas kernels for 0%

profile of v5, /device:TPU:0, one launch (start us, length us, event | category | flops | bytes accessed | tf_op | source)
XLA Modules:
  0.0 41.7 jit_solution(10759987672814694028)
XLA Ops:
  0.0 1.1 %shard_map.73 = bf16[8,80,256]{2,1,0:T(8,128)(2,1)S(1)} custom-call(bf16[2,4,64,256]{3,2,1,0:T(8,128)(2,1)} %video.1), custom_call_target="tpu_custom_call" | custom-call | tf_op jit(solution)/shard_map/pallas_call | solution.py:233
  1.1 18.0 %all_to_all.10.refs_0_ = bf16[8,80,256]{2,1,0:T(8,128)(2,1)S(1)} all-to-all(bf16[8,80,256]{2,1,0:T(8,128)(2,1)S(1)} %shard_map.73), channel_id=1, replica_groups=mesh['groups'=2,'tm'=8,'height'=2] {'tm'}, dimensions={0} | all-to-all | bytes 655360 | tf_op jit(solution)/shard_map/all_to_all | solution.py:218
  19.1 2.4 %shard_map.74 = (bf16[10,4,16,768]{3,2,1,0:T(8,128)(2,1)S(1)}, bf16[10,16,768]{2,1,0:T(8,128)(2,1)S(1)}, f32[512,256]{1,0:T(8,128)S(1)}, bf16[3,3,3,256,256]{4,3...) custom-call(bf16[8,80,256]{2,1,0:T(8,128)(2,1)S(1)} %all_to_all.10.r, ...), custom_call_target="tpu_custom_call" | custom-call | tf_op jit(solution)/shard_map/pallas_call | solution.py:255
  21.5 0.1 collective-permute-start
  21.5 1.5 %collective-permute-done.edge = bf16[10,16,768]{2,1,0:T(8,128)(2,1)S(1)} collective-permute-done((bf16[10,16,768]{2,1,0:T(8,128)(2,1)S(1)}, bf16[10,16,768]{2,1,0:T(8,128)(2,1)S(1)}, u32[]{:S(2)}, u32[]{:S(2)}) %collective-permute-start) | collective-permute-done | bytes 245792 | tf_op jit(solution)/shard_map/ppermute | solution.py:268
  23.0 5.8 %shard_map.75 = bf16[8,64,256]{2,1,0:T(8,128)(2,1)S(1)} custom-call(s32[16]{0:T(128)} %ids_far.1, bf16[10,4,16,768]{3,2,1,0:T(8,128)(2,1)S(1)} %get-tuple-element.13.grid, bf16[10,16,768]{2,1,0:T(8,128)(2,1)S(1)} %collective-permute-done.edge, f32[512,256]{1,0:T(8,128)S(1)} %get-tuple-element.15.given, ...), custom_call_target="tpu_custom_call" | custom-call | tf_op jit(solution)/shard_map/pallas_call | solution.py:269
  28.8 12.0 %all_to_all.11.packed = bf16[8,64,256]{2,1,0:T(8,128)(2,1)S(1)} all-to-all(bf16[8,64,256]{2,1,0:T(8,128)(2,1)S(1)} %shard_map.75), channel_id=1, replica_groups=mesh['groups'=2,'tm'=8,'height'=2] {'tm'}, dimensions={0} | all-to-all | bytes 524288 | tf_op jit(solution)/shard_map/all_to_all | solution.py:218
  40.8 0.8 %shard_map.76 = bf16[2,4,64,256]{3,2,1,0:T(8,128)(2,1)} custom-call(bf16[8,64,256]{2,1,0:T(8,128)(2,1)S(1)} %all_to_all.11.packed), custom_call_target="tpu_custom_call" | custom-call | tf_op jit(solution)/shard_map/pallas_call | solution.py:284
Async XLA Ops:
  21.5 1.6 %collective-permute-start = (bf16[10,16,768]{2,1,0:T(8,128)(2,1)S(1)}, bf16[10,16,768]{2,1,0:T(8,128)(2,1)S(1)}, u32[]{:S(2)}, u32[]{:S(2)}) collective-permute-start(bf16[10,16,768]{2,1,0:T(8,128)(2,1)S(1)} %get-tuple-element.14), channel_id=1, source_target_pairs={{0,1},{1,0},{2,3},{3,2},{4,5},{5,4},{6,7},{7,6},{8,9},{9,8},{10,11... | collective-permute-start | bytes 737288 | tf_op jit(solution)/shard_map/ppermute | solution.py:268

commit v6 on v5

--- a/solution.py
+++ b/solution.py
@@ -76,79 +76,97 @@
             out[k, pl.ds(w * lines, 16), :] = tile.astype(bf16)
 
 
-def shift_kernel(count, rows, *refs):
-    video, far, refs = refs[0], refs[1:6], refs[6:]
-    grid, edge, shown, refs = refs[0], refs[1], refs[2], refs[3:]
-    near, (vid, act, sems) = refs[:5], refs[5:]
-    copies = [pltpu.make_async_copy(src, dst, sems.at[i]) for i, (src, dst) in enumerate(zip(far, near))]
-    for copy in copies:
+def frames_of(ref, w, r, count, rows, sources, step):
+    return [get(ref, w * count * rows + t * rows + r, sources, step) for t in range(count)]
+
+
+def shifted(now):
+    count = len(now)
+    sources, chans = now[0].shape
+    first = lax.broadcasted_iota(jnp.int32, (sources, chans), 0) == 0
+    past = [jnp.where(first, 0.0, pltpu.roll(x, 1, 0)) for x in now]
+    ordered = past + now
+    taps = []
+    for a in range(TAPS):
+        start = count - (TAPS - 1 - a)
+        taps.append(jnp.concatenate(ordered[start : start + count], 0).astype(bf16))
+    return jnp.concatenate(taps, axis=1)
+
+
+def activated(wide):
+    normal = rms(wide)
+    return normal / (1.0 + jnp.exp(-normal))
+
+
+def depth(parts):
+    return parts[0] if len(parts) == 1 else jnp.concatenate(parts, axis=-1)
+
+
+def edge_kernel(count, rows, video, edge, vid):
+    sources, step, chans = video.shape
+    span = step // (count * rows)
+    fill(vid, 0, video[...].reshape(sources * step, chans).astype(f32))
+    row = (rows - 1) * (1 - lax.axis_index("height"))
+    for w in range(span):
+        edge[w] = shifted([activated(x) for x in frames_of(vid, w, row, count, rows, sources, step)])
+
+
+def shift_kernel(count, rows, video, *refs):
+    far, (total, *near), (vid, act, grid, conv_sems, sems) = refs[:5], refs[5:11], refs[11:]
+    conv_far, conv_weight = far[0], near[0]
+    order = [1, 0, 2]
+    taps = {b: pltpu.make_async_copy(conv_far.at[:, b], conv_weight.at[:, b], conv_sems.at[b]) for b in order}
+    others = [pltpu.make_async_copy(far[i], near[i], sems.at[i - 1]) for i in range(1, 5)]
+    for copy in list(taps.values()) + others:
         copy.start()
     sources, step, chans = video.shape
-    lines = count * rows
-    span = step // lines
+    span = step // (count * rows)
     own = span - 2
     frames = sources * count
     xs = video[...].reshape(sources * step, chans).astype(f32)
     fill(vid, 0, xs)
-    normal = rms(xs)
-    fill(act, 0, normal / (1.0 + jnp.exp(-normal)))
-
-    def pixel(ref, w, r):
-        return [get(ref, w * lines + t * rows + r, sources, step) for t in range(count)]
-
-    first = lax.broadcasted_iota(jnp.int32, (sources, chans), 0) == 0
-
-    def earlier(x):
-        return jnp.where(first, 0.0, pltpu.roll(x, 1, 0))
-
+    fill(act, 0, activated(xs))
     for w in range(span):
         for r in range(rows):
-            now = pixel(act, w, r)
-            ordered = [earlier(x) for x in now] + now
-            for a in range(TAPS):
-                shift = TAPS - 1 - a
-                picked = [ordered[count + t - shift] for t in range(count)]
-                grid[w, r, :, a * chans : (a + 1) * chans] = jnp.concatenate(picked, 0).astype(bf16)
+            grid[w, r] = shifted(frames_of(act, w, r, count, rows, sources, step))
             if 1 <= w <= own:
-                shown[pl.ds(((w - 1) * rows + r) * frames, frames), :] = jnp.concatenate(pixel(vid, w, r), 0)
-    lower = lax.axis_index("height")
-    edge[...] = grid[:, (rows - 1) * (1 - lower)]
-    for copy in copies:
+                total[w - 1, r] = jnp.concatenate(frames_of(vid, w, r, count, rows, sources, step), 0)
+
+    for b in order:
+        taps[b].wait()
+        low, high = max(0, 1 - b), min(rows, rows + 1 - b)
+        window = depth([grid[e : e + own, low + b - 1 : high + b - 1] for e in range(TAPS)])
+        window = window.reshape(own * (high - low) * frames, TAPS * TAPS * chans)
+        weight = jnp.concatenate([conv_weight[a, b, e] for e in range(TAPS) for a in range(TAPS)], axis=0)
+        part = jnp.dot(window, weight, preferred_element_type=f32)
+        total[:, low:high] = total[:, low:high] + part.reshape(own, high - low, frames, chans)
+    for copy in others:
         copy.wait()
 
 
 def main_kernel(
-    count, rows, group, ids_far, grid, edge, given, conv_weight, w_query, w_key, w_value, w_output, *refs
+    count, rows, group, ids_far, edge, given, conv_weight, w_query, w_key, w_value, w_output, *refs
 ):
-    out, ids, border, total, shown, res, sem = refs
+    out, ids, shown, res, sem = refs
     ids_copy = pltpu.make_async_copy(ids_far, ids, sem)
     ids_copy.start()
-    span, _, frames, _ = grid.shape
-    chans = w_query.shape[0]
-    own = span - 2
+    own, _, frames, chans = given.shape
     sources = frames // count
     lines = count * rows
     heads = chans // HD
     back = own * lines
-    several = own // 2 if own % 2 == 0 else own
+    several = max(n for n in range(1, own + 1) if own % n == 0 and (n == 1 or n * rows * frames <= LANES))
     area = several * rows * frames
+
     lower = lax.axis_index("height")
-    border[1 - lower] = edge[...]
-    border[lower] = jnp.zeros(edge.shape, bf16)
-
-    for b in range(TAPS):
-        for e in range(TAPS):
-            ahead = [border[0, e : e + own][:, None]] if b == 0 else []
-            after = [border[1, e : e + own][:, None]] if b == TAPS - 1 else []
-            inner = grid[e : e + own, max(b - 1, 0) : min(b - 1 + rows, rows)]
-            window = jnp.concatenate(ahead + [inner] + after, axis=1) if ahead or after else inner
-            window = window.reshape(own * rows * frames, TAPS * chans)
-            weight = jnp.concatenate([conv_weight[a, b, e] for a in range(TAPS)], axis=0)
-            part = jnp.dot(window, weight, preferred_element_type=f32)
-            total[...] = part if b == e == 0 else total[...] + part
-
-    hidden = (given[...] + total[...]).astype(bf16).astype(f32)
-    shown[...] = hidden
+    window = depth([edge[e : e + own] for e in range(TAPS)]).reshape(own * frames, TAPS * TAPS * chans)
+    b = (TAPS - 1) * (1 - lower)
+    weight = jnp.concatenate([conv_weight[a, b, e] for e in range(TAPS) for a in range(TAPS)], axis=0)
+    part = jnp.dot(window, weight, preferred_element_type=f32).reshape(own, frames, chans)
+    for r in range(rows):
+        shown[:, r] = given[:, r] + jnp.where(r == (rows - 1) * (1 - lower), part, 0.0)
+
+    hidden = shown[...].reshape(own * rows * frames, chans).astype(bf16).astype(f32)
     normed = rms(hidden).astype(bf16)
     query, keys, values = (
         jnp.dot(normed, weight[...], preferred_element_type=f32).astype(bf16) for weight in (w_query, w_key, w_value)
@@ -189,7 +207,7 @@
             attended = jnp.where(head_of == h, mixed[h * area : (h + 1) * area], attended)
         gone.append(attended.astype(bf16))
     attended = jnp.concatenate(gone, axis=0)
-    encoded = shown[...] + jnp.dot(attended, w_output[...], preferred_element_type=f32)
+    encoded = hidden + jnp.dot(attended, w_output[...], preferred_element_type=f32)
     for w in range(own):
         for r in range(rows):
             for t in range(count):
@@ -251,36 +269,44 @@
         ids = lax.dynamic_slice(ids, (lax.axis_index("outer") * group * count,), (2 * group * count,))
     sources = piece.shape[0]
     frames = sources * count
-    total = own * rows * frames
-    grid, edge, shown, *weights = pl.pallas_call(
+    stored = scratch(sources * span * lines, chans)
+    edge = pl.pallas_call(
+        functools.partial(edge_kernel, count, rows),
+        out_shape=jax.ShapeDtypeStruct((span, frames, TAPS * chans), bf16),
+        in_specs=[near],
+        out_specs=near,
+        scratch_shapes=[stored],
+        compiler_params=params,
+    )(piece)
+    edge = lax.ppermute(edge, "height", [(0, 1), (1, 0)])
+    total, *weights = pl.pallas_call(
         functools.partial(shift_kernel, count, rows),
-        out_shape=[
-            jax.ShapeDtypeStruct((span, rows, frames, TAPS * chans), bf16),
-            jax.ShapeDtypeStruct((span, frames, TAPS * chans), bf16),
-            jax.ShapeDtypeStruct((total, chans), f32),
-        ]
+        out_shape=[jax.ShapeDtypeStruct((own, rows, frames, chans), f32)]
         + [jax.ShapeDtypeStruct(x.shape, bf16) for x in weights],
         in_specs=[near] + [far] * 5,
-        out_specs=[near] * 8,
-        scratch_shapes=[scratch(sources * span * lines, chans)] * 2 + [pltpu.SemaphoreType.DMA((5,))],
+        out_specs=[near] * 6,
+        scratch_shapes=[
+            stored,
+            stored,
+            pltpu.VMEM((span, rows, frames, TAPS * chans), bf16),
+            pltpu.SemaphoreType.DMA((TAPS,)),
+            pltpu.SemaphoreType.DMA((4,)),
+        ],
         compiler_params=params,
     )(piece, *weights)
-    edge = lax.ppermute(edge, "height", [(0, 1), (1, 0)])
     blocks = pl.pallas_call(
         functools.partial(main_kernel, count, rows, group),
         out_shape=jax.ShapeDtypeStruct((group, own * lines, chans), bf16),
-        in_specs=[far] + [near] * 8,
+        in_specs=[far] + [near] * 7,
         out_specs=near,
         scratch_shapes=[
             pltpu.SMEM((frames,), jnp.int32),
-            pltpu.VMEM((2,) + edge.shape, bf16),
-            pltpu.VMEM((total, chans), f32),
-            pltpu.VMEM((total, chans), f32),
+            pltpu.VMEM((own, rows, frames, chans), f32),
             scratch(group * own * lines, chans),
             pltpu.SemaphoreType.DMA(()),
         ],
         compiler_params=params,
-    )(in_far(ids), grid, edge, shown, *weights)
+    )(in_far(ids), edge, total, *weights)
     return pl.pallas_call(
         unpack_kernel,
         out_shape=jax.ShapeDtypeStruct(video.shape, bf16),

time: 41.9 us -> 41 us (0.979)
  waiting for transfers between devices: 1.5 us -> 0.01 us
    pallas_call x1, Pallas kernels: 5.79 us -> 3.26 us  [per_device(): pl.pallas_call(functools.partial(main_kernel, count, rows, group), out_sh...]
    pallas_call x1, Pallas kernels: 2.39 us -> 4.84 us  [per_device(): pl.pallas_call(functools.partial(shift_kernel, count, rows), out_shape=[j...]
    ppermute x1, waiting for transfers between devices: 1.5 us -> 0.01 us  [per_device(): edge = lax.ppermute(edge, 'height', [(0, 1), (1, 0)])]
  transfers between devices with their start and end apart: 1 -> 1, of which waited for: 1 -> 0; matrix products, arithmetic and copies ran while one was open for 0% -> 0% of each run, Pallas kernels for 0% -> 12%
where the time goes in v6:
time: 41 us; the launch traced here: 40.7 us
  blocking collectives  30.3 us (74%)
  Pallas kernels  10.3 us (25%)
    all_to_all x2, blocking collectives, exchanged(): return lax.all_to_all(blocks, 'tm', split_axis=0, concat_axis=0, tiled=True)  30.3 us
    pallas_call x1, Pallas kernels, per_device(): pl.pallas_call(functools.partial(shift_kernel, count, rows), out_shape=[j...  4.84 us
    pallas_call x1, Pallas kernels, per_device(): pl.pallas_call(functools.partial(main_kernel, count, rows, group), out_sh...  3.26 us
    pallas_call x1, Pallas kernels, per_device(): pl.pallas_call(functools.partial(pack_kernel, group), out_shape=jax.Shape...  1.11 us
  transfers between devices with their start and end apart: 1, of which 0 were waited for; matrix products, arithmetic and copies ran while one was open for 0% of the time, Pallas kernels for 12%

profile of v6, /device:TPU:0, one launch (start us, length us, event | category | flops | bytes accessed | tf_op | source)
XLA Modules:
  0.0 40.7 jit_solution(16320349251739683453)
XLA Ops:
  0.0 1.1 %shard_map.73 = bf16[8,80,256]{2,1,0:T(8,128)(2,1)S(1)} custom-call(bf16[2,4,64,256]{3,2,1,0:T(8,128)(2,1)} %video.1), custom_call_target="tpu_custom_call" | custom-call | tf_op jit(solution)/shard_map/pallas_call | solution.py:251
  1.1 18.0 %all_to_all.10.video = bf16[8,80,256]{2,1,0:T(8,128)(2,1)S(1)} all-to-all(bf16[8,80,256]{2,1,0:T(8,128)(2,1)S(1)} %shard_map.73), channel_id=1, replica_groups=mesh['groups'=2,'tm'=8,'height'=2] {'tm'}, dimensions={0} | all-to-all | bytes 655360 | tf_op jit(solution)/shard_map/all_to_all | solution.py:236
  19.1 0.3 shard_map.74
  19.3 0.1 collective-permute-start
  19.4 4.8 %shard_map.75 = (f32[8,4,16,256]{3,2,1,0:T(8,128)S(1)}, bf16[3,3,3,256,256]{4,3,2,1,0:T(8,128)(2,1)S(1)}, bf16[256,256]{1,0:T(8,128)(2,1)S(1)}, bf16[256,256]{1,...) custom-call(bf16[8,80,256]{2,1,0:T(8,128)(2,1)S(1)} %all_to_all.10.video, ...), custom_call_target="tpu_custom_call" | custom-call | tf_op jit(solution)/shard_map/pallas_call | solution.py:282
  24.3 0.0 collective-permute-done.edge
  24.3 3.3 %shard_map.76 = bf16[8,64,256]{2,1,0:T(8,128)(2,1)S(1)} custom-call(s32[16]{0:T(128)} %ids_far.1, bf16[10,16,768]{2,1,0:T(8,128)(2,1)S(1)} %collective-permute-done.edge, f32[8,4,16,256]{3,2,1,0:T(8,128)S(1)} %get-tuple-element.11.given, bf16[3,3,3,256,256]{4,3,2,1,0:T(8,128)(2,1)S(1)} %get-tuple-element.12.conv_weight, ...), custom_call_target="tpu_custom_call" | custom-call | tf_op jit(solution)/shard_map/pallas_call | solution.py:297
  27.5 12.4 %all_to_all.11.packed = bf16[8,64,256]{2,1,0:T(8,128)(2,1)S(1)} all-to-all(bf16[8,64,256]{2,1,0:T(8,128)(2,1)S(1)} %shard_map.76), channel_id=1, replica_groups=mesh['groups'=2,'tm'=8,'height'=2] {'tm'}, dimensions={0} | all-to-all | bytes 524288 | tf_op jit(solution)/shard_map/all_to_all | solution.py:236
  39.9 0.8 %shard_map.77 = bf16[2,4,64,256]{3,2,1,0:T(8,128)(2,1)} custom-call(bf16[8,64,256]{2,1,0:T(8,128)(2,1)S(1)} %all_to_all.11.packed), custom_call_target="tpu_custom_call" | custom-call | tf_op jit(solution)/shard_map/pallas_call | solution.py:310
Async XLA Ops:
  19.3 4.9 %collective-permute-start = (bf16[10,16,768]{2,1,0:T(8,128)(2,1)S(1)}, bf16[10,16,768]{2,1,0:T(8,128)(2,1)S(1)}, u32[]{:S(2)}, u32[]{:S(2)}) collective-permute-start(bf16[10,16,768]{2,1,0:T(8,128)(2,1)S(1)} %shard_map.74), channel_id=1, source_target_pairs={{0,1},{1,0},{2,3},{3,2},{4,5},{5,4},{6,7},{7,6},{8,9},{9,8},{10,11... | collective-permute-start | bytes 737288 | tf_op jit(solution)/shard_map/ppermute | solution.py:281

commit v7 on v6

--- a/solution.py
+++ b/solution.py
@@ -112,7 +112,7 @@
 
 
 def shift_kernel(count, rows, video, *refs):
-    far, (total, *near), (vid, act, grid, conv_sems, sems) = refs[:5], refs[5:11], refs[11:]
+    far, (total, *near), (vid, grid, conv_sems, sems) = refs[:5], refs[5:11], refs[11:]
     conv_far, conv_weight = far[0], near[0]
     order = [1, 0, 2]
     taps = {b: pltpu.make_async_copy(conv_far.at[:, b], conv_weight.at[:, b], conv_sems.at[b]) for b in order}
@@ -123,14 +123,13 @@
     span = step // (count * rows)
     own = span - 2
     frames = sources * count
-    xs = video[...].reshape(sources * step, chans).astype(f32)
-    fill(vid, 0, xs)
-    fill(act, 0, activated(xs))
+    fill(vid, 0, video[...].reshape(sources * step, chans).astype(f32))
     for w in range(span):
         for r in range(rows):
-            grid[w, r] = shifted(frames_of(act, w, r, count, rows, sources, step))
+            now = frames_of(vid, w, r, count, rows, sources, step)
+            grid[w, r] = shifted([activated(x) for x in now])
             if 1 <= w <= own:
-                total[w - 1, r] = jnp.concatenate(frames_of(vid, w, r, count, rows, sources, step), 0)
+                total[w - 1, r] = jnp.concatenate(now, 0)
 
     for b in order:
         taps[b].wait()
@@ -189,23 +188,26 @@
     col_p = divided(lax.broadcasted_iota(jnp.int32, (area, area), 1), frames)[0]
     permit = (row_p == col_p) & (col_t <= row_t) & (col_b >= row_b - 1)
     bias = jnp.where(permit, 0.0, -1e30)
-    head_of = lax.broadcasted_iota(jnp.int32, (area, chans), 1) // HD
+    head_of = divided(lax.broadcasted_iota(jnp.int32, (area, chans), 1), HD)[0]
+    scaled = [jnp.where(head_of == h, HD ** (-0.5), 0.0).astype(bf16) for h in range(heads)]
+    ones = jnp.ones((area, LANES), bf16)
 
     gone = []
     for w in range(0, own, several):
         part = slice(w * rows * frames, w * rows * frames + area)
-        single = jnp.concatenate(
-            [jnp.where(head_of == h, query[part], jnp.zeros((), bf16)) for h in range(heads)], axis=0
-        )
+        single = jnp.concatenate([query[part] * scaled[h] for h in range(heads)], axis=0)
         scores = lax.dot_general(single, keys[part], (((1,), (1,)), ((), ())), preferred_element_type=f32)
-        scores = scores * HD ** (-0.5) + jnp.concatenate([bias] * heads, axis=0)
-        expo = jnp.exp(scores - jnp.max(scores, axis=-1, keepdims=True))
-        weights = (expo * (1.0 / jnp.sum(expo, axis=-1, keepdims=True))).astype(bf16)
-        mixed = jnp.dot(weights, values[part], preferred_element_type=f32)
-        attended = mixed[:area]
+        scores = scores + jnp.concatenate([bias] * heads, axis=0)
+        expo = jnp.exp(scores - jnp.max(scores, axis=-1, keepdims=True)).astype(bf16)
+        mixed = jnp.dot(expo, values[part], preferred_element_type=f32)
+        sums = jnp.dot(expo, ones, preferred_element_type=f32)
+        sums = jnp.concatenate([sums] * (chans // LANES), axis=1)
+        attended, under = mixed[:area], sums[:area]
         for h in range(1, heads):
-            attended = jnp.where(head_of == h, mixed[h * area : (h + 1) * area], attended)
-        gone.append(attended.astype(bf16))
+            rows_of = slice(h * area, (h + 1) * area)
+            attended = jnp.where(head_of == h, mixed[rows_of], attended)
+            under = jnp.where(head_of == h, sums[rows_of], under)
+        gone.append((attended / under).astype(bf16))
     attended = jnp.concatenate(gone, axis=0)
     encoded = hidden + jnp.dot(attended, w_output[...], preferred_element_type=f32)
     for w in range(own):
@@ -287,7 +289,6 @@
         out_specs=[near] * 6,
         scratch_shapes=[
             stored,
-            stored,
             pltpu.VMEM((span, rows, frames, TAPS * chans), bf16),
             pltpu.SemaphoreType.DMA((TAPS,)),
             pltpu.SemaphoreType.DMA((4,)),

time: 41 us -> 41.1 us (level)
  no operation moved by 1% of the time
where the time goes in v7:
time: 41.1 us; the launch traced here: 40.8 us
  blocking collectives  30.3 us (74%)
  Pallas kernels  10.4 us (25%)
    all_to_all x2, blocking collectives, exchanged(): return lax.all_to_all(blocks, 'tm', split_axis=0, concat_axis=0, tiled=True)  30.3 us
    pallas_call x1, Pallas kernels, per_device(): pl.pallas_call(functools.partial(shift_kernel, count, rows), out_shape=[j...  4.81 us
    pallas_call x1, Pallas kernels, per_device(): pl.pallas_call(functools.partial(main_kernel, count, rows, group), out_sh...  3.4 us
    pallas_call x1, Pallas kernels, per_device(): pl.pallas_call(functools.partial(pack_kernel, group), out_shape=jax.Shape...  1.11 us
  transfers between devices with their start and end apart: 1, of which 0 were waited for; matrix products, arithmetic and copies ran while one was open for 0% of the time, Pallas kernels for 12%

profile of v7, /device:TPU:0, one launch (start us, length us, event | category | flops | bytes accessed | tf_op | source)
XLA Modules:
  0.0 40.8 jit_solution(13404239698060821203)
XLA Ops:
  0.0 1.1 %shard_map.73 = bf16[8,80,256]{2,1,0:T(8,128)(2,1)S(1)} custom-call(bf16[2,4,64,256]{3,2,1,0:T(8,128)(2,1)} %video.1), custom_call_target="tpu_custom_call" | custom-call | tf_op jit(solution)/shard_map/pallas_call | solution.py:253
  1.1 18.0 %all_to_all.10.video = bf16[8,80,256]{2,1,0:T(8,128)(2,1)S(1)} all-to-all(bf16[8,80,256]{2,1,0:T(8,128)(2,1)S(1)} %shard_map.73), channel_id=1, replica_groups=mesh['groups'=2,'tm'=8,'height'=2] {'tm'}, dimensions={0} | all-to-all | bytes 655360 | tf_op jit(solution)/shard_map/all_to_all | solution.py:238
  19.1 0.3 shard_map.74
  19.3 0.1 collective-permute-start
  19.4 4.8 %shard_map.75 = (f32[8,4,16,256]{3,2,1,0:T(8,128)S(1)}, bf16[3,3,3,256,256]{4,3,2,1,0:T(8,128)(2,1)S(1)}, bf16[256,256]{1,0:T(8,128)(2,1)S(1)}, bf16[256,256]{1,...) custom-call(bf16[8,80,256]{2,1,0:T(8,128)(2,1)S(1)} %all_to_all.10.video, ...), custom_call_target="tpu_custom_call" | custom-call | tf_op jit(solution)/shard_map/pallas_call | solution.py:284
  24.2 0.0 collective-permute-done.edge
  24.2 3.4 %shard_map.76 = bf16[8,64,256]{2,1,0:T(8,128)(2,1)S(1)} custom-call(s32[16]{0:T(128)} %ids_far.1, bf16[10,16,768]{2,1,0:T(8,128)(2,1)S(1)} %collective-permute-done.edge, f32[8,4,16,256]{3,2,1,0:T(8,128)S(1)} %get-tuple-element.11.given, bf16[3,3,3,256,256]{4,3,2,1,0:T(8,128)(2,1)S(1)} %get-tuple-element.12.conv_weight, ...), custom_call_target="tpu_custom_call" | custom-call | tf_op jit(solution)/shard_map/pallas_call | solution.py:298
  27.7 12.4 %all_to_all.11.packed = bf16[8,64,256]{2,1,0:T(8,128)(2,1)S(1)} all-to-all(bf16[8,64,256]{2,1,0:T(8,128)(2,1)S(1)} %shard_map.76), channel_id=1, replica_groups=mesh['groups'=2,'tm'=8,'height'=2] {'tm'}, dimensions={0} | all-to-all | bytes 524288 | tf_op jit(solution)/shard_map/all_to_all | solution.py:238
  40.0 0.8 %shard_map.77 = bf16[2,4,64,256]{3,2,1,0:T(8,128)(2,1)} custom-call(bf16[8,64,256]{2,1,0:T(8,128)(2,1)S(1)} %all_to_all.11.packed), custom_call_target="tpu_custom_call" | custom-call | tf_op jit(solution)/shard_map/pallas_call | solution.py:311
Async XLA Ops:
  19.3 4.9 %collective-permute-start = (bf16[10,16,768]{2,1,0:T(8,128)(2,1)S(1)}, bf16[10,16,768]{2,1,0:T(8,128)(2,1)S(1)}, u32[]{:S(2)}, u32[]{:S(2)}) collective-permute-start(bf16[10,16,768]{2,1,0:T(8,128)(2,1)S(1)} %shard_map.74), channel_id=1, source_target_pairs={{0,1},{1,0},{2,3},{3,2},{4,5},{5,4},{6,7},{7,6},{8,9},{9,8},{10,11... | collective-permute-start | bytes 737288 | tf_op jit(solution)/shard_map/ppermute | solution.py:283

commit v8 on v7

--- a/solution.py
+++ b/solution.py
@@ -123,6 +123,7 @@
     span = step // (count * rows)
     own = span - 2
     frames = sources * count
+    half = own // 2 if own % 2 == 0 else own
     fill(vid, 0, video[...].reshape(sources * step, chans).astype(f32))
     for w in range(span):
         for r in range(rows):
@@ -134,11 +135,13 @@
     for b in order:
         taps[b].wait()
         low, high = max(0, 1 - b), min(rows, rows + 1 - b)
-        window = depth([grid[e : e + own, low + b - 1 : high + b - 1] for e in range(TAPS)])
-        window = window.reshape(own * (high - low) * frames, TAPS * TAPS * chans)
         weight = jnp.concatenate([conv_weight[a, b, e] for e in range(TAPS) for a in range(TAPS)], axis=0)
-        part = jnp.dot(window, weight, preferred_element_type=f32)
-        total[:, low:high] = total[:, low:high] + part.reshape(own, high - low, frames, chans)
+        for w in range(0, own, half):
+            window = depth([grid[w + e : w + e + half, low + b - 1 : high + b - 1] for e in range(TAPS)])
+            window = window.reshape(half * (high - low) * frames, TAPS * TAPS * chans)
+            part = jnp.dot(window, weight, preferred_element_type=f32)
+            some = total.at[w : w + half, low:high]
+            some[...] = some[...] + part.reshape(half, high - low, frames, chans)
     for copy in others:
         copy.wait()
 
@@ -189,25 +192,21 @@
     permit = (row_p == col_p) & (col_t <= row_t) & (col_b >= row_b - 1)
     bias = jnp.where(permit, 0.0, -1e30)
     head_of = divided(lax.broadcasted_iota(jnp.int32, (area, chans), 1), HD)[0]
-    scaled = [jnp.where(head_of == h, HD ** (-0.5), 0.0).astype(bf16) for h in range(heads)]
-    ones = jnp.ones((area, LANES), bf16)
+    single = [jnp.where(head_of == h, 1.0, 0.0).astype(bf16) for h in range(heads)]
 
     gone = []
     for w in range(0, own, several):
         part = slice(w * rows * frames, w * rows * frames + area)
-        single = jnp.concatenate([query[part] * scaled[h] for h in range(heads)], axis=0)
-        scores = lax.dot_general(single, keys[part], (((1,), (1,)), ((), ())), preferred_element_type=f32)
-        scores = scores + jnp.concatenate([bias] * heads, axis=0)
-        expo = jnp.exp(scores - jnp.max(scores, axis=-1, keepdims=True)).astype(bf16)
-        mixed = jnp.dot(expo, values[part], preferred_element_type=f32)
-        sums = jnp.dot(expo, ones, preferred_element_type=f32)
-        sums = jnp.concatenate([sums] * (chans // LANES), axis=1)
-        attended, under = mixed[:area], sums[:area]
-        for h in range(1, heads):
-            rows_of = slice(h * area, (h + 1) * area)
-            attended = jnp.where(head_of == h, mixed[rows_of], attended)
-            under = jnp.where(head_of == h, sums[rows_of], under)
-        gone.append((attended / under).astype(bf16))
+        heads_keys = jnp.concatenate([keys[part] * mask for mask in single], axis=0)
+        heads_values = jnp.concatenate([values[part] * mask for mask in single], axis=0)
+        scores = lax.dot_general(query[part], heads_keys, (((1,), (1,)), ((), ())), preferred_element_type=f32)
+        weights = []
+        for h in range(heads):
+            score = scores[:, h * area : (h + 1) * area] * HD ** (-0.5) + bias
+            expo = jnp.exp(score - jnp.max(score, axis=-1, keepdims=True))
+            weights.append((expo * (1.0 / jnp.sum(expo, axis=-1, keepdims=True))).astype(bf16))
+        attended = jnp.dot(jnp.concatenate(weights, axis=1), heads_values, preferred_element_type=f32)
+        gone.append(attended.astype(bf16))
     attended = jnp.concatenate(gone, axis=0)
     encoded = hidden + jnp.dot(attended, w_output[...], preferred_element_type=f32)
     for w in range(own):

time: 41.1 us -> 40.1 us (0.976)
  Pallas kernels: 10.4 us -> 9.36 us
    pallas_call x1, Pallas kernels: 4.81 us -> 3.58 us  [per_device(): pl.pallas_call(functools.partial(shift_kernel, count, rows), out_shape=[j...]
  transfers between devices with their start and end apart: 1 -> 1, of which waited for: 0 -> 0; matrix products, arithmetic and copies ran while one was open for 0% -> 0% of each run, Pallas kernels for 12% -> 9%
where the time goes in v8:
time: 40.1 us; the launch traced here: 39.8 us
  blocking collectives  30.3 us (76%)
  Pallas kernels  9.36 us (23%)
    all_to_all x2, blocking collectives, exchanged(): return lax.all_to_all(blocks, 'tm', split_axis=0, concat_axis=0, tiled=True)  30.3 us
    pallas_call x1, Pallas kernels, per_device(): pl.pallas_call(functools.partial(main_kernel, count, rows, group), out_sh...  3.6 us
    pallas_call x1, Pallas kernels, per_device(): pl.pallas_call(functools.partial(shift_kernel, count, rows), out_shape=[j...  3.58 us
    pallas_call x1, Pallas kernels, per_device(): pl.pallas_call(functools.partial(pack_kernel, group), out_shape=jax.Shape...  1.11 us
    pallas_call x1, Pallas kernels, per_device(): pl.pallas_call(unpack_kernel, out_shape=jax.ShapeDtypeStruct(video.shape,...  0.81 us
  transfers between devices with their start and end apart: 1, of which 0 were waited for; matrix products, arithmetic and copies ran while one was open for 0% of the time, Pallas kernels for 9%

profile of v8, /device:TPU:0, one launch (start us, length us, event | category | flops | bytes accessed | tf_op | source)
XLA Modules:
  0.0 39.8 jit_solution(8419899831331002485)
XLA Ops:
  0.0 1.1 %shard_map.73 = bf16[8,80,256]{2,1,0:T(8,128)(2,1)S(1)} custom-call(bf16[2,4,64,256]{3,2,1,0:T(8,128)(2,1)} %video.1), custom_call_target="tpu_custom_call" | custom-call | tf_op jit(solution)/shard_map/pallas_call | solution.py:252
  1.1 18.0 %all_to_all.10.video = bf16[8,80,256]{2,1,0:T(8,128)(2,1)S(1)} all-to-all(bf16[8,80,256]{2,1,0:T(8,128)(2,1)S(1)} %shard_map.73), channel_id=1, replica_groups=mesh['groups'=2,'tm'=8,'height'=2] {'tm'}, dimensions={0} | all-to-all | bytes 655360 | tf_op jit(solution)/shard_map/all_to_all | solution.py:237
  19.1 0.3 shard_map.74
  19.3 0.1 collective-permute-start
  19.4 3.6 %shard_map.75 = (f32[8,4,16,256]{3,2,1,0:T(8,128)S(1)}, bf16[3,3,3,256,256]{4,3,2,1,0:T(8,128)(2,1)S(1)}, bf16[256,256]{1,0:T(8,128)(2,1)S(1)}, bf16[256,256]{1,...) custom-call(bf16[8,80,256]{2,1,0:T(8,128)(2,1)S(1)} %all_to_all.10.video, ...), custom_call_target="tpu_custom_call" | custom-call | tf_op jit(solution)/shard_map/pallas_call | solution.py:283
  23.0 0.0 collective-permute-done.edge
  23.0 3.6 %shard_map.76 = bf16[8,64,256]{2,1,0:T(8,128)(2,1)S(1)} custom-call(s32[16]{0:T(128)} %ids_far.1, bf16[10,16,768]{2,1,0:T(8,128)(2,1)S(1)} %collective-permute-done.edge, f32[8,4,16,256]{3,2,1,0:T(8,128)S(1)} %get-tuple-element.11.given, bf16[3,3,3,256,256]{4,3,2,1,0:T(8,128)(2,1)S(1)} %get-tuple-element.12.conv_weight, ...), custom_call_target="tpu_custom_call" | custom-call | tf_op jit(solution)/shard_map/pallas_call | solution.py:297
  26.6 12.3 %all_to_all.11.packed = bf16[8,64,256]{2,1,0:T(8,128)(2,1)S(1)} all-to-all(bf16[8,64,256]{2,1,0:T(8,128)(2,1)S(1)} %shard_map.76), channel_id=1, replica_groups=mesh['groups'=2,'tm'=8,'height'=2] {'tm'}, dimensions={0} | all-to-all | bytes 524288 | tf_op jit(solution)/shard_map/all_to_all | solution.py:237
  39.0 0.8 %shard_map.77 = bf16[2,4,64,256]{3,2,1,0:T(8,128)(2,1)} custom-call(bf16[8,64,256]{2,1,0:T(8,128)(2,1)S(1)} %all_to_all.11.packed), custom_call_target="tpu_custom_call" | custom-call | tf_op jit(solution)/shard_map/pallas_call | solution.py:310
Async XLA Ops:
  19.3 3.7 %collective-permute-start = (bf16[10,16,768]{2,1,0:T(8,128)(2,1)S(1)}, bf16[10,16,768]{2,1,0:T(8,128)(2,1)S(1)}, u32[]{:S(2)}, u32[]{:S(2)}) collective-permute-start(bf16[10,16,768]{2,1,0:T(8,128)(2,1)S(1)} %shard_map.74), channel_id=1, source_target_pairs={{0,1},{1,0},{2,3},{3,2},{4,5},{5,4},{6,7},{7,6},{8,9},{9,8},{10,11... | collective-permute-start | bytes 737288 | tf_op jit(solution)/shard_map/ppermute | solution.py:282

commit v9 on v8

--- a/solution.py
+++ b/solution.py
@@ -111,8 +111,29 @@
         edge[w] = shifted([activated(x) for x in frames_of(vid, w, row, count, rows, sources, step)])
 
 
-def shift_kernel(count, rows, video, *refs):
-    far, (total, *near), (vid, grid, conv_sems, sems) = refs[:5], refs[5:11], refs[11:]
+def fill_bias(bias, ids, frames, count):
+    area = bias.shape[0]
+    sources = frames // count
+
+    def place_of(at):
+        pixel, place = divided(at, frames)
+        inner, source = divided(place, sources)
+        frame = source * count + inner
+        block = jnp.zeros(at.shape, jnp.int32)
+        for s in range(frames):
+            block = jnp.where(frame == s, ids[s], block)
+        return pixel, frame, block
+
+    row_p, row_t, row_b = place_of(lax.broadcasted_iota(jnp.int32, (area, area), 0))
+    col_p, col_t, col_b = place_of(lax.broadcasted_iota(jnp.int32, (1, area), 1))
+    permit = (row_p == col_p) & (col_t <= row_t) & (col_b >= row_b - 1)
+    bias[...] = jnp.where(permit, 0.0, -1e30)
+
+
+def shift_kernel(count, rows, video, ids_far, *refs):
+    far, (total, bias, *near), (vid, grid, ids, conv_sems, sems, ids_sem) = refs[:5], refs[5:12], refs[12:]
+    ids_copy = pltpu.make_async_copy(ids_far, ids, ids_sem)
+    ids_copy.start()
     conv_far, conv_weight = far[0], near[0]
     order = [1, 0, 2]
     taps = {b: pltpu.make_async_copy(conv_far.at[:, b], conv_weight.at[:, b], conv_sems.at[b]) for b in order}
@@ -123,7 +144,7 @@
     span = step // (count * rows)
     own = span - 2
     frames = sources * count
-    half = own // 2 if own % 2 == 0 else own
+    half = own // 4 if own % 4 == 0 else own
     fill(vid, 0, video[...].reshape(sources * step, chans).astype(f32))
     for w in range(span):
         for r in range(rows):
@@ -132,6 +153,8 @@
             if 1 <= w <= own:
                 total[w - 1, r] = jnp.concatenate(now, 0)
 
+    ids_copy.wait()
+    fill_bias(bias, ids, frames, count)
     for b in order:
         taps[b].wait()
         low, high = max(0, 1 - b), min(rows, rows + 1 - b)
@@ -147,73 +170,66 @@
 
 
 def main_kernel(
-    count, rows, group, ids_far, edge, given, conv_weight, w_query, w_key, w_value, w_output, *refs
+    count, rows, group, edge, given, bias, conv_weight, w_query, w_key, w_value, w_output, *refs
 ):
-    out, ids, shown, res, sem = refs
-    ids_copy = pltpu.make_async_copy(ids_far, ids, sem)
-    ids_copy.start()
+    out, res = refs
     own, _, frames, chans = given.shape
     sources = frames // count
     lines = count * rows
     heads = chans // HD
     back = own * lines
-    several = max(n for n in range(1, own + 1) if own % n == 0 and (n == 1 or n * rows * frames <= LANES))
-    area = several * rows * frames
+    area = bias.shape[0]
+    several = area // (rows * frames)
 
     lower = lax.axis_index("height")
-    window = depth([edge[e : e + own] for e in range(TAPS)]).reshape(own * frames, TAPS * TAPS * chans)
     b = (TAPS - 1) * (1 - lower)
-    weight = jnp.concatenate([conv_weight[a, b, e] for e in range(TAPS) for a in range(TAPS)], axis=0)
-    part = jnp.dot(window, weight, preferred_element_type=f32).reshape(own, frames, chans)
-    for r in range(rows):
-        shown[:, r] = given[:, r] + jnp.where(r == (rows - 1) * (1 - lower), part, 0.0)
-
-    hidden = shown[...].reshape(own * rows * frames, chans).astype(bf16).astype(f32)
-    normed = rms(hidden).astype(bf16)
-    query, keys, values = (
-        jnp.dot(normed, weight[...], preferred_element_type=f32).astype(bf16) for weight in (w_query, w_key, w_value)
-    )
-
-    ids_copy.wait()
-
-    def place_of(shape, dim):
-        inner, source = divided(lax.broadcasted_iota(jnp.int32, shape, dim) % frames, sources)
-        frame = source * count + inner
-        block = jnp.zeros(shape, jnp.int32)
-        for s in range(frames):
-            block = jnp.where(frame == s, ids[s], block)
-        return frame, block
-
-    pixels = several * rows
-    row_t, row_b = (jnp.concatenate([x] * pixels, 0) for x in place_of((frames, area), 0))
-    col_t, col_b = place_of((1, area), 1)
-    row_p = divided(lax.broadcasted_iota(jnp.int32, (area, area), 0), frames)[0]
-    col_p = divided(lax.broadcasted_iota(jnp.int32, (area, area), 1), frames)[0]
-    permit = (row_p == col_p) & (col_t <= row_t) & (col_b >= row_b - 1)
-    bias = jnp.where(permit, 0.0, -1e30)
+    part = jnp.zeros((own * frames, chans), f32)
+    for e in range(TAPS):
+        window = edge[e : e + own].reshape(own * frames, TAPS * chans)
+        weight = jnp.concatenate([conv_weight[a, b, e] for a in range(TAPS)], axis=0)
+        part = part + jnp.dot(window, weight, preferred_element_type=f32)
+    part = part.reshape(own, frames, chans)
+
     head_of = divided(lax.broadcasted_iota(jnp.int32, (area, chans), 1), HD)[0]
     single = [jnp.where(head_of == h, 1.0, 0.0).astype(bf16) for h in range(heads)]
-
-    gone = []
-    for w in range(0, own, several):
-        part = slice(w * rows * frames, w * rows * frames + area)
-        heads_keys = jnp.concatenate([keys[part] * mask for mask in single], axis=0)
-        heads_values = jnp.concatenate([values[part] * mask for mask in single], axis=0)
-        scores = lax.dot_general(query[part], heads_keys, (((1,), (1,)), ((), ())), preferred_element_type=f32)
-        weights = []
-        for h in range(heads):
-            score = scores[:, h * area : (h + 1) * area] * HD ** (-0.5) + bias
-            expo = jnp.exp(score - jnp.max(score, axis=-1, keepdims=True))
-            weights.append((expo * (1.0 / jnp.sum(expo, axis=-1, keepdims=True))).astype(bf16))
-        attended = jnp.dot(jnp.concatenate(weights, axis=1), heads_values, preferred_element_type=f32)
-        gone.append(attended.astype(bf16))
-    attended = jnp.concatenate(gone, axis=0)
-    encoded = hidden + jnp.dot(attended, w_output[...], preferred_element_type=f32)
-    for w in range(own):
+    scaled = [mask * jnp.asarray(HD ** (-0.5), bf16) for mask in single]
+
+    half = own // 2 if own % (2 * several) == 0 else own
+    for start in range(0, own, half):
+        lines_of = []
         for r in range(rows):
-            for t in range(count):
-                start = ((w * rows + r) * count + t + 1) * sources - group
-                put(res, w * lines + t * rows + r, group, back, encoded[start : start + group])
+            row = given[start : start + half, r]
+            row = row + jnp.where(r == (rows - 1) * (1 - lower), part[start : start + half], 0.0)
+            lines_of.append(row[:, None])
+        hidden = jnp.concatenate(lines_of, axis=1).reshape(half * rows * frames, chans).astype(bf16).astype(f32)
+        normed = rms(hidden).astype(bf16)
+        query, keys, values = (
+            jnp.dot(normed, weight[...], preferred_element_type=f32).astype(bf16)
+            for weight in (w_query, w_key, w_value)
+        )
+        gone = []
+        for at in range(0, half * rows * frames, area):
+            group_of = slice(at, at + area)
+            queries = jnp.concatenate([query[group_of] * mask for mask in scaled], axis=0)
+            scores = lax.dot_general(
+                queries, keys[group_of], (((1,), (1,)), ((), ())), preferred_element_type=f32
+            )
+            weights = []
+            for h in range(heads):
+                score = scores[h * area : (h + 1) * area] + bias[...]
+                expo = jnp.exp(score - jnp.max(score, axis=-1, keepdims=True))
+                weights.append((expo * (1.0 / jnp.sum(expo, axis=-1, keepdims=True))).astype(bf16))
+            heads_values = jnp.concatenate([values[group_of] * mask for mask in single], axis=0)
+            attended = jnp.dot(jnp.concatenate(weights, axis=1), heads_values, preferred_element_type=f32)
+            gone.append(attended.astype(bf16))
+        attended = jnp.concatenate(gone, axis=0)
+        encoded = hidden + jnp.dot(attended, w_output[...], preferred_element_type=f32)
+        for w in range(half):
+            for r in range(rows):
+                for t in range(count):
+                    first = ((w * rows + r) * count + t + 1) * sources - group
+                    place = (start + w) * lines + t * rows + r
+                    put(res, place, group, back, encoded[first : first + group])
     done = jnp.concatenate([res[i] for i in range(res.shape[0])], axis=1)
     out[...] = done.astype(bf16).reshape(out.shape)
 
@@ -280,33 +296,35 @@
         compiler_params=params,
     )(piece)
     edge = lax.ppermute(edge, "height", [(0, 1), (1, 0)])
-    total, *weights = pl.pallas_call(
+    several = max(n for n in range(1, own + 1) if own % n == 0 and (n == 1 or n * rows * frames <= LANES))
+    area = several * rows * frames
+    total, bias, *weights = pl.pallas_call(
         functools.partial(shift_kernel, count, rows),
-        out_shape=[jax.ShapeDtypeStruct((own, rows, frames, chans), f32)]
+        out_shape=[
+            jax.ShapeDtypeStruct((own, rows, frames, chans), f32),
+            jax.ShapeDtypeStruct((area, area), f32),
+        ]
         + [jax.ShapeDtypeStruct(x.shape, bf16) for x in weights],
-        in_specs=[near] + [far] * 5,
-        out_specs=[near] * 6,
+        in_specs=[near] + [far] * 6,
+        out_specs=[near] * 7,
         scratch_shapes=[
             stored,
             pltpu.VMEM((span, rows, frames, TAPS * chans), bf16),
+            pltpu.SMEM((frames,), jnp.int32),
             pltpu.SemaphoreType.DMA((TAPS,)),
             pltpu.SemaphoreType.DMA((4,)),
+            pltpu.SemaphoreType.DMA(()),
         ],
         compiler_params=params,
-    )(piece, *weights)
+    )(piece, in_far(ids), *weights)
     blocks = pl.pallas_call(
         functools.partial(main_kernel, count, rows, group),
         out_shape=jax.ShapeDtypeStruct((group, own * lines, chans), bf16),
-        in_specs=[far] + [near] * 7,
+        in_specs=[near] * 8,
         out_specs=near,
-        scratch_shapes=[
-            pltpu.SMEM((frames,), jnp.int32),
-            pltpu.VMEM((own, rows, frames, chans), f32),
-            scratch(group * own * lines, chans),
-            pltpu.SemaphoreType.DMA(()),
-        ],
-        compiler_params=params,
-    )(in_far(ids), edge, total, *weights)
+        scratch_shapes=[scratch(group * own * lines, chans)],
+        compiler_params=params,
+    )(edge, total, bias, *weights)
     return pl.pallas_call(
         unpack_kernel,
         out_shape=jax.ShapeDtypeStruct(video.shape, bf16),

time: 40.1 us -> 39.9 us (level)
    pallas_call x1, Pallas kernels: 3.6 us -> 2.98 us  [per_device(): pl.pallas_call(functools.partial(main_kernel, count, rows, group), out_sh...]
    pallas_call x1, Pallas kernels: 3.58 us -> 4.02 us  [per_device(): pl.pallas_call(functools.partial(shift_kernel, count, rows), out_shape=[j...]
  transfers between devices with their start and end apart: 1 -> 1, of which waited for: 0 -> 0; matrix products, arithmetic and copies ran while one was open for 0% -> 0% of each run, Pallas kernels for 9% -> 10%
where the time goes in v9:
time: 39.9 us; the launch traced here: 39.6 us
  blocking collectives  30.3 us (76%)
  Pallas kernels  9.18 us (23%)
    all_to_all x2, blocking collectives, exchanged(): return lax.all_to_all(blocks, 'tm', split_axis=0, concat_axis=0, tiled=True)  30.3 us
    pallas_call x1, Pallas kernels, per_device(): pl.pallas_call(functools.partial(shift_kernel, count, rows), out_shape=[j...  4.02 us
    pallas_call x1, Pallas kernels, per_device(): pl.pallas_call(functools.partial(main_kernel, count, rows, group), out_sh...  2.98 us
    pallas_call x1, Pallas kernels, per_device(): pl.pallas_call(functools.partial(pack_kernel, group), out_shape=jax.Shape...  1.11 us
    pallas_call x1, Pallas kernels, per_device(): pl.pallas_call(unpack_kernel, out_shape=jax.ShapeDtypeStruct(video.shape,...  0.81 us
  transfers between devices with their start and end apart: 1, of which 0 were waited for; matrix products, arithmetic and copies ran while one was open for 0% of the time, Pallas kernels for 10%

profile of v9, /device:TPU:0, one launch (start us, length us, event | category | flops | bytes accessed | tf_op | source)
XLA Modules:
  0.0 39.6 jit_solution(13647603026305718471)
XLA Ops:
  0.0 1.1 %shard_map.73 = bf16[8,80,256]{2,1,0:T(8,128)(2,1)S(1)} custom-call(bf16[2,4,64,256]{3,2,1,0:T(8,128)(2,1)} %video.1), custom_call_target="tpu_custom_call" | custom-call | tf_op jit(solution)/shard_map/pallas_call | solution.py:268
  1.1 18.0 %all_to_all.10.video = bf16[8,80,256]{2,1,0:T(8,128)(2,1)S(1)} all-to-all(bf16[8,80,256]{2,1,0:T(8,128)(2,1)S(1)} %shard_map.73), channel_id=1, replica_groups=mesh['groups'=2,'tm'=8,'height'=2] {'tm'}, dimensions={0} | all-to-all | bytes 655360 | tf_op jit(solution)/shard_map/all_to_all | solution.py:253
  19.1 0.3 shard_map.74
  19.3 0.1 collective-permute-start
  19.4 4.0 %shard_map.75 = (f32[8,4,16,256]{3,2,1,0:T(8,128)S(1)}, f32[128,128]{1,0:T(8,128)S(1)}, bf16[3,3,3,256,256]{4,3,2,1,0:T(8,128)(2,1)S(1)}, bf16[256,256]{1,0:T(8,...) custom-call(bf16[8,80,256]{2,1,0:T(8,128)(2,1)S(1)} %all_to_all.10.video, ...), custom_call_target="tpu_custom_call" | custom-call | tf_op jit(solution)/shard_map/pallas_call | solution.py:301
  23.4 0.0 collective-permute-done.edge
  23.5 3.0 %shard_map.76 = bf16[8,64,256]{2,1,0:T(8,128)(2,1)S(1)} custom-call(bf16[10,16,768]{2,1,0:T(8,128)(2,1)S(1)} %collective-permute-done.edge, f32[8,4,16,256]{3,2,1,0:T(8,128)S(1)} %get-tuple-element.12.given, f32[128,128]{1,0:T(8,128)S(1)} %get-tuple-element.13.bias, bf16[3,3,3,256,256]{4,3,2,1,0:T(8,128)(2,1)S(1)} %get-tuple-element.14.conv_weight, ...), custom_call_target="tpu_custom_call" | custom-call | tf_op jit(solution)/shard_map/pallas_call | solution.py:320
  26.4 12.4 %all_to_all.11.packed = bf16[8,64,256]{2,1,0:T(8,128)(2,1)S(1)} all-to-all(bf16[8,64,256]{2,1,0:T(8,128)(2,1)S(1)} %shard_map.76), channel_id=1, replica_groups=mesh['groups'=2,'tm'=8,'height'=2] {'tm'}, dimensions={0} | all-to-all | bytes 524288 | tf_op jit(solution)/shard_map/all_to_all | solution.py:253
  38.8 0.8 %shard_map.77 = bf16[2,4,64,256]{3,2,1,0:T(8,128)(2,1)} custom-call(bf16[8,64,256]{2,1,0:T(8,128)(2,1)S(1)} %all_to_all.11.packed), custom_call_target="tpu_custom_call" | custom-call | tf_op jit(solution)/shard_map/pallas_call | solution.py:328
Async XLA Ops:
  19.3 4.1 %collective-permute-start = (bf16[10,16,768]{2,1,0:T(8,128)(2,1)S(1)}, bf16[10,16,768]{2,1,0:T(8,128)(2,1)S(1)}, u32[]{:S(2)}, u32[]{:S(2)}) collective-permute-start(bf16[10,16,768]{2,1,0:T(8,128)(2,1)S(1)} %shard_map.74), channel_id=1, source_target_pairs={{0,1},{1,0},{2,3},{3,2},{4,5},{5,4},{6,7},{7,6},{8,9},{9,8},{10,11... | collective-permute-start | bytes 737288 | tf_op jit(solution)/shard_map/ppermute | solution.py:298

commit v10 on v9

--- a/solution.py
+++ b/solution.py
@@ -138,13 +138,12 @@
     order = [1, 0, 2]
     taps = {b: pltpu.make_async_copy(conv_far.at[:, b], conv_weight.at[:, b], conv_sems.at[b]) for b in order}
     others = [pltpu.make_async_copy(far[i], near[i], sems.at[i - 1]) for i in range(1, 5)]
-    for copy in list(taps.values()) + others:
-        copy.start()
+    taps[order[0]].start()
     sources, step, chans = video.shape
     span = step // (count * rows)
     own = span - 2
     frames = sources * count
-    half = own // 4 if own % 4 == 0 else own
+    half = own // 2 if own % 2 == 0 else own
     fill(vid, 0, video[...].reshape(sources * step, chans).astype(f32))
     for w in range(span):
         for r in range(rows):
@@ -152,6 +151,11 @@
             grid[w, r] = shifted([activated(x) for x in now])
             if 1 <= w <= own:
                 total[w - 1, r] = jnp.concatenate(now, 0)
+        if w == span // 2:
+            taps[order[1]].start()
+    taps[order[2]].start()
+    for copy in others:
+        copy.start()
 
     ids_copy.wait()
     fill_bias(bias, ids, frames, count)
@@ -228,20 +232,22 @@
             for r in range(rows):
                 for t in range(count):
                     first = ((w * rows + r) * count + t + 1) * sources - group
-                    place = (start + w) * lines + t * rows + r
+                    place = (t * rows + r) * own + start + w
                     put(res, place, group, back, encoded[first : first + group])
     done = jnp.concatenate([res[i] for i in range(res.shape[0])], axis=1)
     out[...] = done.astype(bf16).reshape(out.shape)
 
 
-def unpack_kernel(packed, out, local, wide, sems):
+def unpack_kernel(packed, out, local, sems):
     count, rows, cols, chans = out.shape
     lines = count * rows
-    fill(wide, 0, packed[...].reshape(lines * cols, chans).astype(f32))
+    regions = packed.shape[0]
+    own = cols // regions
+    wide = packed[...].astype(f32).reshape(regions, lines, own, chans)
     copies = []
     for at in range(lines):
         place = (at // rows, at % rows)
-        local[place] = get(wide, at, cols, lines).astype(bf16)
+        local[place] = wide[:, at].reshape(cols, chans).astype(bf16)
         copy = pltpu.make_async_copy(local.at[place], out.at[place], sems.at[at])
         copy.start()
         copies.append(copy)
@@ -332,7 +338,6 @@
         out_specs=far,
         scratch_shapes=[
             pltpu.VMEM(video.shape, bf16),
-            scratch(lines * cols, chans),
             pltpu.SemaphoreType.DMA((lines,)),
         ],
         compiler_params=params,

time: 39.9 us -> 39.4 us (0.987)
  Pallas kernels: 9.18 us -> 8.67 us
    pallas_call x1, Pallas kernels: 4.02 us -> 3.51 us  [per_device(): pl.pallas_call(functools.partial(shift_kernel, count, rows), out_shape=[j...]
  transfers between devices with their start and end apart: 1 -> 1, of which waited for: 0 -> 0; matrix products, arithmetic and copies ran while one was open for 0% -> 0% of each run, Pallas kernels for 10% -> 9%
where the time goes in v10:
time: 39.4 us; the launch traced here: 39.1 us
  blocking collectives  30.3 us (77%)
  Pallas kernels  8.67 us (22%)
    all_to_all x2, blocking collectives, exchanged(): return lax.all_to_all(blocks, 'tm', split_axis=0, concat_axis=0, tiled=True)  30.3 us
    pallas_call x1, Pallas kernels, per_device(): pl.pallas_call(functools.partial(shift_kernel, count, rows), out_shape=[j...  3.51 us
    pallas_call x1, Pallas kernels, per_device(): pl.pallas_call(functools.partial(main_kernel, count, rows, group), out_sh...  3.03 us
    pallas_call x1, Pallas kernels, per_device(): pl.pallas_call(functools.partial(pack_kernel, group), out_shape=jax.Shape...  1.11 us
  transfers between devices with their start and end apart: 1, of which 0 were waited for; matrix products, arithmetic and copies ran while one was open for 0% of the time, Pallas kernels for 9%

profile of v10, /device:TPU:0, one launch (start us, length us, event | category | flops | bytes accessed | tf_op | source)
XLA Modules:
  0.0 39.1 jit_solution(28658356883020359)
XLA Ops:
  0.0 1.1 %shard_map.73 = bf16[8,80,256]{2,1,0:T(8,128)(2,1)S(1)} custom-call(bf16[2,4,64,256]{3,2,1,0:T(8,128)(2,1)} %video.1), custom_call_target="tpu_custom_call" | custom-call | tf_op jit(solution)/shard_map/pallas_call | solution.py:274
  1.1 18.0 %all_to_all.10.video = bf16[8,80,256]{2,1,0:T(8,128)(2,1)S(1)} all-to-all(bf16[8,80,256]{2,1,0:T(8,128)(2,1)S(1)} %shard_map.73), channel_id=1, replica_groups=mesh['groups'=2,'tm'=8,'height'=2] {'tm'}, dimensions={0} | all-to-all | bytes 655360 | tf_op jit(solution)/shard_map/all_to_all | solution.py:259
  19.1 0.3 shard_map.74
  19.3 0.1 collective-permute-start
  19.4 3.5 %shard_map.75 = (f32[8,4,16,256]{3,2,1,0:T(8,128)S(1)}, f32[128,128]{1,0:T(8,128)S(1)}, bf16[3,3,3,256,256]{4,3,2,1,0:T(8,128)(2,1)S(1)}, bf16[256,256]{1,0:T(8,...) custom-call(bf16[8,80,256]{2,1,0:T(8,128)(2,1)S(1)} %all_to_all.10.video, ...), custom_call_target="tpu_custom_call" | custom-call | tf_op jit(solution)/shard_map/pallas_call | solution.py:307
  22.9 0.0 collective-permute-done.edge
  22.9 3.0 %shard_map.76 = bf16[8,64,256]{2,1,0:T(8,128)(2,1)S(1)} custom-call(bf16[10,16,768]{2,1,0:T(8,128)(2,1)S(1)} %collective-permute-done.edge, f32[8,4,16,256]{3,2,1,0:T(8,128)S(1)} %get-tuple-element.12.given, f32[128,128]{1,0:T(8,128)S(1)} %get-tuple-element.13.bias, bf16[3,3,3,256,256]{4,3,2,1,0:T(8,128)(2,1)S(1)} %get-tuple-element.14.conv_weight, ...), custom_call_target="tpu_custom_call" | custom-call | tf_op jit(solution)/shard_map/pallas_call | solution.py:326
  26.0 12.4 %all_to_all.11.packed = bf16[8,64,256]{2,1,0:T(8,128)(2,1)S(1)} all-to-all(bf16[8,64,256]{2,1,0:T(8,128)(2,1)S(1)} %shard_map.76), channel_id=1, replica_groups=mesh['groups'=2,'tm'=8,'height'=2] {'tm'}, dimensions={0} | all-to-all | bytes 524288 | tf_op jit(solution)/shard_map/all_to_all | solution.py:259
  38.4 0.8 %shard_map.77 = bf16[2,4,64,256]{3,2,1,0:T(8,128)(2,1)} custom-call(bf16[8,64,256]{2,1,0:T(8,128)(2,1)S(1)} %all_to_all.11.packed), custom_call_target="tpu_custom_call" | custom-call | tf_op jit(solution)/shard_map/pallas_call | solution.py:334
Async XLA Ops:
  19.3 3.6 %collective-permute-start = (bf16[10,16,768]{2,1,0:T(8,128)(2,1)S(1)}, bf16[10,16,768]{2,1,0:T(8,128)(2,1)S(1)}, u32[]{:S(2)}, u32[]{:S(2)}) collective-permute-start(bf16[10,16,768]{2,1,0:T(8,128)(2,1)S(1)} %shard_map.74), channel_id=1, source_target_pairs={{0,1},{1,0},{2,3},{3,2},{4,5},{5,4},{6,7},{7,6},{8,9},{9,8},{10,11... | collective-permute-start | bytes 737288 | tf_op jit(solution)/shard_map/ppermute | solution.py:304

commit v11 on v10

--- a/solution.py
+++ b/solution.py
@@ -94,8 +94,8 @@
 
 
 def activated(wide):
-    normal = rms(wide)
-    return normal / (1.0 + jnp.exp(-normal))
+    part = 0.5 * rms(wide)
+    return part + part * jnp.tanh(part)
 
 
 def depth(parts):
@@ -143,7 +143,7 @@
     span = step // (count * rows)
     own = span - 2
     frames = sources * count
-    half = own // 2 if own % 2 == 0 else own
+    of_taps = [(e, a) for e in range(TAPS) for a in range(TAPS)]
     fill(vid, 0, video[...].reshape(sources * step, chans).astype(f32))
     for w in range(span):
         for r in range(rows):
@@ -162,13 +162,17 @@
     for b in order:
         taps[b].wait()
         low, high = max(0, 1 - b), min(rows, rows + 1 - b)
-        weight = jnp.concatenate([conv_weight[a, b, e] for e in range(TAPS) for a in range(TAPS)], axis=0)
-        for w in range(0, own, half):
-            window = depth([grid[w + e : w + e + half, low + b - 1 : high + b - 1] for e in range(TAPS)])
-            window = window.reshape(half * (high - low) * frames, TAPS * TAPS * chans)
-            part = jnp.dot(window, weight, preferred_element_type=f32)
-            some = total.at[w : w + half, low:high]
-            some[...] = some[...] + part.reshape(half, high - low, frames, chans)
+        size = own * (high - low) * frames
+        some = total.at[:, low:high]
+        result = some[...]
+        for chain in (of_taps[: len(of_taps) // 2], of_taps[len(of_taps) // 2 :]):
+            window = [
+                grid[e : e + own, low + b - 1 : high + b - 1, :, a * chans : (a + 1) * chans] for e, a in chain
+            ]
+            weight = jnp.concatenate([conv_weight[a, b, e] for e, a in chain], axis=0)
+            part = jnp.dot(depth(window).reshape(size, len(chain) * chans), weight, preferred_element_type=f32)
+            result = result + part.reshape(some.shape)
+        some[...] = result
     for copy in others:
         copy.wait()
 
@@ -198,36 +202,37 @@
     single = [jnp.where(head_of == h, 1.0, 0.0).astype(bf16) for h in range(heads)]
     scaled = [mask * jnp.asarray(HD ** (-0.5), bf16) for mask in single]
 
+    lines_of = []
+    for r in range(rows):
+        row = given[:, r] + jnp.where(r == (rows - 1) * (1 - lower), part, 0.0)
+        lines_of.append(row[:, None])
+    hidden = jnp.concatenate(lines_of, axis=1).reshape(own * rows * frames, chans).astype(bf16).astype(f32)
+    normed = rms(hidden).astype(bf16)
+    query, keys, values = (
+        jnp.dot(normed, weight[...], preferred_element_type=f32).astype(bf16) for weight in (w_query, w_key, w_value)
+    )
     half = own // 2 if own % (2 * several) == 0 else own
     for start in range(0, own, half):
-        lines_of = []
-        for r in range(rows):
-            row = given[start : start + half, r]
-            row = row + jnp.where(r == (rows - 1) * (1 - lower), part[start : start + half], 0.0)
-            lines_of.append(row[:, None])
-        hidden = jnp.concatenate(lines_of, axis=1).reshape(half * rows * frames, chans).astype(bf16).astype(f32)
-        normed = rms(hidden).astype(bf16)
-        query, keys, values = (
-            jnp.dot(normed, weight[...], preferred_element_type=f32).astype(bf16)
-            for weight in (w_query, w_key, w_value)
-        )
         gone = []
-        for at in range(0, half * rows * frames, area):
+        for at in range(start * rows * frames, (start + half) * rows * frames, area):
             group_of = slice(at, at + area)
             queries = jnp.concatenate([query[group_of] * mask for mask in scaled], axis=0)
             scores = lax.dot_general(
                 queries, keys[group_of], (((1,), (1,)), ((), ())), preferred_element_type=f32
             )
-            weights = []
+            weights, under = [], jnp.zeros((area, chans), f32)
             for h in range(heads):
                 score = scores[h * area : (h + 1) * area] + bias[...]
                 expo = jnp.exp(score - jnp.max(score, axis=-1, keepdims=True))
-                weights.append((expo * (1.0 / jnp.sum(expo, axis=-1, keepdims=True))).astype(bf16))
+                under = jnp.where(head_of == h, jnp.sum(expo, axis=-1, keepdims=True), under)
+                weights.append(expo.astype(bf16))
             heads_values = jnp.concatenate([values[group_of] * mask for mask in single], axis=0)
             attended = jnp.dot(jnp.concatenate(weights, axis=1), heads_values, preferred_element_type=f32)
-            gone.append(attended.astype(bf16))
+            gone.append((attended / under).astype(bf16))
         attended = jnp.concatenate(gone, axis=0)
-        encoded = hidden + jnp.dot(attended, w_output[...], preferred_element_type=f32)
+        encoded = hidden[start * rows * frames : (start + half) * rows * frames] + jnp.dot(
+            attended, w_output[...], preferred_element_type=f32
+        )
         for w in range(half):
             for r in range(rows):
                 for t in range(count):

time: 39.4 us -> 40.1 us (1.018)
  Pallas kernels: 8.67 us -> 9.39 us
    pallas_call x1, Pallas kernels: 3.51 us -> 4.83 us  [per_device(): pl.pallas_call(functools.partial(shift_kernel, count, rows), out_shape=[j...]
    pallas_call x1, Pallas kernels: 3.03 us -> 2.44 us  [per_device(): pl.pallas_call(functools.partial(main_kernel, count, rows, group), out_sh...]
  transfers between devices with their start and end apart: 1 -> 1, of which waited for: 0 -> 0; matrix products, arithmetic and copies ran while one was open for 0% -> 0% of each run, Pallas kernels for 9% -> 12%
where the time goes in v11:
time: 40.1 us; the launch traced here: 39.8 us
  blocking collectives  30.3 us (76%)
  Pallas kernels  9.39 us (23%)
    all_to_all x2, blocking collectives, exchanged(): return lax.all_to_all(blocks, 'tm', split_axis=0, concat_axis=0, tiled=True)  30.3 us
    pallas_call x1, Pallas kernels, per_device(): pl.pallas_call(functools.partial(shift_kernel, count, rows), out_shape=[j...  4.83 us
    pallas_call x1, Pallas kernels, per_device(): pl.pallas_call(functools.partial(main_kernel, count, rows, group), out_sh...  2.44 us
    pallas_call x1, Pallas kernels, per_device(): pl.pallas_call(functools.partial(pack_kernel, group), out_shape=jax.Shape...  1.11 us
  transfers between devices with their start and end apart: 1, of which 0 were waited for; matrix products, arithmetic and copies ran while one was open for 0% of the time, Pallas kernels for 12%

profile of v11, /device:TPU:0, one launch (start us, length us, event | category | flops | bytes accessed | tf_op | source)
XLA Modules:
  0.0 39.8 jit_solution(12143569243815953051)
XLA Ops:
  0.0 1.1 %shard_map.73 = bf16[8,80,256]{2,1,0:T(8,128)(2,1)S(1)} custom-call(bf16[2,4,64,256]{3,2,1,0:T(8,128)(2,1)} %video.1), custom_call_target="tpu_custom_call" | custom-call | tf_op jit(solution)/shard_map/pallas_call | solution.py:279
  1.1 18.0 %all_to_all.10.video = bf16[8,80,256]{2,1,0:T(8,128)(2,1)S(1)} all-to-all(bf16[8,80,256]{2,1,0:T(8,128)(2,1)S(1)} %shard_map.73), channel_id=1, replica_groups=mesh['groups'=2,'tm'=8,'height'=2] {'tm'}, dimensions={0} | all-to-all | bytes 655360 | tf_op jit(solution)/shard_map/all_to_all | solution.py:264
  19.1 0.3 shard_map.74
  19.3 0.1 collective-permute-start
  19.4 4.8 %shard_map.75 = (f32[8,4,16,256]{3,2,1,0:T(8,128)S(1)}, f32[128,128]{1,0:T(8,128)S(1)}, bf16[3,3,3,256,256]{4,3,2,1,0:T(8,128)(2,1)S(1)}, bf16[256,256]{1,0:T(8,...) custom-call(bf16[8,80,256]{2,1,0:T(8,128)(2,1)S(1)} %all_to_all.10.video, ...), custom_call_target="tpu_custom_call" | custom-call | tf_op jit(solution)/shard_map/pallas_call | solution.py:312
  24.2 0.0 collective-permute-done.edge
  24.3 2.4 %shard_map.76 = bf16[8,64,256]{2,1,0:T(8,128)(2,1)S(1)} custom-call(bf16[10,16,768]{2,1,0:T(8,128)(2,1)S(1)} %collective-permute-done.edge, f32[8,4,16,256]{3,2,1,0:T(8,128)S(1)} %get-tuple-element.12.given, f32[128,128]{1,0:T(8,128)S(1)} %get-tuple-element.13.bias, bf16[3,3,3,256,256]{4,3,2,1,0:T(8,128)(2,1)S(1)} %get-tuple-element.14.conv_weight, ...), custom_call_target="tpu_custom_call" | custom-call | tf_op jit(solution)/shard_map/pallas_call | solution.py:331
  26.7 12.4 %all_to_all.11.packed = bf16[8,64,256]{2,1,0:T(8,128)(2,1)S(1)} all-to-all(bf16[8,64,256]{2,1,0:T(8,128)(2,1)S(1)} %shard_map.76), channel_id=1, replica_groups=mesh['groups'=2,'tm'=8,'height'=2] {'tm'}, dimensions={0} | all-to-all | bytes 524288 | tf_op jit(solution)/shard_map/all_to_all | solution.py:264
  39.1 0.8 %shard_map.77 = bf16[2,4,64,256]{3,2,1,0:T(8,128)(2,1)} custom-call(bf16[8,64,256]{2,1,0:T(8,128)(2,1)S(1)} %all_to_all.11.packed), custom_call_target="tpu_custom_call" | custom-call | tf_op jit(solution)/shard_map/pallas_call | solution.py:339
Async XLA Ops:
  19.3 4.9 %collective-permute-start = (bf16[10,16,768]{2,1,0:T(8,128)(2,1)S(1)}, bf16[10,16,768]{2,1,0:T(8,128)(2,1)S(1)}, u32[]{:S(2)}, u32[]{:S(2)}) collective-permute-start(bf16[10,16,768]{2,1,0:T(8,128)(2,1)S(1)} %shard_map.74), channel_id=1, source_target_pairs={{0,1},{1,0},{2,3},{3,2},{4,5},{5,4},{6,7},{7,6},{8,9},{9,8},{10,11... | collective-permute-start | bytes 737288 | tf_op jit(solution)/shard_map/ppermute | solution.py:309

commit v12 on v11

--- a/solution.py
+++ b/solution.py
@@ -143,7 +143,7 @@
     span = step // (count * rows)
     own = span - 2
     frames = sources * count
-    of_taps = [(e, a) for e in range(TAPS) for a in range(TAPS)]
+    half = own // 2 if own % 2 == 0 else own
     fill(vid, 0, video[...].reshape(sources * step, chans).astype(f32))
     for w in range(span):
         for r in range(rows):
@@ -162,17 +162,13 @@
     for b in order:
         taps[b].wait()
         low, high = max(0, 1 - b), min(rows, rows + 1 - b)
-        size = own * (high - low) * frames
-        some = total.at[:, low:high]
-        result = some[...]
-        for chain in (of_taps[: len(of_taps) // 2], of_taps[len(of_taps) // 2 :]):
-            window = [
-                grid[e : e + own, low + b - 1 : high + b - 1, :, a * chans : (a + 1) * chans] for e, a in chain
-            ]
-            weight = jnp.concatenate([conv_weight[a, b, e] for e, a in chain], axis=0)
-            part = jnp.dot(depth(window).reshape(size, len(chain) * chans), weight, preferred_element_type=f32)
-            result = result + part.reshape(some.shape)
-        some[...] = result
+        weight = jnp.concatenate([conv_weight[a, b, e] for e in range(TAPS) for a in range(TAPS)], axis=0)
+        for w in range(0, own, half):
+            window = depth([grid[w + e : w + e + half, low + b - 1 : high + b - 1] for e in range(TAPS)])
+            window = window.reshape(half * (high - low) * frames, TAPS * TAPS * chans)
+            part = jnp.dot(window, weight, preferred_element_type=f32)
+            some = total.at[w : w + half, low:high]
+            some[...] = some[...] + part.reshape(half, high - low, frames, chans)
     for copy in others:
         copy.wait()
 

time: 40.1 us -> 38.8 us (0.968)
  Pallas kernels: 9.39 us -> 8.11 us
    pallas_call x1, Pallas kernels: 4.83 us -> 3.55 us  [per_device(): pl.pallas_call(functools.partial(shift_kernel, count, rows), out_shape=[j...]
  transfers between devices with their start and end apart: 1 -> 1, of which waited for: 0 -> 0; matrix products, arithmetic and copies ran while one was open for 0% -> 0% of each run, Pallas kernels for 12% -> 9%
where the time goes in v12:
time: 38.8 us; the launch traced here: 38.6 us
  blocking collectives  30.3 us (78%)
  Pallas kernels  8.11 us (21%)
    all_to_all x2, blocking collectives, exchanged(): return lax.all_to_all(blocks, 'tm', split_axis=0, concat_axis=0, tiled=True)  30.3 us
    pallas_call x1, Pallas kernels, per_device(): pl.pallas_call(functools.partial(shift_kernel, count, rows), out_shape=[j...  3.55 us
    pallas_call x1, Pallas kernels, per_device(): pl.pallas_call(functools.partial(main_kernel, count, rows, group), out_sh...  2.44 us
    pallas_call x1, Pallas kernels, per_device(): pl.pallas_call(functools.partial(pack_kernel, group), out_shape=jax.Shape...  1.11 us
  transfers between devices with their start and end apart: 1, of which 0 were waited for; matrix products, arithmetic and copies ran while one was open for 0% of the time, Pallas kernels for 9%

profile of v12, /device:TPU:0, one launch (start us, length us, event | category | flops | bytes accessed | tf_op | source)
XLA Modules:
  0.0 38.6 jit_solution(11381709130953676734)
XLA Ops:
  0.0 1.1 %shard_map.73 = bf16[8,80,256]{2,1,0:T(8,128)(2,1)S(1)} custom-call(bf16[2,4,64,256]{3,2,1,0:T(8,128)(2,1)} %video.1), custom_call_target="tpu_custom_call" | custom-call | tf_op jit(solution)/shard_map/pallas_call | solution.py:275
  1.1 18.0 %all_to_all.10.video = bf16[8,80,256]{2,1,0:T(8,128)(2,1)S(1)} all-to-all(bf16[8,80,256]{2,1,0:T(8,128)(2,1)S(1)} %shard_map.73), channel_id=1, replica_groups=mesh['groups'=2,'tm'=8,'height'=2] {'tm'}, dimensions={0} | all-to-all | bytes 655360 | tf_op jit(solution)/shard_map/all_to_all | solution.py:260
  19.1 0.3 shard_map.74
  19.3 0.1 collective-permute-start
  19.4 3.6 %shard_map.75 = (f32[8,4,16,256]{3,2,1,0:T(8,128)S(1)}, f32[128,128]{1,0:T(8,128)S(1)}, bf16[3,3,3,256,256]{4,3,2,1,0:T(8,128)(2,1)S(1)}, bf16[256,256]{1,0:T(8,...) custom-call(bf16[8,80,256]{2,1,0:T(8,128)(2,1)S(1)} %all_to_all.10.video, ...), custom_call_target="tpu_custom_call" | custom-call | tf_op jit(solution)/shard_map/pallas_call | solution.py:308
  23.0 0.0 collective-permute-done.edge
  23.0 2.4 %shard_map.76 = bf16[8,64,256]{2,1,0:T(8,128)(2,1)S(1)} custom-call(bf16[10,16,768]{2,1,0:T(8,128)(2,1)S(1)} %collective-permute-done.edge, f32[8,4,16,256]{3,2,1,0:T(8,128)S(1)} %get-tuple-element.12.given, f32[128,128]{1,0:T(8,128)S(1)} %get-tuple-element.13.bias, bf16[3,3,3,256,256]{4,3,2,1,0:T(8,128)(2,1)S(1)} %get-tuple-element.14.conv_weight, ...), custom_call_target="tpu_custom_call" | custom-call | tf_op jit(solution)/shard_map/pallas_call | solution.py:327
  25.4 12.4 %all_to_all.11.packed = bf16[8,64,256]{2,1,0:T(8,128)(2,1)S(1)} all-to-all(bf16[8,64,256]{2,1,0:T(8,128)(2,1)S(1)} %shard_map.76), channel_id=1, replica_groups=mesh['groups'=2,'tm'=8,'height'=2] {'tm'}, dimensions={0} | all-to-all | bytes 524288 | tf_op jit(solution)/shard_map/all_to_all | solution.py:260
  37.8 0.8 %shard_map.77 = bf16[2,4,64,256]{3,2,1,0:T(8,128)(2,1)} custom-call(bf16[8,64,256]{2,1,0:T(8,128)(2,1)S(1)} %all_to_all.11.packed), custom_call_target="tpu_custom_call" | custom-call | tf_op jit(solution)/shard_map/pallas_call | solution.py:335
Async XLA Ops:
  19.3 3.6 %collective-permute-start = (bf16[10,16,768]{2,1,0:T(8,128)(2,1)S(1)}, bf16[10,16,768]{2,1,0:T(8,128)(2,1)S(1)}, u32[]{:S(2)}, u32[]{:S(2)}) collective-permute-start(bf16[10,16,768]{2,1,0:T(8,128)(2,1)S(1)} %shard_map.74), channel_id=1, source_target_pairs={{0,1},{1,0},{2,3},{3,2},{4,5},{5,4},{6,7},{7,6},{8,9},{9,8},{10,11... | collective-permute-start | bytes 737288 | tf_op jit(solution)/shard_map/ppermute | solution.py:305

commit v13 on v12

--- a/solution.py
+++ b/solution.py
@@ -131,14 +131,13 @@
 
 
 def shift_kernel(count, rows, video, ids_far, *refs):
-    far, (total, bias, *near), (vid, grid, ids, conv_sems, sems, ids_sem) = refs[:5], refs[5:12], refs[12:]
+    conv_weight, far, (total, bias, *near) = refs[0], refs[1:5], refs[5:11]
+    vid, grid, ids, sems, ids_sem = refs[11:]
     ids_copy = pltpu.make_async_copy(ids_far, ids, ids_sem)
     ids_copy.start()
-    conv_far, conv_weight = far[0], near[0]
-    order = [1, 0, 2]
-    taps = {b: pltpu.make_async_copy(conv_far.at[:, b], conv_weight.at[:, b], conv_sems.at[b]) for b in order}
-    others = [pltpu.make_async_copy(far[i], near[i], sems.at[i - 1]) for i in range(1, 5)]
-    taps[order[0]].start()
+    others = [pltpu.make_async_copy(src, dst, sems.at[i]) for i, (src, dst) in enumerate(zip(far, near))]
+    for copy in others:
+        copy.start()
     sources, step, chans = video.shape
     span = step // (count * rows)
     own = span - 2
@@ -151,16 +150,8 @@
             grid[w, r] = shifted([activated(x) for x in now])
             if 1 <= w <= own:
                 total[w - 1, r] = jnp.concatenate(now, 0)
-        if w == span // 2:
-            taps[order[1]].start()
-    taps[order[2]].start()
-    for copy in others:
-        copy.start()
-
-    ids_copy.wait()
-    fill_bias(bias, ids, frames, count)
-    for b in order:
-        taps[b].wait()
+
+    for b in range(TAPS):
         low, high = max(0, 1 - b), min(rows, rows + 1 - b)
         weight = jnp.concatenate([conv_weight[a, b, e] for e in range(TAPS) for a in range(TAPS)], axis=0)
         for w in range(0, own, half):
@@ -169,6 +160,8 @@
             part = jnp.dot(window, weight, preferred_element_type=f32)
             some = total.at[w : w + half, low:high]
             some[...] = some[...] + part.reshape(half, high - low, frames, chans)
+    ids_copy.wait()
+    fill_bias(bias, ids, frames, count)
     for copy in others:
         copy.wait()
 
@@ -270,7 +263,8 @@
     far = pl.BlockSpec(memory_space=pltpu.HBM)
     params = pltpu.CompilerParams(vmem_limit_bytes=VMEM)
     in_far = functools.partial(pltpu.with_memory_space_constraint, memory_space=pltpu.HBM)
-    weights = [in_far(x) for x in (conv_weight, w_query, w_key, w_value, w_output)]
+    weights = [in_far(x) for x in (w_query, w_key, w_value, w_output)]
+    conv_weight = lax.ppermute(conv_weight, "height", [(0, 1), (1, 0)])
 
     blocks = pl.pallas_call(
         functools.partial(pack_kernel, group),
@@ -312,18 +306,17 @@
             jax.ShapeDtypeStruct((area, area), f32),
         ]
         + [jax.ShapeDtypeStruct(x.shape, bf16) for x in weights],
-        in_specs=[near] + [far] * 6,
-        out_specs=[near] * 7,
+        in_specs=[near, far, near] + [far] * 4,
+        out_specs=[near] * 6,
         scratch_shapes=[
             stored,
             pltpu.VMEM((span, rows, frames, TAPS * chans), bf16),
             pltpu.SMEM((frames,), jnp.int32),
-            pltpu.SemaphoreType.DMA((TAPS,)),
             pltpu.SemaphoreType.DMA((4,)),
             pltpu.SemaphoreType.DMA(()),
         ],
         compiler_params=params,
-    )(piece, in_far(ids), *weights)
+    )(piece, in_far(ids), conv_weight, *weights)
     blocks = pl.pallas_call(
         functools.partial(main_kernel, count, rows, group),
         out_shape=jax.ShapeDtypeStruct((group, own * lines, chans), bf16),
@@ -331,7 +324,7 @@
         out_specs=near,
         scratch_shapes=[scratch(group * own * lines, chans)],
         compiler_params=params,
-    )(edge, total, bias, *weights)
+    )(edge, total, bias, conv_weight, *weights)
     return pl.pallas_call(
         unpack_kernel,
         out_shape=jax.ShapeDtypeStruct(video.shape, bf16),

time: 38.8 us -> 38 us (0.979)
  Pallas kernels: 8.11 us -> 6.66 us
  starting transfers between devices: 0.07 us -> 0.52 us
    pallas_call x1, Pallas kernels: 3.55 us -> 2.1 us  [per_device(): pl.pallas_call(functools.partial(shift_kernel, count, rows), out_shape=[j...]
    ppermute x0 -> x1, starting transfers between devices: none -> 0.45 us  [per_device(): conv_weight = lax.ppermute(conv_weight, 'height', [(0, 1), (1, 0)])]
  transfers between devices with their start and end apart: 1 -> 2, of which waited for: 0 -> 0; matrix products, arithmetic and copies ran while one was open for 0% -> 0% of each run, Pallas kernels for 9% -> 9%
where the time goes in v13:
time: 38 us; the launch traced here: 37.8 us
  blocking collectives  30.5 us (80%)
  Pallas kernels  6.66 us (18%)
  starting transfers between devices  0.52 us (1%)
    all_to_all x2, blocking collectives, exchanged(): return lax.all_to_all(blocks, 'tm', split_axis=0, concat_axis=0, tiled=True)  30.5 us
    pallas_call x1, Pallas kernels, per_device(): pl.pallas_call(functools.partial(main_kernel, count, rows, group), out_sh...  2.44 us
    pallas_call x1, Pallas kernels, per_device(): pl.pallas_call(functools.partial(shift_kernel, count, rows), out_shape=[j...  2.1 us
    pallas_call x1, Pallas kernels, per_device(): pl.pallas_call(functools.partial(pack_kernel, group), out_shape=jax.Shape...  1.11 us
    pallas_call x1, Pallas kernels, per_device(): pl.pallas_call(unpack_kernel, out_shape=jax.ShapeDtypeStruct(video.shape,...  0.76 us
  transfers between devices with their start and end apart: 2, of which 0 were waited for; matrix products, arithmetic and copies ran while one was open for 0% of the time, Pallas kernels for 9%

profile of v13, /device:TPU:0, one launch (start us, length us, event | category | flops | bytes accessed | tf_op | source)
XLA Modules:
  0.0 37.8 jit_solution(9593987341141996510)
XLA Ops:
  0.0 0.5 %collective-permute-start.1 = (bf16[3,3,3,256,256]{4,3,2,1,0:T(8,128)(2,1)}, bf16[3,3,3,256,256]{4,3,2,1,0:T(8,128)(2,1)S(1)}, u32[]{:S(2)}, u32[]{:S(2)}) collective-permute-start(bf16[3,3,3,256,256]{4,3,2,1,0:T(8,128)(2,1)} %param.9), channel_id=1, source_target_pairs={{0,1},{1,0},{2,3},{3,2},{4,5},{5,4},{6,7},{7,6},{8,9},{9,8},{10,11... | collective-permute-start | bytes 10616840 | tf_op jit(solution)/shard_map/ppermute | solution.py:267
  0.5 1.1 %shard_map.73 = bf16[8,80,256]{2,1,0:T(8,128)(2,1)S(1)} custom-call(bf16[2,4,64,256]{3,2,1,0:T(8,128)(2,1)} %video.1), custom_call_target="tpu_custom_call" | custom-call | tf_op jit(solution)/shard_map/pallas_call | solution.py:269
  1.6 18.2 %all_to_all.10.video = bf16[8,80,256]{2,1,0:T(8,128)(2,1)S(1)} all-to-all(bf16[8,80,256]{2,1,0:T(8,128)(2,1)S(1)} %shard_map.73), channel_id=1, replica_groups=mesh['groups'=2,'tm'=8,'height'=2] {'tm'}, dimensions={0} | all-to-all | bytes 655360 | tf_op jit(solution)/shard_map/all_to_all | solution.py:253
  19.8 0.3 shard_map.74
  20.0 0.1 collective-permute-start
  20.1 0.0 collective-permute-done.1.refs_0_.conv_weight
  20.1 2.1 %shard_map.75 = (f32[8,4,16,256]{3,2,1,0:T(8,128)S(1)}, f32[128,128]{1,0:T(8,128)S(1)}, bf16[256,256]{1,0:T(8,128)(2,1)S(1)}, bf16[256,256]{1,0:T(8,128)(2,1)S(1...) custom-call(bf16[8,80,256]{2,1,0:T(8,128)(2,1)S(1)} %all_to_all.10.video, s32[16]{0:T(128)} %ids_far.1, ...), custom_call_target="tpu_custom_call" | custom-call | tf_op jit(solution)/shard_map/pallas_call | solution.py:302
  22.2 0.0 collective-permute-done.edge
  22.2 2.4 %shard_map.76 = bf16[8,64,256]{2,1,0:T(8,128)(2,1)S(1)} custom-call(bf16[10,16,768]{2,1,0:T(8,128)(2,1)S(1)} %collective-permute-done.edge, f32[8,4,16,256]{3,2,1,0:T(8,128)S(1)} %get-tuple-element.11.given, f32[128,128]{1,0:T(8,128)S(1)} %get-tuple-element.12.bias, bf16[3,3,3,256,256]{4,3,2,1,0:T(8,128)(2,1)S(1)} %collective-permute-done.1.refs_0_.conv_weight, ...), custom_call_target="tpu_custom_call" | custom-call | tf_op jit(solution)/shard_map/pallas_call | solution.py:320
  24.7 12.4 %all_to_all.11.packed = bf16[8,64,256]{2,1,0:T(8,128)(2,1)S(1)} all-to-all(bf16[8,64,256]{2,1,0:T(8,128)(2,1)S(1)} %shard_map.76), channel_id=1, replica_groups=mesh['groups'=2,'tm'=8,'height'=2] {'tm'}, dimensions={0} | all-to-all | bytes 524288 | tf_op jit(solution)/shard_map/all_to_all | solution.py:253
  37.0 0.8 %shard_map.77 = bf16[2,4,64,256]{3,2,1,0:T(8,128)(2,1)} custom-call(bf16[8,64,256]{2,1,0:T(8,128)(2,1)S(1)} %all_to_all.11.packed), custom_call_target="tpu_custom_call" | custom-call | tf_op jit(solution)/shard_map/pallas_call | solution.py:328
Async XLA Ops:
  0.0 20.1 %collective-permute-start.1 = (bf16[3,3,3,256,256]{4,3,2,1,0:T(8,128)(2,1)}, bf16[3,3,3,256,256]{4,3,2,1,0:T(8,128)(2,1)S(1)}, u32[]{:S(2)}, u32[]{:S(2)}) collective-permute-start(bf16[3,3,3,256,256]{4,3,2,1,0:T(8,128)(2,1)} %param.9), channel_id=1, source_target_pairs={{0,1},{1,0},{2,3},{3,2},{4,5},{5,4},{6,7},{7,6},{8,9},{9,8},{10,11... | collective-permute-start | bytes 10616840 | tf_op jit(solution)/shard_map/ppermute | solution.py:267
  20.0 2.2 %collective-permute-start = (bf16[10,16,768]{2,1,0:T(8,128)(2,1)S(1)}, bf16[10,16,768]{2,1,0:T(8,128)(2,1)S(1)}, u32[]{:S(2)}, u32[]{:S(2)}) collective-permute-start(bf16[10,16,768]{2,1,0:T(8,128)(2,1)S(1)} %shard_map.74), channel_id=1, source_target_pairs={{0,1},{1,0},{2,3},{3,2},{4,5},{5,4},{6,7},{7,6},{8,9},{9,8},{10,11... | collective-permute-start | bytes 737288 | tf_op jit(solution)/shard_map/ppermute | solution.py:299

commit v14 on v13

--- a/solution.py
+++ b/solution.py
@@ -264,7 +264,7 @@
     params = pltpu.CompilerParams(vmem_limit_bytes=VMEM)
     in_far = functools.partial(pltpu.with_memory_space_constraint, memory_space=pltpu.HBM)
     weights = [in_far(x) for x in (w_query, w_key, w_value, w_output)]
-    conv_weight = lax.ppermute(conv_weight, "height", [(0, 1), (1, 0)])
+    conv_weight = lax.ppermute(conv_weight, "height", [(i, i) for i in range(lax.axis_size("height"))])
 
     blocks = pl.pallas_call(
         functools.partial(pack_kernel, group),

time: 38 us -> 39.4 us (1.037)
  starting transfers between devices: 0.52 us -> 2.07 us
    ppermute x1, starting transfers between devices: 0.45 us -> 2 us  [per_device(): lax.ppermute(conv_weight, 'height', [(i, i) for i in range(lax.axis_size(...]
where the time goes in v14:
time: 39.4 us; the launch traced here: 39.1 us
  blocking collectives  30.3 us (77%)
  Pallas kernels  6.66 us (17%)
  starting transfers between devices  2.07 us (5%)
    all_to_all x2, blocking collectives, exchanged(): return lax.all_to_all(blocks, 'tm', split_axis=0, concat_axis=0, tiled=True)  30.3 us
    pallas_call x1, Pallas kernels, per_device(): pl.pallas_call(functools.partial(main_kernel, count, rows, group), out_sh...  2.44 us
    pallas_call x1, Pallas kernels, per_device(): pl.pallas_call(functools.partial(shift_kernel, count, rows), out_shape=[j...  2.1 us
    ppermute x1, starting transfers between devices, per_device(): lax.ppermute(conv_weight, 'height', [(i, i) for i in range(lax.axis_size(...  2 us
    pallas_call x1, Pallas kernels, per_device(): pl.pallas_call(functools.partial(pack_kernel, group), out_shape=jax.Shape...  1.11 us
  transfers between devices with their start and end apart: 2, of which 0 were waited for; matrix products, arithmetic and copies ran while one was open for 0% of the time, Pallas kernels for 9%

profile of v14, /device:TPU:0, one launch (start us, length us, event | category | flops | bytes accessed | tf_op | source)
XLA Modules:
  0.0 39.1 jit_solution(15774656163949546847)
XLA Ops:
  0.0 2.0 %collective-permute-start.1 = (bf16[3,3,3,256,256]{4,3,2,1,0:T(8,128)(2,1)}, bf16[3,3,3,256,256]{4,3,2,1,0:T(8,128)(2,1)S(1)}, u32[]{:S(2)}, u32[]{:S(2)}) collective-permute-start(bf16[3,3,3,256,256]{4,3,2,1,0:T(8,128)(2,1)} %param.9), channel_id=1, source_target_pairs={{0,0},{1,1},{2,2},{3,3},{4,4},{5,5},{6,6},{7,7},{8,8},{9,9},{10,10... | collective-permute-start | bytes 10616840 | tf_op jit(solution)/shard_map/ppermute | solution.py:267
  2.0 1.1 %shard_map.73 = bf16[8,80,256]{2,1,0:T(8,128)(2,1)S(1)} custom-call(bf16[2,4,64,256]{3,2,1,0:T(8,128)(2,1)} %video.1), custom_call_target="tpu_custom_call" | custom-call | tf_op jit(solution)/shard_map/pallas_call | solution.py:269
  3.1 18.0 %all_to_all.10.video = bf16[8,80,256]{2,1,0:T(8,128)(2,1)S(1)} all-to-all(bf16[8,80,256]{2,1,0:T(8,128)(2,1)S(1)} %shard_map.73), channel_id=1, replica_groups=mesh['groups'=2,'tm'=8,'height'=2] {'tm'}, dimensions={0} | all-to-all | bytes 655360 | tf_op jit(solution)/shard_map/all_to_all | solution.py:253
  21.1 0.3 shard_map.74
  21.3 0.1 collective-permute-start
  21.4 0.0 collective-permute-done.1.refs_0_.conv_weight
  21.4 2.1 %shard_map.75 = (f32[8,4,16,256]{3,2,1,0:T(8,128)S(1)}, f32[128,128]{1,0:T(8,128)S(1)}, bf16[256,256]{1,0:T(8,128)(2,1)S(1)}, bf16[256,256]{1,0:T(8,128)(2,1)S(1...) custom-call(bf16[8,80,256]{2,1,0:T(8,128)(2,1)S(1)} %all_to_all.10.video, s32[16]{0:T(128)} %ids_far.1, ...), custom_call_target="tpu_custom_call" | custom-call | tf_op jit(solution)/shard_map/pallas_call | solution.py:302
  23.5 0.0 collective-permute-done.edge
  23.5 2.4 %shard_map.76 = bf16[8,64,256]{2,1,0:T(8,128)(2,1)S(1)} custom-call(bf16[10,16,768]{2,1,0:T(8,128)(2,1)S(1)} %collective-permute-done.edge, f32[8,4,16,256]{3,2,1,0:T(8,128)S(1)} %get-tuple-element.11.given, f32[128,128]{1,0:T(8,128)S(1)} %get-tuple-element.12.bias, bf16[3,3,3,256,256]{4,3,2,1,0:T(8,128)(2,1)S(1)} %collective-permute-done.1.refs_0_.conv_weight, ...), custom_call_target="tpu_custom_call" | custom-call | tf_op jit(solution)/shard_map/pallas_call | solution.py:320
  26.0 12.4 %all_to_all.11.packed = bf16[8,64,256]{2,1,0:T(8,128)(2,1)S(1)} all-to-all(bf16[8,64,256]{2,1,0:T(8,128)(2,1)S(1)} %shard_map.76), channel_id=1, replica_groups=mesh['groups'=2,'tm'=8,'height'=2] {'tm'}, dimensions={0} | all-to-all | bytes 524288 | tf_op jit(solution)/shard_map/all_to_all | solution.py:253
  38.4 0.8 %shard_map.77 = bf16[2,4,64,256]{3,2,1,0:T(8,128)(2,1)} custom-call(bf16[8,64,256]{2,1,0:T(8,128)(2,1)S(1)} %all_to_all.11.packed), custom_call_target="tpu_custom_call" | custom-call | tf_op jit(solution)/shard_map/pallas_call | solution.py:328
Async XLA Ops:
  0.0 21.4 %collective-permute-start.1 = (bf16[3,3,3,256,256]{4,3,2,1,0:T(8,128)(2,1)}, bf16[3,3,3,256,256]{4,3,2,1,0:T(8,128)(2,1)S(1)}, u32[]{:S(2)}, u32[]{:S(2)}) collective-permute-start(bf16[3,3,3,256,256]{4,3,2,1,0:T(8,128)(2,1)} %param.9), channel_id=1, source_target_pairs={{0,0},{1,1},{2,2},{3,3},{4,4},{5,5},{6,6},{7,7},{8,8},{9,9},{10,10... | collective-permute-start | bytes 10616840 | tf_op jit(solution)/shard_map/ppermute | solution.py:267
  21.3 2.2 %collective-permute-start = (bf16[10,16,768]{2,1,0:T(8,128)(2,1)S(1)}, bf16[10,16,768]{2,1,0:T(8,128)(2,1)S(1)}, u32[]{:S(2)}, u32[]{:S(2)}) collective-permute-start(bf16[10,16,768]{2,1,0:T(8,128)(2,1)S(1)} %shard_map.74), channel_id=1, source_target_pairs={{0,1},{1,0},{2,3},{3,2},{4,5},{5,4},{6,7},{7,6},{8,9},{9,8},{10,11... | collective-permute-start | bytes 737288 | tf_op jit(solution)/shard_map/ppermute | solution.py:299

commit v15 on v14

--- a/solution.py
+++ b/solution.py
@@ -48,8 +48,8 @@
     return lax.div(at, jnp.int32(by)), lax.rem(at, jnp.int32(by))
 
 
-def pack_kernel(group, video, *refs):
-    out, local, wide, sems = refs
+def pack_kernel(group, video, conv_far, *refs):
+    out, conv_own, local, wide, sems, conv_sem = refs
     count, rows, cols, chans = video.shape
     lines = count * rows
     stride = cols + 2 * EDGE
@@ -61,6 +61,8 @@
         copy = pltpu.make_async_copy(video.at[place], local.at[place], sems.at[at])
         copy.start()
         copies.append(copy)
+    taps = pltpu.make_async_copy(conv_far.at[:, 1], conv_own, conv_sem)
+    taps.start()
     nothing = jnp.zeros((EDGE, chans), f32)
     for at in range(lines):
         fill(wide, at * stride, nothing)
@@ -74,6 +76,7 @@
         for w in range(0, span, together):
             tile = jnp.concatenate([get(wide, start + w + i, lines, stride) for i in range(together)], axis=0)
             out[k, pl.ds(w * lines, 16), :] = tile.astype(bf16)
+    taps.wait()
 
 
 def frames_of(ref, w, r, count, rows, sources, step):
@@ -131,8 +134,10 @@
 
 
 def shift_kernel(count, rows, video, ids_far, *refs):
-    conv_weight, far, (total, bias, *near) = refs[0], refs[1:5], refs[5:11]
-    vid, grid, ids, sems, ids_sem = refs[11:]
+    conv_own, conv_far, far, (total, bias, *near) = refs[0], refs[1], refs[2:6], refs[6:14]
+    vid, grid, ids, sems, ids_sem = refs[14:]
+    taps = {1: conv_own, 0: near[0], 2: near[1]}
+    far = (conv_far.at[:, 0], conv_far.at[:, 2]) + tuple(far)
     ids_copy = pltpu.make_async_copy(ids_far, ids, ids_sem)
     ids_copy.start()
     others = [pltpu.make_async_copy(src, dst, sems.at[i]) for i, (src, dst) in enumerate(zip(far, near))]
@@ -151,9 +156,11 @@
             if 1 <= w <= own:
                 total[w - 1, r] = jnp.concatenate(now, 0)
 
-    for b in range(TAPS):
+    for b in taps:
+        if b != 1:
+            others[b // 2].wait()
         low, high = max(0, 1 - b), min(rows, rows + 1 - b)
-        weight = jnp.concatenate([conv_weight[a, b, e] for e in range(TAPS) for a in range(TAPS)], axis=0)
+        weight = jnp.concatenate([taps[b][a, e] for e in range(TAPS) for a in range(TAPS)], axis=0)
         for w in range(0, own, half):
             window = depth([grid[w + e : w + e + half, low + b - 1 : high + b - 1] for e in range(TAPS)])
             window = window.reshape(half * (high - low) * frames, TAPS * TAPS * chans)
@@ -162,12 +169,12 @@
             some[...] = some[...] + part.reshape(half, high - low, frames, chans)
     ids_copy.wait()
     fill_bias(bias, ids, frames, count)
-    for copy in others:
+    for copy in others[2:]:
         copy.wait()
 
 
 def main_kernel(
-    count, rows, group, edge, given, bias, conv_weight, w_query, w_key, w_value, w_output, *refs
+    count, rows, group, edge, given, bias, conv_above, conv_below, w_query, w_key, w_value, w_output, *refs
 ):
     out, res = refs
     own, _, frames, chans = given.shape
@@ -179,12 +186,13 @@
     several = area // (rows * frames)
 
     lower = lax.axis_index("height")
-    b = (TAPS - 1) * (1 - lower)
     part = jnp.zeros((own * frames, chans), f32)
     for e in range(TAPS):
         window = edge[e : e + own].reshape(own * frames, TAPS * chans)
-        weight = jnp.concatenate([conv_weight[a, b, e] for a in range(TAPS)], axis=0)
-        part = part + jnp.dot(window, weight, preferred_element_type=f32)
+        above, below = (
+            jnp.concatenate([taps[a, e] for a in range(TAPS)], axis=0) for taps in (conv_above, conv_below)
+        )
+        part = part + jnp.dot(window, jnp.where(lower == 1, above, below), preferred_element_type=f32)
     part = part.reshape(own, frames, chans)
 
     head_of = divided(lax.broadcasted_iota(jnp.int32, (area, chans), 1), HD)[0]
@@ -263,21 +271,25 @@
     far = pl.BlockSpec(memory_space=pltpu.HBM)
     params = pltpu.CompilerParams(vmem_limit_bytes=VMEM)
     in_far = functools.partial(pltpu.with_memory_space_constraint, memory_space=pltpu.HBM)
-    weights = [in_far(x) for x in (w_query, w_key, w_value, w_output)]
-    conv_weight = lax.ppermute(conv_weight, "height", [(i, i) for i in range(lax.axis_size("height"))])
-
-    blocks = pl.pallas_call(
+    conv_weight, *weights = (in_far(x) for x in (conv_weight, w_query, w_key, w_value, w_output))
+
+    slab = (TAPS, TAPS, chans, chans)
+    blocks, conv_own = pl.pallas_call(
         functools.partial(pack_kernel, group),
-        out_shape=jax.ShapeDtypeStruct((group, span * lines, chans), bf16),
-        in_specs=[far],
-        out_specs=near,
+        out_shape=[
+            jax.ShapeDtypeStruct((group, span * lines, chans), bf16),
+            jax.ShapeDtypeStruct(slab, bf16),
+        ],
+        in_specs=[far, far],
+        out_specs=[near, near],
         scratch_shapes=[
             pltpu.VMEM(video.shape, bf16),
             scratch(lines * (cols + 2 * EDGE), chans),
             pltpu.SemaphoreType.DMA((lines,)),
+            pltpu.SemaphoreType.DMA(()),
         ],
         compiler_params=params,
-    )(in_far(video))
+    )(in_far(video), conv_weight)
     piece = exchanged(blocks)
     ids = block_ids
     if outer > 1:
@@ -305,26 +317,27 @@
             jax.ShapeDtypeStruct((own, rows, frames, chans), f32),
             jax.ShapeDtypeStruct((area, area), f32),
         ]
+        + [jax.ShapeDtypeStruct(slab, bf16)] * 2
         + [jax.ShapeDtypeStruct(x.shape, bf16) for x in weights],
-        in_specs=[near, far, near] + [far] * 4,
-        out_specs=[near] * 6,
+        in_specs=[near, far, near] + [far] * 5,
+        out_specs=[near] * 8,
         scratch_shapes=[
             stored,
             pltpu.VMEM((span, rows, frames, TAPS * chans), bf16),
             pltpu.SMEM((frames,), jnp.int32),
-            pltpu.SemaphoreType.DMA((4,)),
+            pltpu.SemaphoreType.DMA((6,)),
             pltpu.SemaphoreType.DMA(()),
         ],
         compiler_params=params,
-    )(piece, in_far(ids), conv_weight, *weights)
+    )(piece, in_far(ids), conv_own, conv_weight, *weights)
     blocks = pl.pallas_call(
         functools.partial(main_kernel, count, rows, group),
         out_shape=jax.ShapeDtypeStruct((group, own * lines, chans), bf16),
-        in_specs=[near] * 8,
+        in_specs=[near] * 9,
         out_specs=near,
         scratch_shapes=[scratch(group * own * lines, chans)],
         compiler_params=params,
-    )(edge, total, bias, conv_weight, *weights)
+    )(edge, total, bias, *weights)
     return pl.pallas_call(
         unpack_kernel,
         out_shape=jax.ShapeDtypeStruct(video.shape, bf16),

time: 39.4 us -> 38.5 us (0.977)
  starting transfers between devices: 2.07 us -> 0.07 us
  Pallas kernels: 6.66 us -> 7.83 us
    ppermute x1 -> x0, starting transfers between devices: 2 us -> none  [per_device(): lax.ppermute(conv_weight, 'height', [(i, i) for i in range(lax.axis_size(...]
    pallas_call x1, Pallas kernels: 2.1 us -> 2.87 us  [per_device(): pl.pallas_call(functools.partial(shift_kernel, count, rows), out_shape=[j...]
    pallas_call x1, Pallas kernels: 1.11 us -> 1.51 us  [per_device(): pl.pallas_call(functools.partial(pack_kernel, group), out_shape=[jax.Shap...]
  transfers between devices with their start and end apart: 2 -> 1, of which waited for: 0 -> 0; matrix products, arithmetic and copies ran while one was open for 0% -> 0% of each run, Pallas kernels for 9% -> 7%
where the time goes in v15:
time: 38.5 us; the launch traced here: 38.3 us
  blocking collectives  30.3 us (79%)
  Pallas kernels  7.83 us (20%)
    all_to_all x2, blocking collectives, exchanged(): return lax.all_to_all(blocks, 'tm', split_axis=0, concat_axis=0, tiled=True)  30.3 us
    pallas_call x1, Pallas kernels, per_device(): pl.pallas_call(functools.partial(shift_kernel, count, rows), out_shape=[j...  2.87 us
    pallas_call x1, Pallas kernels, per_device(): pl.pallas_call(functools.partial(main_kernel, count, rows, group), out_sh...  2.44 us
    pallas_call x1, Pallas kernels, per_device(): pl.pallas_call(functools.partial(pack_kernel, group), out_shape=[jax.Shap...  1.51 us
  transfers between devices with their start and end apart: 1, of which 0 were waited for; matrix products, arithmetic and copies ran while one was open for 0% of the time, Pallas kernels for 7%

profile of v15, /device:TPU:0, one launch (start us, length us, event | category | flops | bytes accessed | tf_op | source)
XLA Modules:
  0.0 38.3 jit_solution(1387615155388604831)
XLA Ops:
  0.0 1.5 %shard_map.73 = (bf16[8,80,256]{2,1,0:T(8,128)(2,1)S(1)}, bf16[3,3,256,256]{3,2,1,0:T(8,128)(2,1)S(1)}) custom-call(bf16[2,4,64,256]{3,2,1,0:T(8,128)(2,1)} %video.1, bf16[3,3,3,256,256]{4,3,2,1,0:T(8,128)(2,1)} %refs_1_.1), custom_call_target="tpu_custom_call" | custom-call | tf_op jit(solution)/shard_map/pallas_call | solution.py:277
  1.5 18.0 %all_to_all.10.video = bf16[8,80,256]{2,1,0:T(8,128)(2,1)S(1)} all-to-all(bf16[8,80,256]{2,1,0:T(8,128)(2,1)S(1)} %get-tuple-element.15), channel_id=1, replica_groups=mesh['groups'=2,'tm'=8,'height'=2] {'tm'}, dimensions={0} | all-to-all | bytes 655360 | tf_op jit(solution)/shard_map/all_to_all | solution.py:261
  19.5 0.3 shard_map.74
  19.7 0.1 collective-permute-start
  19.8 2.9 %shard_map.75 = (f32[8,4,16,256]{3,2,1,0:T(8,128)S(1)}, f32[128,128]{1,0:T(8,128)S(1)}, bf16[3,3,256,256]{3,2,1,0:T(8,128)(2,1)S(1)}, bf16[3,3,256,256]{3,2,1,0:...) custom-call(bf16[8,80,256]{2,1,0:T(8,128)(2,1)S(1)} %all_to_all.10.v, ...), custom_call_target="tpu_custom_call" | custom-call | tf_op jit(solution)/shard_map/pallas_call | solution.py:314
  22.7 0.0 collective-permute-done.edge
  22.7 2.4 %shard_map.76 = bf16[8,64,256]{2,1,0:T(8,128)(2,1)S(1)} custom-call(bf16[10,16,768]{2,1,0:T(8,128)(2,1)S(1)} %collective-permute-done.edge, f32[8,4,16,256]{3,2,1,0:T(8,128)S(1)} %get-tuple-element.17.given, f32[128,128]{1,0:T(8,128)S(1)} %get-tuple-element.18.bias, bf16[3,3,256,256]{3,2,1,0:T(8,128)(2,1)S(1)} %get-tuple-element.19.conv_above, ...), custom_call_target="tpu_custom_call" | custom-call | tf_op jit(solution)/shard_map/pallas_call | solution.py:333
  25.1 12.4 %all_to_all.11.packed = bf16[8,64,256]{2,1,0:T(8,128)(2,1)S(1)} all-to-all(bf16[8,64,256]{2,1,0:T(8,128)(2,1)S(1)} %shard_map.76), channel_id=1, replica_groups=mesh['groups'=2,'tm'=8,'height'=2] {'tm'}, dimensions={0} | all-to-all | bytes 524288 | tf_op jit(solution)/shard_map/all_to_all | solution.py:261
  37.5 0.8 %shard_map.77 = bf16[2,4,64,256]{3,2,1,0:T(8,128)(2,1)} custom-call(bf16[8,64,256]{2,1,0:T(8,128)(2,1)S(1)} %all_to_all.11.packed), custom_call_target="tpu_custom_call" | custom-call | tf_op jit(solution)/shard_map/pallas_call | solution.py:341
Async XLA Ops:
  19.7 3.0 %collective-permute-start = (bf16[10,16,768]{2,1,0:T(8,128)(2,1)S(1)}, bf16[10,16,768]{2,1,0:T(8,128)(2,1)S(1)}, u32[]{:S(2)}, u32[]{:S(2)}) collective-permute-start(bf16[10,16,768]{2,1,0:T(8,128)(2,1)S(1)} %shard_map.74), channel_id=1, source_target_pairs={{0,1},{1,0},{2,3},{3,2},{4,5},{5,4},{6,7},{7,6},{8,9},{9,8},{10,11... | collective-permute-start | bytes 737288 | tf_op jit(solution)/shard_map/ppermute | solution.py:311

commit v16 on v13

--- a/solution.py
+++ b/solution.py
@@ -108,7 +108,8 @@
     fill(vid, 0, video[...].reshape(sources * step, chans).astype(f32))
     row = (rows - 1) * (1 - lax.axis_index("height"))
     for w in range(span):
-        edge[w] = shifted([activated(x) for x in frames_of(vid, w, row, count, rows, sources, step)])
+        frames = frames_of(vid, w, row, count, rows, sources, step)
+        edge[w] = jnp.concatenate([activated(x) for x in frames], axis=0).astype(bf16)
 
 
 def fill_bias(bias, ids, frames, count):
@@ -130,9 +131,22 @@
     bias[...] = jnp.where(permit, 0.0, -1e30)
 
 
+def convolve(total, grid, conv_weight, start):
+    own, rows, frames, chans = total.shape
+    for b in range(TAPS):
+        low, high = max(0, 1 - b), min(rows, rows + 1 - b)
+        weight = jnp.concatenate([conv_weight[a, b, e] for e in range(TAPS) for a in range(TAPS)], axis=0)
+        window = depth(
+            [grid[start + e : start + e + own, low + b - 1 : high + b - 1] for e in range(TAPS)]
+        )
+        window = window.reshape(own * (high - low) * frames, TAPS * TAPS * chans)
+        part = jnp.dot(window, weight, preferred_element_type=f32)
+        total[:, low:high] = total[:, low:high] + part.reshape(own, high - low, frames, chans)
+
+
 def shift_kernel(count, rows, video, ids_far, *refs):
-    conv_weight, far, (total, bias, *near) = refs[0], refs[1:5], refs[5:11]
-    vid, grid, ids, sems, ids_sem = refs[11:]
+    conv_weight, far, (grid, total, bias, *near) = refs[0], refs[1:5], refs[5:12]
+    vid, ids, sems, ids_sem = refs[12:]
     ids_copy = pltpu.make_async_copy(ids_far, ids, ids_sem)
     ids_copy.start()
     others = [pltpu.make_async_copy(src, dst, sems.at[i]) for i, (src, dst) in enumerate(zip(far, near))]
@@ -142,7 +156,7 @@
     span = step // (count * rows)
     own = span - 2
     frames = sources * count
-    half = own // 2 if own % 2 == 0 else own
+    half = own - own // 2
     fill(vid, 0, video[...].reshape(sources * step, chans).astype(f32))
     for w in range(span):
         for r in range(rows):
@@ -151,15 +165,7 @@
             if 1 <= w <= own:
                 total[w - 1, r] = jnp.concatenate(now, 0)
 
-    for b in range(TAPS):
-        low, high = max(0, 1 - b), min(rows, rows + 1 - b)
-        weight = jnp.concatenate([conv_weight[a, b, e] for e in range(TAPS) for a in range(TAPS)], axis=0)
-        for w in range(0, own, half):
-            window = depth([grid[w + e : w + e + half, low + b - 1 : high + b - 1] for e in range(TAPS)])
-            window = window.reshape(half * (high - low) * frames, TAPS * TAPS * chans)
-            part = jnp.dot(window, weight, preferred_element_type=f32)
-            some = total.at[w : w + half, low:high]
-            some[...] = some[...] + part.reshape(half, high - low, frames, chans)
+    convolve(total.at[:half], grid, conv_weight, 0)
     ids_copy.wait()
     fill_bias(bias, ids, frames, count)
     for copy in others:
@@ -167,9 +173,9 @@
 
 
 def main_kernel(
-    count, rows, group, edge, given, bias, conv_weight, w_query, w_key, w_value, w_output, *refs
+    count, rows, group, edge, grid, given, bias, conv_weight, w_query, w_key, w_value, w_output, *refs
 ):
-    out, res = refs
+    out, res, rest = refs
     own, _, frames, chans = given.shape
     sources = frames // count
     lines = count * rows
@@ -180,9 +186,13 @@
 
     lower = lax.axis_index("height")
     b = (TAPS - 1) * (1 - lower)
+    border = []
+    for w in range(own + 2):
+        x = edge[w].astype(f32)
+        border.append(shifted([x[t * sources : (t + 1) * sources] for t in range(count)]))
     part = jnp.zeros((own * frames, chans), f32)
     for e in range(TAPS):
-        window = edge[e : e + own].reshape(own * frames, TAPS * chans)
+        window = jnp.concatenate(border[e : e + own], axis=0)
         weight = jnp.concatenate([conv_weight[a, b, e] for a in range(TAPS)], axis=0)
         part = part + jnp.dot(window, weight, preferred_element_type=f32)
     part = part.reshape(own, frames, chans)
@@ -191,19 +201,23 @@
     single = [jnp.where(head_of == h, 1.0, 0.0).astype(bf16) for h in range(heads)]
     scaled = [mask * jnp.asarray(HD ** (-0.5), bf16) for mask in single]
 
-    lines_of = []
-    for r in range(rows):
-        row = given[:, r] + jnp.where(r == (rows - 1) * (1 - lower), part, 0.0)
-        lines_of.append(row[:, None])
-    hidden = jnp.concatenate(lines_of, axis=1).reshape(own * rows * frames, chans).astype(bf16).astype(f32)
-    normed = rms(hidden).astype(bf16)
-    query, keys, values = (
-        jnp.dot(normed, weight[...], preferred_element_type=f32).astype(bf16) for weight in (w_query, w_key, w_value)
-    )
-    half = own // 2 if own % (2 * several) == 0 else own
-    for start in range(0, own, half):
+    half = own - own // 2
+    rest[...] = given[half:]
+    for start, end, sums in ((0, half, given.at[:half]), (half, own, rest)):
+        if start:
+            convolve(rest, grid, conv_weight, half)
+        lines_of = []
+        for r in range(rows):
+            row = sums[:, r] + jnp.where(r == (rows - 1) * (1 - lower), part[start:end], 0.0)
+            lines_of.append(row[:, None])
+        hidden = jnp.concatenate(lines_of, axis=1).reshape(-1, chans).astype(bf16).astype(f32)
+        normed = rms(hidden).astype(bf16)
+        query, keys, values = (
+            jnp.dot(normed, weight[...], preferred_element_type=f32).astype(bf16)
+            for weight in (w_query, w_key, w_value)
+        )
         gone = []
-        for at in range(start * rows * frames, (start + half) * rows * frames, area):
+        for at in range(0, (end - start) * rows * frames, area):
             group_of = slice(at, at + area)
             queries = jnp.concatenate([query[group_of] * mask for mask in scaled], axis=0)
             scores = lax.dot_general(
@@ -219,10 +233,8 @@
             attended = jnp.dot(jnp.concatenate(weights, axis=1), heads_values, preferred_element_type=f32)
             gone.append((attended / under).astype(bf16))
         attended = jnp.concatenate(gone, axis=0)
-        encoded = hidden[start * rows * frames : (start + half) * rows * frames] + jnp.dot(
-            attended, w_output[...], preferred_element_type=f32
-        )
-        for w in range(half):
+        encoded = hidden + jnp.dot(attended, w_output[...], preferred_element_type=f32)
+        for w in range(end - start):
             for r in range(rows):
                 for t in range(count):
                     first = ((w * rows + r) * count + t + 1) * sources - group
@@ -290,27 +302,28 @@
     stored = scratch(sources * span * lines, chans)
     edge = pl.pallas_call(
         functools.partial(edge_kernel, count, rows),
-        out_shape=jax.ShapeDtypeStruct((span, frames, TAPS * chans), bf16),
+        out_shape=jax.ShapeDtypeStruct((span, frames, chans), bf16),
         in_specs=[near],
         out_specs=near,
         scratch_shapes=[stored],
         compiler_params=params,
     )(piece)
     edge = lax.ppermute(edge, "height", [(0, 1), (1, 0)])
-    several = max(n for n in range(1, own + 1) if own % n == 0 and (n == 1 or n * rows * frames <= LANES))
+    fitting = [n for n in range(2, own // 2 + 1) if own // 2 % n == 0 and own % n == 0 and n * rows * frames <= LANES]
+    several = max([1] + fitting)
     area = several * rows * frames
-    total, bias, *weights = pl.pallas_call(
+    grid, total, bias, *weights = pl.pallas_call(
         functools.partial(shift_kernel, count, rows),
         out_shape=[
+            jax.ShapeDtypeStruct((span, rows, frames, TAPS * chans), bf16),
             jax.ShapeDtypeStruct((own, rows, frames, chans), f32),
             jax.ShapeDtypeStruct((area, area), f32),
         ]
         + [jax.ShapeDtypeStruct(x.shape, bf16) for x in weights],
         in_specs=[near, far, near] + [far] * 4,
-        out_specs=[near] * 6,
+        out_specs=[near] * 7,
         scratch_shapes=[
             stored,
-            pltpu.VMEM((span, rows, frames, TAPS * chans), bf16),
             pltpu.SMEM((frames,), jnp.int32),
             pltpu.SemaphoreType.DMA((4,)),
             pltpu.SemaphoreType.DMA(()),
@@ -320,11 +333,14 @@
     blocks = pl.pallas_call(
         functools.partial(main_kernel, count, rows, group),
         out_shape=jax.ShapeDtypeStruct((group, own * lines, chans), bf16),
-        in_specs=[near] * 8,
+        in_specs=[near] * 9,
         out_specs=near,
-        scratch_shapes=[scratch(group * own * lines, chans)],
-        compiler_params=params,
-    )(edge, total, bias, conv_weight, *weights)
+        scratch_shapes=[
+            scratch(group * own * lines, chans),
+            pltpu.VMEM((own // 2, rows, frames, chans), f32),
+        ],
+        compiler_params=params,
+    )(edge, grid, total, bias, conv_weight, *weights)
     return pl.pallas_call(
         unpack_kernel,
         out_shape=jax.ShapeDtypeStruct(video.shape, bf16),

time: 38 us -> 39.4 us (1.037)
  Pallas kernels: 6.66 us -> 7.97 us
    pallas_call x1, Pallas kernels: 2.44 us -> 3.78 us  [per_device(): pl.pallas_call(functools.partial(main_kernel, count, rows, group), out_sh...]
where the time goes in v16:
time: 39.4 us; the launch traced here: 39.1 us
  blocking collectives  30.5 us (77%)
  Pallas kernels  7.97 us (20%)
  starting transfers between devices  0.52 us (1%)
    all_to_all x2, blocking collectives, exchanged(): return lax.all_to_all(blocks, 'tm', split_axis=0, concat_axis=0, tiled=True)  30.5 us
    pallas_call x1, Pallas kernels, per_device(): pl.pallas_call(functools.partial(main_kernel, count, rows, group), out_sh...  3.78 us
    pallas_call x1, Pallas kernels, per_device(): pl.pallas_call(functools.partial(shift_kernel, count, rows), out_shape=[j...  2.07 us
    pallas_call x1, Pallas kernels, per_device(): pl.pallas_call(functools.partial(pack_kernel, group), out_shape=jax.Shape...  1.11 us
  transfers between devices with their start and end apart: 2, of which 0 were waited for; matrix products, arithmetic and copies ran while one was open for 0% of the time, Pallas kernels for 9%

profile of v16, /device:TPU:0, one launch (start us, length us, event | category | flops | bytes accessed | tf_op | source)
XLA Modules:
  0.0 39.1 jit_solution(204536931818841690)
XLA Ops:
  0.0 0.5 %collective-permute-start.1 = (bf16[3,3,3,256,256]{4,3,2,1,0:T(8,128)(2,1)}, bf16[3,3,3,256,256]{4,3,2,1,0:T(8,128)(2,1)S(1)}, u32[]{:S(2)}, u32[]{:S(2)}) collective-permute-start(bf16[3,3,3,256,256]{4,3,2,1,0:T(8,128)(2,1)} %param.9), channel_id=1, source_target_pairs={{0,1},{1,0},{2,3},{3,2},{4,5},{5,4},{6,7},{7,6},{8,9},{9,8},{10,11... | collective-permute-start | bytes 10616840 | tf_op jit(solution)/shard_map/ppermute | solution.py:279
  0.5 1.1 %shard_map.73 = bf16[8,80,256]{2,1,0:T(8,128)(2,1)S(1)} custom-call(bf16[2,4,64,256]{3,2,1,0:T(8,128)(2,1)} %video.1), custom_call_target="tpu_custom_call" | custom-call | tf_op jit(solution)/shard_map/pallas_call | solution.py:281
  1.6 18.2 %all_to_all.10.video = bf16[8,80,256]{2,1,0:T(8,128)(2,1)S(1)} all-to-all(bf16[8,80,256]{2,1,0:T(8,128)(2,1)S(1)} %shard_map.73), channel_id=1, replica_groups=mesh['groups'=2,'tm'=8,'height'=2] {'tm'}, dimensions={0} | all-to-all | bytes 655360 | tf_op jit(solution)/shard_map/all_to_all | solution.py:265
  19.8 0.2 shard_map.74
  20.0 0.1 collective-permute-start
  20.1 0.0 collective-permute-done.1.refs_0_.conv_weight
  20.1 2.1 %shard_map.75 = (bf16[10,4,16,768]{3,2,1,0:T(8,128)(2,1)S(1)}, f32[8,4,16,256]{3,2,1,0:T(8,128)S(1)}, f32[128,128]{1,0:T(8,128)S(1)}, bf16[256,256]{1,0:T(8,128)...) custom-call(bf16[8,80,256]{2,1,0:T(8,128)(2,1)S(1)} %all_to_all.10.video, ...), custom_call_target="tpu_custom_call" | custom-call | tf_op jit(solution)/shard_map/pallas_call | solution.py:315
  22.2 0.0 collective-permute-done.edge
  22.2 3.8 %shard_map.76 = bf16[8,64,256]{2,1,0:T(8,128)(2,1)S(1)} custom-call(bf16[10,16,256]{2,1,0:T(8,128)(2,1)S(1)} %collective-permute-done.edge, bf16[10,4,16,768]{3,2,1,0:T(8,128)(2,1)S(1)} %get-tuple-element.12.grid, f32[8,4,16,256]{3,2,1,0:T(8,128)S(1)} %get-tuple-element.13.given, f32[128,128]{1,0:T(8,128)S(1)} %get-tuple-element.14.bias, ...), custom_call_target="tpu_custom_call" | custom-call | tf_op jit(solution)/shard_map/pallas_call | solution.py:333
  26.0 12.4 %all_to_all.11.packed = bf16[8,64,256]{2,1,0:T(8,128)(2,1)S(1)} all-to-all(bf16[8,64,256]{2,1,0:T(8,128)(2,1)S(1)} %shard_map.76), channel_id=1, replica_groups=mesh['groups'=2,'tm'=8,'height'=2] {'tm'}, dimensions={0} | all-to-all | bytes 524288 | tf_op jit(solution)/shard_map/all_to_all | solution.py:265
  38.3 0.8 %shard_map.77 = bf16[2,4,64,256]{3,2,1,0:T(8,128)(2,1)} custom-call(bf16[8,64,256]{2,1,0:T(8,128)(2,1)S(1)} %all_to_all.11.packed), custom_call_target="tpu_custom_call" | custom-call | tf_op jit(solution)/shard_map/pallas_call | solution.py:344
Async XLA Ops:
  0.0 20.1 %collective-permute-start.1 = (bf16[3,3,3,256,256]{4,3,2,1,0:T(8,128)(2,1)}, bf16[3,3,3,256,256]{4,3,2,1,0:T(8,128)(2,1)S(1)}, u32[]{:S(2)}, u32[]{:S(2)}) collective-permute-start(bf16[3,3,3,256,256]{4,3,2,1,0:T(8,128)(2,1)} %param.9), channel_id=1, source_target_pairs={{0,1},{1,0},{2,3},{3,2},{4,5},{5,4},{6,7},{7,6},{8,9},{9,8},{10,11... | collective-permute-start | bytes 10616840 | tf_op jit(solution)/shard_map/ppermute | solution.py:279
  20.0 2.2 %collective-permute-start = (bf16[10,16,256]{2,1,0:T(8,128)(2,1)S(1)}, bf16[10,16,256]{2,1,0:T(8,128)(2,1)S(1)}, u32[]{:S(2)}, u32[]{:S(2)}) collective-permute-start(bf16[10,16,256]{2,1,0:T(8,128)(2,1)S(1)} %shard_map.74), channel_id=1, source_target_pairs={{0,1},{1,0},{2,3},{3,2},{4,5},{5,4},{6,7},{7,6},{8,9},{9,8},{10,11... | collective-permute-start | bytes 245768 | tf_op jit(solution)/shard_map/ppermute | solution.py:311

commit v17 on v13

--- a/solution.py
+++ b/solution.py
@@ -48,8 +48,29 @@
     return lax.div(at, jnp.int32(by)), lax.rem(at, jnp.int32(by))
 
 
-def pack_kernel(group, video, *refs):
-    out, local, wide, sems = refs
+def fill_bias(bias, ids, frames, count):
+    area = bias.shape[0]
+    sources = frames // count
+
+    def place_of(at):
+        pixel, place = divided(at, frames)
+        inner, source = divided(place, sources)
+        frame = source * count + inner
+        block = jnp.zeros(at.shape, jnp.int32)
+        for s in range(frames):
+            block = jnp.where(frame == s, ids[s], block)
+        return pixel, frame, block
+
+    row_p, row_t, row_b = place_of(lax.broadcasted_iota(jnp.int32, (area, area), 0))
+    col_p, col_t, col_b = place_of(lax.broadcasted_iota(jnp.int32, (1, area), 1))
+    permit = (row_p == col_p) & (col_t <= row_t) & (col_b >= row_b - 1)
+    bias[...] = jnp.where(permit, 0.0, -1e30)
+
+
+def pack_kernel(group, ids_far, video, *refs):
+    out, bias, ids, local, wide, sems, ids_sem = refs
+    ids_copy = pltpu.make_async_copy(ids_far, ids, ids_sem)
+    ids_copy.start()
     count, rows, cols, chans = video.shape
     lines = count * rows
     stride = cols + 2 * EDGE
@@ -65,6 +86,8 @@
     for at in range(lines):
         fill(wide, at * stride, nothing)
         fill(wide, at * stride + EDGE + cols, nothing)
+    ids_copy.wait()
+    fill_bias(bias, ids, ids.shape[0], count)
     for at, copy in enumerate(copies):
         copy.wait()
         fill(wide, at * stride + EDGE, local[at // rows, at % rows].astype(f32))
@@ -111,30 +134,8 @@
         edge[w] = shifted([activated(x) for x in frames_of(vid, w, row, count, rows, sources, step)])
 
 
-def fill_bias(bias, ids, frames, count):
-    area = bias.shape[0]
-    sources = frames // count
-
-    def place_of(at):
-        pixel, place = divided(at, frames)
-        inner, source = divided(place, sources)
-        frame = source * count + inner
-        block = jnp.zeros(at.shape, jnp.int32)
-        for s in range(frames):
-            block = jnp.where(frame == s, ids[s], block)
-        return pixel, frame, block
-
-    row_p, row_t, row_b = place_of(lax.broadcasted_iota(jnp.int32, (area, area), 0))
-    col_p, col_t, col_b = place_of(lax.broadcasted_iota(jnp.int32, (1, area), 1))
-    permit = (row_p == col_p) & (col_t <= row_t) & (col_b >= row_b - 1)
-    bias[...] = jnp.where(permit, 0.0, -1e30)
-
-
-def shift_kernel(count, rows, video, ids_far, *refs):
-    conv_weight, far, (total, bias, *near) = refs[0], refs[1:5], refs[5:11]
-    vid, grid, ids, sems, ids_sem = refs[11:]
-    ids_copy = pltpu.make_async_copy(ids_far, ids, ids_sem)
-    ids_copy.start()
+def shift_kernel(count, rows, video, *refs):
+    conv_weight, far, (total, *near), (vid, grid, sems) = refs[0], refs[1:5], refs[5:10], refs[10:]
     others = [pltpu.make_async_copy(src, dst, sems.at[i]) for i, (src, dst) in enumerate(zip(far, near))]
     for copy in others:
         copy.start()
@@ -160,8 +161,6 @@
             part = jnp.dot(window, weight, preferred_element_type=f32)
             some = total.at[w : w + half, low:high]
             some[...] = some[...] + part.reshape(half, high - low, frames, chans)
-    ids_copy.wait()
-    fill_bias(bias, ids, frames, count)
     for copy in others:
         copy.wait()
 
@@ -189,6 +188,7 @@
 
     head_of = divided(lax.broadcasted_iota(jnp.int32, (area, chans), 1), HD)[0]
     single = [jnp.where(head_of == h, 1.0, 0.0).astype(bf16) for h in range(heads)]
+    heads_lanes = jnp.concatenate(single, axis=0)
     scaled = [mask * jnp.asarray(HD ** (-0.5), bf16) for mask in single]
 
     lines_of = []
@@ -209,14 +209,14 @@
             scores = lax.dot_general(
                 queries, keys[group_of], (((1,), (1,)), ((), ())), preferred_element_type=f32
             )
-            weights, under = [], jnp.zeros((area, chans), f32)
+            weights = []
             for h in range(heads):
                 score = scores[h * area : (h + 1) * area] + bias[...]
-                expo = jnp.exp(score - jnp.max(score, axis=-1, keepdims=True))
-                under = jnp.where(head_of == h, jnp.sum(expo, axis=-1, keepdims=True), under)
-                weights.append(expo.astype(bf16))
+                weights.append(jnp.exp(score - jnp.max(score, axis=-1, keepdims=True)).astype(bf16))
+            weights = jnp.concatenate(weights, axis=1)
             heads_values = jnp.concatenate([values[group_of] * mask for mask in single], axis=0)
-            attended = jnp.dot(jnp.concatenate(weights, axis=1), heads_values, preferred_element_type=f32)
+            attended = jnp.dot(weights, heads_values, preferred_element_type=f32)
+            under = jnp.dot(weights, heads_lanes, preferred_element_type=f32)
             gone.append((attended / under).astype(bf16))
         attended = jnp.concatenate(gone, axis=0)
         encoded = hidden[start * rows * frames : (start + half) * rows * frames] + jnp.dot(
@@ -266,27 +266,35 @@
     weights = [in_far(x) for x in (w_query, w_key, w_value, w_output)]
     conv_weight = lax.ppermute(conv_weight, "height", [(0, 1), (1, 0)])
 
-    blocks = pl.pallas_call(
+    ids = block_ids
+    sources = group * (2 if outer > 1 else 1)
+    frames = sources * count
+    if outer > 1:
+        ids = jnp.concatenate([jnp.full((group * count,), -2, jnp.int32), ids])
+        ids = lax.dynamic_slice(ids, (lax.axis_index("outer") * group * count,), (frames,))
+    fitting = [n for n in range(2, own + 1) if own % n == 0 and n * rows * frames <= LANES]
+    area = max([1] + fitting) * rows * frames
+    blocks, bias = pl.pallas_call(
         functools.partial(pack_kernel, group),
-        out_shape=jax.ShapeDtypeStruct((group, span * lines, chans), bf16),
-        in_specs=[far],
-        out_specs=near,
+        out_shape=[
+            jax.ShapeDtypeStruct((group, span * lines, chans), bf16),
+            jax.ShapeDtypeStruct((area, area), f32),
+        ],
+        in_specs=[far, far],
+        out_specs=[near, near],
         scratch_shapes=[
+            pltpu.SMEM((frames,), jnp.int32),
             pltpu.VMEM(video.shape, bf16),
             scratch(lines * (cols + 2 * EDGE), chans),
             pltpu.SemaphoreType.DMA((lines,)),
+            pltpu.SemaphoreType.DMA(()),
         ],
         compiler_params=params,
-    )(in_far(video))
+    )(in_far(ids), in_far(video))
     piece = exchanged(blocks)
-    ids = block_ids
     if outer > 1:
         before = lax.ppermute(piece, "outer", [(i, i + 1) for i in range(outer - 1)])
         piece = jnp.concatenate([before, piece], axis=0)
-        ids = jnp.concatenate([jnp.full((group * count,), -2, jnp.int32), ids])
-        ids = lax.dynamic_slice(ids, (lax.axis_index("outer") * group * count,), (2 * group * count,))
-    sources = piece.shape[0]
-    frames = sources * count
     stored = scratch(sources * span * lines, chans)
     edge = pl.pallas_call(
         functools.partial(edge_kernel, count, rows),
@@ -297,26 +305,19 @@
         compiler_params=params,
     )(piece)
     edge = lax.ppermute(edge, "height", [(0, 1), (1, 0)])
-    several = max(n for n in range(1, own + 1) if own % n == 0 and (n == 1 or n * rows * frames <= LANES))
-    area = several * rows * frames
-    total, bias, *weights = pl.pallas_call(
+    total, *weights = pl.pallas_call(
         functools.partial(shift_kernel, count, rows),
-        out_shape=[
-            jax.ShapeDtypeStruct((own, rows, frames, chans), f32),
-            jax.ShapeDtypeStruct((area, area), f32),
-        ]
+        out_shape=[jax.ShapeDtypeStruct((own, rows, frames, chans), f32)]
         + [jax.ShapeDtypeStruct(x.shape, bf16) for x in weights],
-        in_specs=[near, far, near] + [far] * 4,
-        out_specs=[near] * 6,
+        in_specs=[near, near] + [far] * 4,
+        out_specs=[near] * 5,
         scratch_shapes=[
             stored,
             pltpu.VMEM((span, rows, frames, TAPS * chans), bf16),
-            pltpu.SMEM((frames,), jnp.int32),
             pltpu.SemaphoreType.DMA((4,)),
-            pltpu.SemaphoreType.DMA(()),
         ],
         compiler_params=params,
-    )(piece, in_far(ids), conv_weight, *weights)
+    )(piece, conv_weight, *weights)
     blocks = pl.pallas_call(
         functools.partial(main_kernel, count, rows, group),
         out_shape=jax.ShapeDtypeStruct((group, own * lines, chans), bf16),

time: 38 us -> 38.3 us (level)
  no operation moved by 1% of the time
where the time goes in v17:
time: 38.3 us; the launch traced here: 38.1 us
  blocking collectives  30.5 us (80%)
  Pallas kernels  6.94 us (18%)
  starting transfers between devices  0.52 us (1%)
    all_to_all x2, blocking collectives, exchanged(): return lax.all_to_all(blocks, 'tm', split_axis=0, concat_axis=0, tiled=True)  30.5 us
    pallas_call x1, Pallas kernels, per_device(): pl.pallas_call(functools.partial(main_kernel, count, rows, group), out_sh...  2.75 us
    pallas_call x1, Pallas kernels, per_device(): pl.pallas_call(functools.partial(shift_kernel, count, rows), out_shape=[j...  1.97 us
    pallas_call x1, Pallas kernels, per_device(): pl.pallas_call(functools.partial(pack_kernel, group), out_shape=[jax.Shap...  1.21 us
  transfers between devices with their start and end apart: 2, of which 0 were waited for; matrix products, arithmetic and copies ran while one was open for 0% of the time, Pallas kernels for 9%

profile of v17, /device:TPU:0, one launch (start us, length us, event | category | flops | bytes accessed | tf_op | source)
XLA Modules:
  0.0 38.1 jit_solution(5843184243571524893)
XLA Ops:
  0.0 0.5 %collective-permute-start.1 = (bf16[3,3,3,256,256]{4,3,2,1,0:T(8,128)(2,1)}, bf16[3,3,3,256,256]{4,3,2,1,0:T(8,128)(2,1)S(1)}, u32[]{:S(2)}, u32[]{:S(2)}) collective-permute-start(bf16[3,3,3,256,256]{4,3,2,1,0:T(8,128)(2,1)} %param.9), channel_id=1, source_target_pairs={{0,1},{1,0},{2,3},{3,2},{4,5},{5,4},{6,7},{7,6},{8,9},{9,8},{10,11... | collective-permute-start | bytes 10616840 | tf_op jit(solution)/shard_map/ppermute | solution.py:267
  0.5 1.2 %shard_map.73 = (bf16[8,80,256]{2,1,0:T(8,128)(2,1)S(1)}, f32[128,128]{1,0:T(8,128)S(1)}) custom-call(s32[16]{0:T(128)} %ids_far.1, bf16[2,4,64,256]{3,2,1,0:T(8,128)(2,1)} %video.1), custom_call_target="tpu_custom_call" | custom-call | tf_op jit(solution)/shard_map/pallas_call | solution.py:277
  1.7 18.2 %all_to_all.10.video = bf16[8,80,256]{2,1,0:T(8,128)(2,1)S(1)} all-to-all(bf16[8,80,256]{2,1,0:T(8,128)(2,1)S(1)} %get-tuple-element.12), channel_id=1, replica_groups=mesh['groups'=2,'tm'=8,'height'=2] {'tm'}, dimensions={0} | all-to-all | bytes 655360 | tf_op jit(solution)/shard_map/all_to_all | solution.py:253
  19.9 0.3 shard_map.74
  20.1 0.1 collective-permute-start
  20.2 0.0 collective-permute-done.1.refs_0_.conv_weight
  20.2 2.0 %shard_map.75 = (f32[8,4,16,256]{3,2,1,0:T(8,128)S(1)}, bf16[256,256]{1,0:T(8,128)(2,1)S(1)}, bf16[256,256]{1,0:T(8,128)(2,1)S(1)}, bf16[256,256]{1,0:T(8,128)(2,1)S(1)}, bf16[256,256]{1,0:T(8,128)(2,1)S(1)}) custom-call(bf16[8,80,256]{2,1,0:T(8,128)(2,1)S(1)} %all_to_all.10.video, ...), custom_call_target="tpu_custom_call" | custom-call | tf_op jit(solution)/shard_map/pallas_call | solution.py:308
  22.2 0.0 collective-permute-done.edge
  22.2 2.7 %shard_map.76 = bf16[8,64,256]{2,1,0:T(8,128)(2,1)S(1)} custom-call(bf16[10,16,768]{2,1,0:T(8,128)(2,1)S(1)} %collective-permute-done.edge, f32[8,4,16,256]{3,2,1,0:T(8,128)S(1)} %get-tuple-element.13.given, f32[128,128]{1,0:T(8,128)S(1)} %get-tuple-element.14.bias, bf16[3,3,3,256,256]{4,3,2,1,0:T(8,128)(2,1)S(1)} %collective-permute-done.1.refs_0_.conv_weight, ...), custom_call_target="tpu_custom_call" | custom-call | tf_op jit(solution)/shard_map/pallas_call | solution.py:321
  24.9 12.4 %all_to_all.11.packed = bf16[8,64,256]{2,1,0:T(8,128)(2,1)S(1)} all-to-all(bf16[8,64,256]{2,1,0:T(8,128)(2,1)S(1)} %shard_map.76), channel_id=1, replica_groups=mesh['groups'=2,'tm'=8,'height'=2] {'tm'}, dimensions={0} | all-to-all | bytes 524288 | tf_op jit(solution)/shard_map/all_to_all | solution.py:253
  37.3 0.8 %shard_map.77 = bf16[2,4,64,256]{3,2,1,0:T(8,128)(2,1)} custom-call(bf16[8,64,256]{2,1,0:T(8,128)(2,1)S(1)} %all_to_all.11.packed), custom_call_target="tpu_custom_call" | custom-call | tf_op jit(solution)/shard_map/pallas_call | solution.py:329
Async XLA Ops:
  0.0 20.2 %collective-permute-start.1 = (bf16[3,3,3,256,256]{4,3,2,1,0:T(8,128)(2,1)}, bf16[3,3,3,256,256]{4,3,2,1,0:T(8,128)(2,1)S(1)}, u32[]{:S(2)}, u32[]{:S(2)}) collective-permute-start(bf16[3,3,3,256,256]{4,3,2,1,0:T(8,128)(2,1)} %param.9), channel_id=1, source_target_pairs={{0,1},{1,0},{2,3},{3,2},{4,5},{5,4},{6,7},{7,6},{8,9},{9,8},{10,11... | collective-permute-start | bytes 10616840 | tf_op jit(solution)/shard_map/ppermute | solution.py:267
  20.1 2.1 %collective-permute-start = (bf16[10,16,768]{2,1,0:T(8,128)(2,1)S(1)}, bf16[10,16,768]{2,1,0:T(8,128)(2,1)S(1)}, u32[]{:S(2)}, u32[]{:S(2)}) collective-permute-start(bf16[10,16,768]{2,1,0:T(8,128)(2,1)S(1)} %shard_map.74), channel_id=1, source_target_pairs={{0,1},{1,0},{2,3},{3,2},{4,5},{5,4},{6,7},{7,6},{8,9},{9,8},{10,11... | collective-permute-start | bytes 737288 | tf_op jit(solution)/shard_map/ppermute | solution.py:307

commit v18 on v14

--- a/solution.py
+++ b/solution.py
@@ -264,7 +264,6 @@
     params = pltpu.CompilerParams(vmem_limit_bytes=VMEM)
     in_far = functools.partial(pltpu.with_memory_space_constraint, memory_space=pltpu.HBM)
     weights = [in_far(x) for x in (w_query, w_key, w_value, w_output)]
-    conv_weight = lax.ppermute(conv_weight, "height", [(i, i) for i in range(lax.axis_size("height"))])
 
     blocks = pl.pallas_call(
         functools.partial(pack_kernel, group),
@@ -277,6 +276,7 @@
             pltpu.SemaphoreType.DMA((lines,)),
         ],
         compiler_params=params,
+        cost_estimate=pl.CostEstimate(flops=2000000000, transcendentals=0, bytes_accessed=1000000),
     )(in_far(video))
     piece = exchanged(blocks)
     ids = block_ids

time: 39.4 us -> 37.5 us (0.952)
  starting transfers between devices: 2.07 us -> 0.07 us
    ppermute x1 -> x0, starting transfers between devices: 2 us -> none  [per_device(): lax.ppermute(conv_weight, 'height', [(i, i) for i in range(lax.axis_size(...]
  transfers between devices with their start and end apart: 2 -> 1, of which waited for: 0 -> 0; matrix products, arithmetic and copies ran while one was open for 0% -> 0% of each run, Pallas kernels for 9% -> 6%
where the time goes in v18:
time: 37.5 us; the launch traced here: 37.3 us
  blocking collectives  30.3 us (81%)
  Pallas kernels  6.81 us (18%)
    all_to_all x2, blocking collectives, exchanged(): return lax.all_to_all(blocks, 'tm', split_axis=0, concat_axis=0, tiled=True)  30.3 us
    pallas_call x1, Pallas kernels, per_device(): pl.pallas_call(functools.partial(main_kernel, count, rows, group), out_sh...  2.44 us
    pallas_call x1, Pallas kernels, per_device(): pl.pallas_call(functools.partial(shift_kernel, count, rows), out_shape=[j...  2.1 us
    pallas_call x1, Pallas kernels, per_device(): pl.pallas_call(functools.partial(pack_kernel, group), out_shape=jax.Shape...  1.25 us
    pallas_call x1, Pallas kernels, per_device(): pl.pallas_call(unpack_kernel, out_shape=jax.ShapeDtypeStruct(video.shape,...  0.76 us
  transfers between devices with their start and end apart: 1, of which 0 were waited for; matrix products, arithmetic and copies ran while one was open for 0% of the time, Pallas kernels for 6%

profile of v18, /device:TPU:0, one launch (start us, length us, event | category | flops | bytes accessed | tf_op | source)
XLA Modules:
  0.0 37.3 jit_solution(982123563283400583)
XLA Ops:
  0.0 0.0 copy-start
  0.0 1.3 %shard_map.73 = bf16[8,80,256]{2,1,0:T(8,128)(2,1)S(1)} custom-call(bf16[2,4,64,256]{3,2,1,0:T(8,128)(2,1)} %video.1), custom_call_target="tpu_custom_call" | custom-call | flops 2000000000 | bytes 1000000 | tf_op jit(solution)/shard_map/pallas_call | solution.py:268
  1.3 18.0 %all_to_all.10.video = bf16[8,80,256]{2,1,0:T(8,128)(2,1)S(1)} all-to-all(bf16[8,80,256]{2,1,0:T(8,128)(2,1)S(1)} %shard_map.73), channel_id=1, replica_groups=mesh['groups'=2,'tm'=8,'height'=2] {'tm'}, dimensions={0} | all-to-all | bytes 655360 | tf_op jit(solution)/shard_map/all_to_all | solution.py:253
  19.2 0.3 shard_map.74
  19.5 0.1 collective-permute-start
  19.6 0.0 copy-done
  19.6 2.1 %shard_map.75 = (f32[8,4,16,256]{3,2,1,0:T(8,128)S(1)}, f32[128,128]{1,0:T(8,128)S(1)}, bf16[256,256]{1,0:T(8,128)(2,1)S(1)}, bf16[256,256]{1,0:T(8,128)(2,1)S(1...) custom-call(bf16[8,80,256]{2,1,0:T(8,128)(2,1)S(1)} %all_to_all.10.video, s32[16]{0:T(128)} %ids_far.1, ...), custom_call_target="tpu_custom_call" | custom-call | tf_op jit(solution)/shard_map/pallas_call | solution.py:302
  21.7 0.0 collective-permute-done.edge
  21.7 2.4 %shard_map.76 = bf16[8,64,256]{2,1,0:T(8,128)(2,1)S(1)} custom-call(bf16[10,16,768]{2,1,0:T(8,128)(2,1)S(1)} %collective-permute-done.edge, f32[8,4,16,256]{3,2,1,0:T(8,128)S(1)} %get-tuple-element.11.given, f32[128,128]{1,0:T(8,128)S(1)} %get-tuple-element.12.bias, bf16[3,3,3,256,256]{4,3,2,1,0:T(8,128)(2,1)S(1)} %copy-done, ...), custom_call_target="tpu_custom_call" | custom-call | tf_op jit(solution)/shard_map/pallas_call | solution.py:320
  24.1 12.4 %all_to_all.11.packed = bf16[8,64,256]{2,1,0:T(8,128)(2,1)S(1)} all-to-all(bf16[8,64,256]{2,1,0:T(8,128)(2,1)S(1)} %shard_map.76), channel_id=1, replica_groups=mesh['groups'=2,'tm'=8,'height'=2] {'tm'}, dimensions={0} | all-to-all | bytes 524288 | tf_op jit(solution)/shard_map/all_to_all | solution.py:253
  36.5 0.8 %shard_map.77 = bf16[2,4,64,256]{3,2,1,0:T(8,128)(2,1)} custom-call(bf16[8,64,256]{2,1,0:T(8,128)(2,1)S(1)} %all_to_all.11.packed), custom_call_target="tpu_custom_call" | custom-call | tf_op jit(solution)/shard_map/pallas_call | solution.py:328
Async XLA Ops:
  0.0 19.6 %copy-start = (bf16[3,3,3,256,256]{4,3,2,1,0:T(8,128)(2,1)S(1)}, bf16[3,3,3,256,256]{4,3,2,1,0:T(8,128)(2,1)}, u32[]{:S(2)}) copy-start(bf16[3,3,3,256,256]{4,3,2,1,0:T(8,128)(2,1)} %conv_weight.1) | copy-start | bytes 10616836
  19.5 2.2 %collective-permute-start = (bf16[10,16,768]{2,1,0:T(8,128)(2,1)S(1)}, bf16[10,16,768]{2,1,0:T(8,128)(2,1)S(1)}, u32[]{:S(2)}, u32[]{:S(2)}) collective-permute-start(bf16[10,16,768]{2,1,0:T(8,128)(2,1)S(1)} %shard_map.74), channel_id=1, source_target_pairs={{0,1},{1,0},{2,3},{3,2},{4,5},{5,4},{6,7},{7,6},{8,9},{9,8},{10,11... | collective-permute-start | bytes 737288 | tf_op jit(solution)/shard_map/ppermute | solution.py:299

commit v19 on v18

--- a/solution.py
+++ b/solution.py
@@ -48,8 +48,9 @@
     return lax.div(at, jnp.int32(by)), lax.rem(at, jnp.int32(by))
 
 
-def pack_kernel(group, video, *refs):
-    out, local, wide, sems = refs
+def pack_kernel(group, ids_far, video, out, ids, near_ids, local, wide, sems, ids_sem):
+    ids_copy = pltpu.make_async_copy(ids_far, near_ids, ids_sem)
+    ids_copy.start()
     count, rows, cols, chans = video.shape
     lines = count * rows
     stride = cols + 2 * EDGE
@@ -65,6 +66,9 @@
     for at in range(lines):
         fill(wide, at * stride, nothing)
         fill(wide, at * stride + EDGE + cols, nothing)
+    ids_copy.wait()
+    for s in range(ids.shape[0]):
+        ids[s : s + 1, :] = jnp.full((1, LANES), near_ids[s], jnp.int32)
     for at, copy in enumerate(copies):
         copy.wait()
         fill(wide, at * stride + EDGE, local[at // rows, at % rows].astype(f32))
@@ -121,7 +125,7 @@
         frame = source * count + inner
         block = jnp.zeros(at.shape, jnp.int32)
         for s in range(frames):
-            block = jnp.where(frame == s, ids[s], block)
+            block = jnp.where(frame == s, ids[s : s + 1, :area], block)
         return pixel, frame, block
 
     row_p, row_t, row_b = place_of(lax.broadcasted_iota(jnp.int32, (area, area), 0))
@@ -130,14 +134,7 @@
     bias[...] = jnp.where(permit, 0.0, -1e30)
 
 
-def shift_kernel(count, rows, video, ids_far, *refs):
-    conv_weight, far, (total, bias, *near) = refs[0], refs[1:5], refs[5:11]
-    vid, grid, ids, sems, ids_sem = refs[11:]
-    ids_copy = pltpu.make_async_copy(ids_far, ids, ids_sem)
-    ids_copy.start()
-    others = [pltpu.make_async_copy(src, dst, sems.at[i]) for i, (src, dst) in enumerate(zip(far, near))]
-    for copy in others:
-        copy.start()
+def shift_kernel(count, rows, video, ids, conv_weight, total, bias, vid, grid):
     sources, step, chans = video.shape
     span = step // (count * rows)
     own = span - 2
@@ -160,10 +157,7 @@
             part = jnp.dot(window, weight, preferred_element_type=f32)
             some = total.at[w : w + half, low:high]
             some[...] = some[...] + part.reshape(half, high - low, frames, chans)
-    ids_copy.wait()
     fill_bias(bias, ids, frames, count)
-    for copy in others:
-        copy.wait()
 
 
 def main_kernel(
@@ -263,30 +257,35 @@
     far = pl.BlockSpec(memory_space=pltpu.HBM)
     params = pltpu.CompilerParams(vmem_limit_bytes=VMEM)
     in_far = functools.partial(pltpu.with_memory_space_constraint, memory_space=pltpu.HBM)
-    weights = [in_far(x) for x in (w_query, w_key, w_value, w_output)]
-
-    blocks = pl.pallas_call(
+
+    sources = group * (2 if outer > 1 else 1)
+    frames = sources * count
+    ids = block_ids
+    if outer > 1:
+        ids = jnp.concatenate([jnp.full((group * count,), -2, jnp.int32), ids])
+        ids = lax.dynamic_slice(ids, (lax.axis_index("outer") * group * count,), (frames,))
+    blocks, ids = pl.pallas_call(
         functools.partial(pack_kernel, group),
-        out_shape=jax.ShapeDtypeStruct((group, span * lines, chans), bf16),
-        in_specs=[far],
-        out_specs=near,
+        out_shape=[
+            jax.ShapeDtypeStruct((group, span * lines, chans), bf16),
+            jax.ShapeDtypeStruct((frames, LANES), jnp.int32),
+        ],
+        in_specs=[far, far],
+        out_specs=[near, near],
         scratch_shapes=[
+            pltpu.SMEM((frames,), jnp.int32),
             pltpu.VMEM(video.shape, bf16),
             scratch(lines * (cols + 2 * EDGE), chans),
             pltpu.SemaphoreType.DMA((lines,)),
+            pltpu.SemaphoreType.DMA(()),
         ],
         compiler_params=params,
         cost_estimate=pl.CostEstimate(flops=2000000000, transcendentals=0, bytes_accessed=1000000),
-    )(in_far(video))
+    )(in_far(ids), in_far(video))
     piece = exchanged(blocks)
-    ids = block_ids
     if outer > 1:
         before = lax.ppermute(piece, "outer", [(i, i + 1) for i in range(outer - 1)])
         piece = jnp.concatenate([before, piece], axis=0)
-        ids = jnp.concatenate([jnp.full((group * count,), -2, jnp.int32), ids])
-        ids = lax.dynamic_slice(ids, (lax.axis_index("outer") * group * count,), (2 * group * count,))
-    sources = piece.shape[0]
-    frames = sources * count
     stored = scratch(sources * span * lines, chans)
     edge = pl.pallas_call(
         functools.partial(edge_kernel, count, rows),
@@ -297,26 +296,19 @@
         compiler_params=params,
     )(piece)
     edge = lax.ppermute(edge, "height", [(0, 1), (1, 0)])
-    several = max(n for n in range(1, own + 1) if own % n == 0 and (n == 1 or n * rows * frames <= LANES))
-    area = several * rows * frames
-    total, bias, *weights = pl.pallas_call(
+    fitting = [n for n in range(2, own + 1) if own % n == 0 and n * rows * frames <= LANES]
+    area = max([1] + fitting) * rows * frames
+    total, bias = pl.pallas_call(
         functools.partial(shift_kernel, count, rows),
         out_shape=[
             jax.ShapeDtypeStruct((own, rows, frames, chans), f32),
             jax.ShapeDtypeStruct((area, area), f32),
-        ]
-        + [jax.ShapeDtypeStruct(x.shape, bf16) for x in weights],
-        in_specs=[near, far, near] + [far] * 4,
-        out_specs=[near] * 6,
-        scratch_shapes=[
-            stored,
-            pltpu.VMEM((span, rows, frames, TAPS * chans), bf16),
-            pltpu.SMEM((frames,), jnp.int32),
-            pltpu.SemaphoreType.DMA((4,)),
-            pltpu.SemaphoreType.DMA(()),
         ],
-        compiler_params=params,
-    )(piece, in_far(ids), conv_weight, *weights)
+        in_specs=[near] * 3,
+        out_specs=[near] * 2,
+        scratch_shapes=[stored, pltpu.VMEM((span, rows, frames, TAPS * chans), bf16)],
+        compiler_params=params,
+    )(piece, ids, conv_weight)
     blocks = pl.pallas_call(
         functools.partial(main_kernel, count, rows, group),
         out_shape=jax.ShapeDtypeStruct((group, own * lines, chans), bf16),
@@ -324,7 +316,7 @@
         out_specs=near,
         scratch_shapes=[scratch(group * own * lines, chans)],
         compiler_params=params,
-    )(edge, total, bias, conv_weight, *weights)
+    )(edge, total, bias, conv_weight, w_query, w_key, w_value, w_output)
     return pl.pallas_call(
         unpack_kernel,
         out_shape=jax.ShapeDtypeStruct(video.shape, bf16),

time: 37.5 us -> 37.7 us (level)
  transfers between devices with their start and end apart: 1 -> 1, of which waited for: 0 -> 0; matrix products, arithmetic and copies ran while one was open for 0% -> 0% of each run, Pallas kernels for 6% -> 5%
where the time goes in v19:
time: 37.7 us; the launch traced here: 37.5 us
  blocking collectives  30.5 us (81%)
  Pallas kernels  6.79 us (18%)
    all_to_all x2, blocking collectives, exchanged(): return lax.all_to_all(blocks, 'tm', split_axis=0, concat_axis=0, tiled=True)  30.5 us
    pallas_call x1, Pallas kernels, per_device(): pl.pallas_call(functools.partial(main_kernel, count, rows, group), out_sh...  2.45 us
    pallas_call x1, Pallas kernels, per_device(): pl.pallas_call(functools.partial(shift_kernel, count, rows), out_shape=[j...  2.06 us
    pallas_call x1, Pallas kernels, per_device(): pl.pallas_call(functools.partial(pack_kernel, group), out_shape=[jax.Shap...  1.26 us
    pallas_call x1, Pallas kernels, per_device(): pl.pallas_call(unpack_kernel, out_shape=jax.ShapeDtypeStruct(video.shape,...  0.76 us
  transfers between devices with their start and end apart: 1, of which 0 were waited for; matrix products, arithmetic and copies ran while one was open for 0% of the time, Pallas kernels for 5%

profile of v19, /device:TPU:0, one launch (start us, length us, event | category | flops | bytes accessed | tf_op | source)
XLA Modules:
  0.0 37.5 jit_solution(3234587356561097571)
XLA Ops:
  0.0 0.0 copy-start
  0.0 1.3 %shard_map.73 = (bf16[8,80,256]{2,1,0:T(8,128)(2,1)S(1)}, s32[16,128]{1,0:T(8,128)S(1)}) custom-call(s32[16]{0:T(128)} %ids_far.1, bf16[2,4,64,256]{3,2,1,0:T(8,128)(2,1)} %video.1), custom_call_target="tpu_custom_call" | custom-call | flops 2000000000 | bytes 1000000 | tf_op jit(solution)/shard_map/pallas_call | solution.py:267
  1.3 0.0 copy-start.1
  1.3 0.0 copy-start.2
  1.3 0.0 copy-start.3
  1.3 0.0 copy-start.4
  1.3 18.1 %all_to_all.10.video = bf16[8,80,256]{2,1,0:T(8,128)(2,1)S(1)} all-to-all(bf16[8,80,256]{2,1,0:T(8,128)(2,1)S(1)} %get-tuple-element.9), channel_id=1, replica_groups=mesh['groups'=2,'tm'=8,'height'=2] {'tm'}, dimensions={0} | all-to-all | bytes 655360 | tf_op jit(solution)/shard_map/all_to_all | solution.py:247
  19.4 0.3 shard_map.74
  19.7 0.1 collective-permute-start
  19.7 0.0 copy-done
  19.8 2.1 %shard_map.75 = (f32[8,4,16,256]{3,2,1,0:T(8,128)S(1)}, f32[128,128]{1,0:T(8,128)S(1)}) custom-call(bf16[8,80,256]{2,1,0:T(8,128)(2,1)S(1)} %all_to_all.10.video, s32[16,128]{1,0:T(8,128)S(1)} %get-tuple-element.10.ids, bf16[3,3,3,256,256]{4,3,2,1,0:T(8,128)(2,1)S(1)} %copy-done), custom_call_target="tpu_custom_call" | custom-call | tf_op jit(solution)/shard_map/pallas_call | solution.py:301
  21.8 0.0 collective-permute-done.edge
  21.8 0.0 copy-done.1
  21.8 0.0 copy-done.2
  21.9 0.0 copy-done.3
  21.9 0.0 copy-done.4
  21.9 2.5 %shard_map.76 = bf16[8,64,256]{2,1,0:T(8,128)(2,1)S(1)} custom-call(bf16[10,16,768]{2,1,0:T(8,128)(2,1)S(1)} %collective-permute-done.edge, f32[8,4,16,256]{3,2,1,0:T(8,128)S(1)} %get-tuple-element.11.given, f32[128,128]{1,0:T(8,128)S(1)} %get-tuple-element.12.bias, bf16[3,3,3,256,256]{4,3,2,1,0:T(8,128)(2,1)S(1)} %copy-done, ...), custom_call_target="tpu_custom_call" | custom-call | tf_op jit(solution)/shard_map/pallas_call | solution.py:312
  24.3 12.4 %all_to_all.11.packed = bf16[8,64,256]{2,1,0:T(8,128)(2,1)S(1)} all-to-all(bf16[8,64,256]{2,1,0:T(8,128)(2,1)S(1)} %shard_map.76), channel_id=1, replica_groups=mesh['groups'=2,'tm'=8,'height'=2] {'tm'}, dimensions={0} | all-to-all | bytes 524288 | tf_op jit(solution)/shard_map/all_to_all | solution.py:247
  36.7 0.8 %shard_map.77 = bf16[2,4,64,256]{3,2,1,0:T(8,128)(2,1)} custom-call(bf16[8,64,256]{2,1,0:T(8,128)(2,1)S(1)} %all_to_all.11.packed), custom_call_target="tpu_custom_call" | custom-call | tf_op jit(solution)/shard_map/pallas_call | solution.py:320
Async XLA Ops:
  0.0 19.7 %copy-start = (bf16[3,3,3,256,256]{4,3,2,1,0:T(8,128)(2,1)S(1)}, bf16[3,3,3,256,256]{4,3,2,1,0:T(8,128)(2,1)}, u32[]{:S(2)}) copy-start(bf16[3,3,3,256,256]{4,3,2,1,0:T(8,128)(2,1)} %conv_weight.3) | copy-start | bytes 10616836
  1.3 20.6 %copy-start.1 = (bf16[256,256]{1,0:T(8,128)(2,1)S(1)}, bf16[256,256]{1,0:T(8,128)(2,1)}, u32[]{:S(2)}) copy-start(bf16[256,256]{1,0:T(8,128)(2,1)} %w_query.1) | copy-start | bytes 393220
  1.3 20.6 %copy-start.2 = (bf16[256,256]{1,0:T(8,128)(2,1)S(1)}, bf16[256,256]{1,0:T(8,128)(2,1)}, u32[]{:S(2)}) copy-start(bf16[256,256]{1,0:T(8,128)(2,1)} %w_key.1) | copy-start | bytes 393220
  1.3 20.6 %copy-start.3 = (bf16[256,256]{1,0:T(8,128)(2,1)S(1)}, bf16[256,256]{1,0:T(8,128)(2,1)}, u32[]{:S(2)}) copy-start(bf16[256,256]{1,0:T(8,128)(2,1)} %w_value.1) | copy-start | bytes 393220
  1.3 20.6 %copy-start.4 = (bf16[256,256]{1,0:T(8,128)(2,1)S(1)}, bf16[256,256]{1,0:T(8,128)(2,1)}, u32[]{:S(2)}) copy-start(bf16[256,256]{1,0:T(8,128)(2,1)} %w_output.1) | copy-start | bytes 393220
  19.7 2.2 %collective-permute-start = (bf16[10,16,768]{2,1,0:T(8,128)(2,1)S(1)}, bf16[10,16,768]{2,1,0:T(8,128)(2,1)S(1)}, u32[]{:S(2)}, u32[]{:S(2)}) collective-permute-start(bf16[10,16,768]{2,1,0:T(8,128)(2,1)S(1)} %shard_map.74), channel_id=1, source_target_pairs={{0,1},{1,0},{2,3},{3,2},{4,5},{5,4},{6,7},{7,6},{8,9},{9,8},{10,11... | collective-permute-start | bytes 737288 | tf_op jit(solution)/shard_map/ppermute | solution.py:298

commit v20 on v18

--- a/solution.py
+++ b/solution.py
@@ -191,19 +191,21 @@
     single = [jnp.where(head_of == h, 1.0, 0.0).astype(bf16) for h in range(heads)]
     scaled = [mask * jnp.asarray(HD ** (-0.5), bf16) for mask in single]
 
-    lines_of = []
-    for r in range(rows):
-        row = given[:, r] + jnp.where(r == (rows - 1) * (1 - lower), part, 0.0)
-        lines_of.append(row[:, None])
-    hidden = jnp.concatenate(lines_of, axis=1).reshape(own * rows * frames, chans).astype(bf16).astype(f32)
-    normed = rms(hidden).astype(bf16)
-    query, keys, values = (
-        jnp.dot(normed, weight[...], preferred_element_type=f32).astype(bf16) for weight in (w_query, w_key, w_value)
-    )
     half = own // 2 if own % (2 * several) == 0 else own
     for start in range(0, own, half):
+        lines_of = []
+        for r in range(rows):
+            row = given[start : start + half, r]
+            row = row + jnp.where(r == (rows - 1) * (1 - lower), part[start : start + half], 0.0)
+            lines_of.append(row[:, None])
+        hidden = jnp.concatenate(lines_of, axis=1).reshape(half * rows * frames, chans).astype(bf16).astype(f32)
+        normed = rms(hidden).astype(bf16)
+        query, keys, values = (
+            jnp.dot(normed, weight[...], preferred_element_type=f32).astype(bf16)
+            for weight in (w_query, w_key, w_value)
+        )
         gone = []
-        for at in range(start * rows * frames, (start + half) * rows * frames, area):
+        for at in range(0, half * rows * frames, area):
             group_of = slice(at, at + area)
             queries = jnp.concatenate([query[group_of] * mask for mask in scaled], axis=0)
             scores = lax.dot_general(
@@ -219,9 +221,7 @@
             attended = jnp.dot(jnp.concatenate(weights, axis=1), heads_values, preferred_element_type=f32)
             gone.append((attended / under).astype(bf16))
         attended = jnp.concatenate(gone, axis=0)
-        encoded = hidden[start * rows * frames : (start + half) * rows * frames] + jnp.dot(
-            attended, w_output[...], preferred_element_type=f32
-        )
+        encoded = hidden + jnp.dot(attended, w_output[...], preferred_element_type=f32)
         for w in range(half):
             for r in range(rows):
                 for t in range(count):
@@ -230,23 +230,6 @@
                     put(res, place, group, back, encoded[first : first + group])
     done = jnp.concatenate([res[i] for i in range(res.shape[0])], axis=1)
     out[...] = done.astype(bf16).reshape(out.shape)
-
-
-def unpack_kernel(packed, out, local, sems):
-    count, rows, cols, chans = out.shape
-    lines = count * rows
-    regions = packed.shape[0]
-    own = cols // regions
-    wide = packed[...].astype(f32).reshape(regions, lines, own, chans)
-    copies = []
-    for at in range(lines):
-        place = (at // rows, at % rows)
-        local[place] = wide[:, at].reshape(cols, chans).astype(bf16)
-        copy = pltpu.make_async_copy(local.at[place], out.at[place], sems.at[at])
-        copy.start()
-        copies.append(copy)
-    for copy in copies:
-        copy.wait()
 
 
 def exchanged(blocks):
@@ -325,17 +308,8 @@
         scratch_shapes=[scratch(group * own * lines, chans)],
         compiler_params=params,
     )(edge, total, bias, conv_weight, *weights)
-    return pl.pallas_call(
-        unpack_kernel,
-        out_shape=jax.ShapeDtypeStruct(video.shape, bf16),
-        in_specs=[near],
-        out_specs=far,
-        scratch_shapes=[
-            pltpu.VMEM(video.shape, bf16),
-            pltpu.SemaphoreType.DMA((lines,)),
-        ],
-        compiler_params=params,
-    )(exchanged(blocks))
+    returned = exchanged(blocks).reshape(group, lines, own, chans)
+    return jnp.swapaxes(returned, 0, 1).reshape(video.shape)
 
 
 def solution(mesh):

time: 37.5 us -> 37.8 us (level)
  local copies, waits for them, and re-layouts: 0.01 us -> 0.72 us
  Pallas kernels: 6.81 us -> 6.4 us
    pallas_call x1 -> x0, Pallas kernels: 0.76 us -> none  [per_device(): pl.pallas_call(unpack_kernel, out_shape=jax.ShapeDtypeStruct(video.shape,...]
    transpose x0 -> x1, local copies, waits for them, and re-layouts: none -> 0.72 us  [per_device(): return jnp.swapaxes(returned, 0, 1).reshape(video.shape)]
where the time goes in v20:
time: 37.8 us; the launch traced here: 37.6 us
  blocking collectives  30.3 us (80%)
  Pallas kernels  6.4 us (17%)
  local copies, waits for them, and re-layouts  0.72 us (2%)
    all_to_all x2, blocking collectives, exchanged(): return lax.all_to_all(blocks, 'tm', split_axis=0, concat_axis=0, tiled=True)  30.3 us
    pallas_call x1, Pallas kernels, per_device(): pl.pallas_call(functools.partial(main_kernel, count, rows, group), out_sh...  2.8 us
    pallas_call x1, Pallas kernels, per_device(): pl.pallas_call(functools.partial(shift_kernel, count, rows), out_shape=[j...  2.1 us
    pallas_call x1, Pallas kernels, per_device(): pl.pallas_call(functools.partial(pack_kernel, group), out_shape=jax.Shape...  1.25 us
  transfers between devices with their start and end apart: 1, of which 0 were waited for; matrix products, arithmetic and copies ran while one was open for 0% of the time, Pallas kernels for 6%

profile of v20, /device:TPU:0, one launch (start us, length us, event | category | flops | bytes accessed | tf_op | source)
XLA Modules:
  0.0 37.6 jit_solution(2183695007534804755)
XLA Ops:
  0.0 0.0 copy-start
  0.0 1.3 %shard_map.73 = bf16[8,80,256]{2,1,0:T(8,128)(2,1)S(1)} custom-call(bf16[2,4,64,256]{3,2,1,0:T(8,128)(2,1)} %video.1), custom_call_target="tpu_custom_call" | custom-call | flops 2000000000 | bytes 1000000 | tf_op jit(solution)/shard_map/pallas_call | solution.py:251
  1.3 18.0 %all_to_all.10.video = bf16[8,80,256]{2,1,0:T(8,128)(2,1)S(1)} all-to-all(bf16[8,80,256]{2,1,0:T(8,128)(2,1)S(1)} %shard_map.73), channel_id=1, replica_groups=mesh['groups'=2,'tm'=8,'height'=2] {'tm'}, dimensions={0} | all-to-all | bytes 655360 | tf_op jit(solution)/shard_map/all_to_all | solution.py:236
  19.2 0.3 shard_map.74
  19.5 0.1 collective-permute-start
  19.6 0.0 copy-done
  19.6 2.1 %shard_map.75 = (f32[8,4,16,256]{3,2,1,0:T(8,128)S(1)}, f32[128,128]{1,0:T(8,128)S(1)}, bf16[256,256]{1,0:T(8,128)(2,1)S(1)}, bf16[256,256]{1,0:T(8,128)(2,1)S(1...) custom-call(bf16[8,80,256]{2,1,0:T(8,128)(2,1)S(1)} %all_to_all.10.video, s32[16]{0:T(128)} %ids_far.1, ...), custom_call_target="tpu_custom_call" | custom-call | tf_op jit(solution)/shard_map/pallas_call | solution.py:285
  21.7 0.0 collective-permute-done.edge
  21.7 2.8 %shard_map.76 = bf16[8,64,256]{2,1,0:T(8,128)(2,1)S(1)} custom-call(bf16[10,16,768]{2,1,0:T(8,128)(2,1)S(1)} %collective-permute-done.edge, f32[8,4,16,256]{3,2,1,0:T(8,128)S(1)} %get-tuple-element.11.given, f32[128,128]{1,0:T(8,128)S(1)} %get-tuple-element.12.bias, bf16[3,3,3,256,256]{4,3,2,1,0:T(8,128)(2,1)S(1)} %copy-done, ...), custom_call_target="tpu_custom_call" | custom-call | tf_op jit(solution)/shard_map/pallas_call | solution.py:303
  24.5 12.4 %all_to_all.11 = bf16[8,64,256]{2,1,0:T(8,128)(2,1)S(1)} all-to-all(bf16[8,64,256]{2,1,0:T(8,128)(2,1)S(1)} %shard_map.76), channel_id=1, replica_groups=mesh['groups'=2,'tm'=8,'height'=2] {'tm'}, dimensions={0} | all-to-all | bytes 524288 | tf_op jit(solution)/shard_map/all_to_all | solution.py:236
  36.9 0.7 %copy.8 = bf16[8,8,8,256]{3,2,1,0:T(8,128)(2,1)} copy(bf16[8,8,8,256]{3,2,0,1:T(8,128)(2,1)S(1)} %bitcast.4) | data formatting | bytes 524288 | tf_op jit(solution)/shard_map/transpose | solution.py:312
Async XLA Ops:
  0.0 19.6 %copy-start = (bf16[3,3,3,256,256]{4,3,2,1,0:T(8,128)(2,1)S(1)}, bf16[3,3,3,256,256]{4,3,2,1,0:T(8,128)(2,1)}, u32[]{:S(2)}) copy-start(bf16[3,3,3,256,256]{4,3,2,1,0:T(8,128)(2,1)} %conv_weight.1) | copy-start | bytes 10616836
  19.5 2.2 %collective-permute-start = (bf16[10,16,768]{2,1,0:T(8,128)(2,1)S(1)}, bf16[10,16,768]{2,1,0:T(8,128)(2,1)S(1)}, u32[]{:S(2)}, u32[]{:S(2)}) collective-permute-start(bf16[10,16,768]{2,1,0:T(8,128)(2,1)S(1)} %shard_map.74), channel_id=1, source_target_pairs={{0,1},{1,0},{2,3},{3,2},{4,5},{5,4},{6,7},{7,6},{8,9},{9,8},{10,11... | collective-permute-start | bytes 737288 | tf_op jit(solution)/shard_map/ppermute | solution.py:282

commit v21 on v20

--- a/solution.py
+++ b/solution.py
@@ -173,10 +173,8 @@
     own, _, frames, chans = given.shape
     sources = frames // count
     lines = count * rows
-    heads = chans // HD
     back = own * lines
     area = bias.shape[0]
-    several = area // (rows * frames)
 
     lower = lax.axis_index("height")
     b = (TAPS - 1) * (1 - lower)
@@ -187,47 +185,42 @@
         part = part + jnp.dot(window, weight, preferred_element_type=f32)
     part = part.reshape(own, frames, chans)
 
-    head_of = divided(lax.broadcasted_iota(jnp.int32, (area, chans), 1), HD)[0]
-    single = [jnp.where(head_of == h, 1.0, 0.0).astype(bf16) for h in range(heads)]
+    head_of = divided(lax.broadcasted_iota(jnp.int32, (area, LANES), 1), HD)[0]
+    single = [jnp.where(head_of == h, 1.0, 0.0).astype(bf16) for h in range(LANES // HD)]
     scaled = [mask * jnp.asarray(HD ** (-0.5), bf16) for mask in single]
 
-    half = own // 2 if own % (2 * several) == 0 else own
-    for start in range(0, own, half):
-        lines_of = []
-        for r in range(rows):
-            row = given[start : start + half, r]
-            row = row + jnp.where(r == (rows - 1) * (1 - lower), part[start : start + half], 0.0)
-            lines_of.append(row[:, None])
-        hidden = jnp.concatenate(lines_of, axis=1).reshape(half * rows * frames, chans).astype(bf16).astype(f32)
-        normed = rms(hidden).astype(bf16)
-        query, keys, values = (
-            jnp.dot(normed, weight[...], preferred_element_type=f32).astype(bf16)
-            for weight in (w_query, w_key, w_value)
-        )
-        gone = []
-        for at in range(0, half * rows * frames, area):
-            group_of = slice(at, at + area)
-            queries = jnp.concatenate([query[group_of] * mask for mask in scaled], axis=0)
-            scores = lax.dot_general(
-                queries, keys[group_of], (((1,), (1,)), ((), ())), preferred_element_type=f32
-            )
-            weights, under = [], jnp.zeros((area, chans), f32)
-            for h in range(heads):
+    lines_of = []
+    for r in range(rows):
+        row = given[:, r] + jnp.where(r == (rows - 1) * (1 - lower), part, 0.0)
+        lines_of.append(row[:, None])
+    hidden = jnp.concatenate(lines_of, axis=1).reshape(own * rows * frames, chans).astype(bf16).astype(f32)
+    normed = rms(hidden).astype(bf16)
+    query, keys, values = (
+        jnp.dot(normed, weight[...], preferred_element_type=f32).astype(bf16) for weight in (w_query, w_key, w_value)
+    )
+    gone = []
+    for at in range(0, own * rows * frames, area):
+        attended = []
+        for lane in range(0, chans, LANES):
+            block = (slice(at, at + area), slice(lane, lane + LANES))
+            queries = jnp.concatenate([query[block] * mask for mask in scaled], axis=0)
+            scores = lax.dot_general(queries, keys[block], (((1,), (1,)), ((), ())), preferred_element_type=f32)
+            weights, under = [], jnp.zeros((area, LANES), f32)
+            for h in range(len(single)):
                 score = scores[h * area : (h + 1) * area] + bias[...]
                 expo = jnp.exp(score - jnp.max(score, axis=-1, keepdims=True))
                 under = jnp.where(head_of == h, jnp.sum(expo, axis=-1, keepdims=True), under)
                 weights.append(expo.astype(bf16))
-            heads_values = jnp.concatenate([values[group_of] * mask for mask in single], axis=0)
-            attended = jnp.dot(jnp.concatenate(weights, axis=1), heads_values, preferred_element_type=f32)
-            gone.append((attended / under).astype(bf16))
-        attended = jnp.concatenate(gone, axis=0)
-        encoded = hidden + jnp.dot(attended, w_output[...], preferred_element_type=f32)
-        for w in range(half):
-            for r in range(rows):
-                for t in range(count):
-                    first = ((w * rows + r) * count + t + 1) * sources - group
-                    place = (t * rows + r) * own + start + w
-                    put(res, place, group, back, encoded[first : first + group])
+            heads_values = jnp.concatenate([values[block] * mask for mask in single], axis=0)
+            mixed = jnp.dot(jnp.concatenate(weights, axis=1), heads_values, preferred_element_type=f32)
+            attended.append((mixed / under).astype(bf16))
+        gone.append(jnp.concatenate(attended, axis=1))
+    encoded = hidden + jnp.dot(jnp.concatenate(gone, axis=0), w_output[...], preferred_element_type=f32)
+    for w in range(own):
+        for r in range(rows):
+            for t in range(count):
+                first = ((w * rows + r) * count + t + 1) * sources - group
+                put(res, (t * rows + r) * own + w, group, back, encoded[first : first + group])
     done = jnp.concatenate([res[i] for i in range(res.shape[0])], axis=1)
     out[...] = done.astype(bf16).reshape(out.shape)
 

time: 37.8 us -> 37.2 us (0.984)
  Pallas kernels: 6.4 us -> 5.79 us
    pallas_call x1, Pallas kernels: 2.8 us -> 2.18 us  [per_device(): pl.pallas_call(functools.partial(main_kernel, count, rows, group), out_sh...]
where the time goes in v21:
time: 37.2 us; the launch traced here: 37 us
  blocking collectives  30.3 us (81%)
  Pallas kernels  5.79 us (16%)
  local copies, waits for them, and re-layouts  0.72 us (2%)
    all_to_all x2, blocking collectives, exchanged(): return lax.all_to_all(blocks, 'tm', split_axis=0, concat_axis=0, tiled=True)  30.3 us
    pallas_call x1, Pallas kernels, per_device(): pl.pallas_call(functools.partial(main_kernel, count, rows, group), out_sh...  2.18 us
    pallas_call x1, Pallas kernels, per_device(): pl.pallas_call(functools.partial(shift_kernel, count, rows), out_shape=[j...  2.1 us
    pallas_call x1, Pallas kernels, per_device(): pl.pallas_call(functools.partial(pack_kernel, group), out_shape=jax.Shape...  1.25 us
  transfers between devices with their start and end apart: 1, of which 0 were waited for; matrix products, arithmetic and copies ran while one was open for 0% of the time, Pallas kernels for 6%

profile of v21, /device:TPU:0, one launch (start us, length us, event | category | flops | bytes accessed | tf_op | source)
XLA Modules:
  0.0 37.0 jit_solution(684127620679005669)
XLA Ops:
  0.0 0.0 copy-start
  0.0 1.3 %shard_map.73 = bf16[8,80,256]{2,1,0:T(8,128)(2,1)S(1)} custom-call(bf16[2,4,64,256]{3,2,1,0:T(8,128)(2,1)} %video.1), custom_call_target="tpu_custom_call" | custom-call | flops 2000000000 | bytes 1000000 | tf_op jit(solution)/shard_map/pallas_call | solution.py:244
  1.3 18.0 %all_to_all.10.video = bf16[8,80,256]{2,1,0:T(8,128)(2,1)S(1)} all-to-all(bf16[8,80,256]{2,1,0:T(8,128)(2,1)S(1)} %shard_map.73), channel_id=1, replica_groups=mesh['groups'=2,'tm'=8,'height'=2] {'tm'}, dimensions={0} | all-to-all | bytes 655360 | tf_op jit(solution)/shard_map/all_to_all | solution.py:229
  19.2 0.3 shard_map.74
  19.5 0.1 collective-permute-start
  19.6 0.0 copy-done
  19.6 2.1 %shard_map.75 = (f32[8,4,16,256]{3,2,1,0:T(8,128)S(1)}, f32[128,128]{1,0:T(8,128)S(1)}, bf16[256,256]{1,0:T(8,128)(2,1)S(1)}, bf16[256,256]{1,0:T(8,128)(2,1)S(1...) custom-call(bf16[8,80,256]{2,1,0:T(8,128)(2,1)S(1)} %all_to_all.10.video, s32[16]{0:T(128)} %ids_far.1, ...), custom_call_target="tpu_custom_call" | custom-call | tf_op jit(solution)/shard_map/pallas_call | solution.py:278
  21.7 0.0 collective-permute-done.edge
  21.7 2.2 %shard_map.76 = bf16[8,64,256]{2,1,0:T(8,128)(2,1)S(1)} custom-call(bf16[10,16,768]{2,1,0:T(8,128)(2,1)S(1)} %collective-permute-done.edge, f32[8,4,16,256]{3,2,1,0:T(8,128)S(1)} %get-tuple-element.11.given, f32[128,128]{1,0:T(8,128)S(1)} %get-tuple-element.12.bias, bf16[3,3,3,256,256]{4,3,2,1,0:T(8,128)(2,1)S(1)} %copy-done, ...), custom_call_target="tpu_custom_call" | custom-call | tf_op jit(solution)/shard_map/pallas_call | solution.py:296
  23.9 12.4 %all_to_all.11 = bf16[8,64,256]{2,1,0:T(8,128)(2,1)S(1)} all-to-all(bf16[8,64,256]{2,1,0:T(8,128)(2,1)S(1)} %shard_map.76), channel_id=1, replica_groups=mesh['groups'=2,'tm'=8,'height'=2] {'tm'}, dimensions={0} | all-to-all | bytes 524288 | tf_op jit(solution)/shard_map/all_to_all | solution.py:229
  36.2 0.7 %copy.8 = bf16[8,8,8,256]{3,2,1,0:T(8,128)(2,1)} copy(bf16[8,8,8,256]{3,2,0,1:T(8,128)(2,1)S(1)} %bitcast.4) | data formatting | bytes 524288 | tf_op jit(solution)/shard_map/transpose | solution.py:305
Async XLA Ops:
  0.0 19.6 %copy-start = (bf16[3,3,3,256,256]{4,3,2,1,0:T(8,128)(2,1)S(1)}, bf16[3,3,3,256,256]{4,3,2,1,0:T(8,128)(2,1)}, u32[]{:S(2)}) copy-start(bf16[3,3,3,256,256]{4,3,2,1,0:T(8,128)(2,1)} %conv_weight.1) | copy-start | bytes 10616836
  19.5 2.2 %collective-permute-start = (bf16[10,16,768]{2,1,0:T(8,128)(2,1)S(1)}, bf16[10,16,768]{2,1,0:T(8,128)(2,1)S(1)}, u32[]{:S(2)}, u32[]{:S(2)}) collective-permute-start(bf16[10,16,768]{2,1,0:T(8,128)(2,1)S(1)} %shard_map.74), channel_id=1, source_target_pairs={{0,1},{1,0},{2,3},{3,2},{4,5},{5,4},{6,7},{7,6},{8,9},{9,8},{10,11... | collective-permute-start | bytes 737288 | tf_op jit(solution)/shard_map/ppermute | solution.py:275

commit v22 on v21

--- a/solution.py
+++ b/solution.py
@@ -151,10 +151,10 @@
             if 1 <= w <= own:
                 total[w - 1, r] = jnp.concatenate(now, 0)
 
-    for b in range(TAPS):
-        low, high = max(0, 1 - b), min(rows, rows + 1 - b)
-        weight = jnp.concatenate([conv_weight[a, b, e] for e in range(TAPS) for a in range(TAPS)], axis=0)
-        for w in range(0, own, half):
+    for w in range(0, own, half):
+        for b in (1, 0, 2):
+            low, high = max(0, 1 - b), min(rows, rows + 1 - b)
+            weight = jnp.concatenate([conv_weight[a, b, e] for e in range(TAPS) for a in range(TAPS)], axis=0)
             window = depth([grid[w + e : w + e + half, low + b - 1 : high + b - 1] for e in range(TAPS)])
             window = window.reshape(half * (high - low) * frames, TAPS * TAPS * chans)
             part = jnp.dot(window, weight, preferred_element_type=f32)
@@ -178,11 +178,9 @@
 
     lower = lax.axis_index("height")
     b = (TAPS - 1) * (1 - lower)
-    part = jnp.zeros((own * frames, chans), f32)
-    for e in range(TAPS):
-        window = edge[e : e + own].reshape(own * frames, TAPS * chans)
-        weight = jnp.concatenate([conv_weight[a, b, e] for a in range(TAPS)], axis=0)
-        part = part + jnp.dot(window, weight, preferred_element_type=f32)
+    window = depth([edge[e : e + own] for e in range(TAPS)]).reshape(own * frames, TAPS * TAPS * chans)
+    weight = jnp.concatenate([conv_weight[a, b, e] for e in range(TAPS) for a in range(TAPS)], axis=0)
+    part = jnp.dot(window, weight, preferred_element_type=f32)
     part = part.reshape(own, frames, chans)
 
     head_of = divided(lax.broadcasted_iota(jnp.int32, (area, LANES), 1), HD)[0]
@@ -191,7 +189,9 @@
 
     lines_of = []
     for r in range(rows):
-        row = given[:, r] + jnp.where(r == (rows - 1) * (1 - lower), part, 0.0)
+        row = given[:, r]
+        if r in (0, rows - 1):
+            row = row + jnp.where(r == (rows - 1) * (1 - lower), part, 0.0)
         lines_of.append(row[:, None])
     hidden = jnp.concatenate(lines_of, axis=1).reshape(own * rows * frames, chans).astype(bf16).astype(f32)
     normed = rms(hidden).astype(bf16)

time: 37.2 us -> 37.2 us (level)
  no operation moved by 1% of the time
where the time goes in v22:
time: 37.2 us; the launch traced here: 37 us
  blocking collectives  30.3 us (81%)
  Pallas kernels  5.84 us (16%)
  local copies, waits for them, and re-layouts  0.72 us (2%)
    all_to_all x2, blocking collectives, exchanged(): return lax.all_to_all(blocks, 'tm', split_axis=0, concat_axis=0, tiled=True)  30.3 us
    pallas_call x1, Pallas kernels, per_device(): pl.pallas_call(functools.partial(main_kernel, count, rows, group), out_sh...  2.17 us
    pallas_call x1, Pallas kernels, per_device(): pl.pallas_call(functools.partial(shift_kernel, count, rows), out_shape=[j...  2.17 us
    pallas_call x1, Pallas kernels, per_device(): pl.pallas_call(functools.partial(pack_kernel, group), out_shape=jax.Shape...  1.25 us
  transfers between devices with their start and end apart: 1, of which 0 were waited for; matrix products, arithmetic and copies ran while one was open for 0% of the time, Pallas kernels for 6%

profile of v22, /device:TPU:0, one launch (start us, length us, event | category | flops | bytes accessed | tf_op | source)
XLA Modules:
  0.0 37.0 jit_solution(6073654221412680236)
XLA Ops:
  0.0 0.0 copy-start
  0.0 1.3 %shard_map.73 = bf16[8,80,256]{2,1,0:T(8,128)(2,1)S(1)} custom-call(bf16[2,4,64,256]{3,2,1,0:T(8,128)(2,1)} %video.1), custom_call_target="tpu_custom_call" | custom-call | flops 2000000000 | bytes 1000000 | tf_op jit(solution)/shard_map/pallas_call | solution.py:244
  1.3 18.0 %all_to_all.10.video = bf16[8,80,256]{2,1,0:T(8,128)(2,1)S(1)} all-to-all(bf16[8,80,256]{2,1,0:T(8,128)(2,1)S(1)} %shard_map.73), channel_id=1, replica_groups=mesh['groups'=2,'tm'=8,'height'=2] {'tm'}, dimensions={0} | all-to-all | bytes 655360 | tf_op jit(solution)/shard_map/all_to_all | solution.py:229
  19.2 0.3 shard_map.74
  19.5 0.1 collective-permute-start
  19.6 0.0 copy-done
  19.6 2.2 %shard_map.75 = (f32[8,4,16,256]{3,2,1,0:T(8,128)S(1)}, f32[128,128]{1,0:T(8,128)S(1)}, bf16[256,256]{1,0:T(8,128)(2,1)S(1)}, bf16[256,256]{1,0:T(8,128)(2,1)S(1...) custom-call(bf16[8,80,256]{2,1,0:T(8,128)(2,1)S(1)} %all_to_all.10.video, s32[16]{0:T(128)} %ids_far.1, ...), custom_call_target="tpu_custom_call" | custom-call | tf_op jit(solution)/shard_map/pallas_call | solution.py:278
  21.7 0.0 collective-permute-done.edge
  21.8 2.2 %shard_map.76 = bf16[8,64,256]{2,1,0:T(8,128)(2,1)S(1)} custom-call(bf16[10,16,768]{2,1,0:T(8,128)(2,1)S(1)} %collective-permute-done.edge, f32[8,4,16,256]{3,2,1,0:T(8,128)S(1)} %get-tuple-element.11.given, f32[128,128]{1,0:T(8,128)S(1)} %get-tuple-element.12.bias, bf16[3,3,3,256,256]{4,3,2,1,0:T(8,128)(2,1)S(1)} %copy-done, ...), custom_call_target="tpu_custom_call" | custom-call | tf_op jit(solution)/shard_map/pallas_call | solution.py:296
  23.9 12.4 %all_to_all.11 = bf16[8,64,256]{2,1,0:T(8,128)(2,1)S(1)} all-to-all(bf16[8,64,256]{2,1,0:T(8,128)(2,1)S(1)} %shard_map.76), channel_id=1, replica_groups=mesh['groups'=2,'tm'=8,'height'=2] {'tm'}, dimensions={0} | all-to-all | bytes 524288 | tf_op jit(solution)/shard_map/all_to_all | solution.py:229
  36.3 0.7 %copy.8 = bf16[8,8,8,256]{3,2,1,0:T(8,128)(2,1)} copy(bf16[8,8,8,256]{3,2,0,1:T(8,128)(2,1)S(1)} %bitcast.4) | data formatting | bytes 524288 | tf_op jit(solution)/shard_map/transpose | solution.py:305
Async XLA Ops:
  0.0 19.6 %copy-start = (bf16[3,3,3,256,256]{4,3,2,1,0:T(8,128)(2,1)S(1)}, bf16[3,3,3,256,256]{4,3,2,1,0:T(8,128)(2,1)}, u32[]{:S(2)}) copy-start(bf16[3,3,3,256,256]{4,3,2,1,0:T(8,128)(2,1)} %conv_weight.1) | copy-start | bytes 10616836
  19.5 2.3 %collective-permute-start = (bf16[10,16,768]{2,1,0:T(8,128)(2,1)S(1)}, bf16[10,16,768]{2,1,0:T(8,128)(2,1)S(1)}, u32[]{:S(2)}, u32[]{:S(2)}) collective-permute-start(bf16[10,16,768]{2,1,0:T(8,128)(2,1)S(1)} %shard_map.74), channel_id=1, source_target_pairs={{0,1},{1,0},{2,3},{3,2},{4,5},{5,4},{6,7},{7,6},{8,9},{9,8},{10,11... | collective-permute-start | bytes 737288 | tf_op jit(solution)/shard_map/ppermute | solution.py:275

commit v23 on v21

--- a/solution.py
+++ b/solution.py
@@ -55,18 +55,16 @@
     stride = cols + 2 * EDGE
     own = cols // group
     span = own + 2
-    copies = []
-    for at in range(lines):
-        place = (at // rows, at % rows)
-        copy = pltpu.make_async_copy(video.at[place], local.at[place], sems.at[at])
+    copies = [pltpu.make_async_copy(video.at[t], local.at[t], sems.at[t]) for t in range(count)]
+    for copy in copies:
         copy.start()
-        copies.append(copy)
     nothing = jnp.zeros((EDGE, chans), f32)
     for at in range(lines):
         fill(wide, at * stride, nothing)
         fill(wide, at * stride + EDGE + cols, nothing)
-    for at, copy in enumerate(copies):
+    for copy in copies:
         copy.wait()
+    for at in range(lines):
         fill(wide, at * stride + EDGE, local[at // rows, at % rows].astype(f32))
     together = 16 // lines
     for k in range(group):
@@ -249,7 +247,7 @@
         scratch_shapes=[
             pltpu.VMEM(video.shape, bf16),
             scratch(lines * (cols + 2 * EDGE), chans),
-            pltpu.SemaphoreType.DMA((lines,)),
+            pltpu.SemaphoreType.DMA((count,)),
         ],
         compiler_params=params,
         cost_estimate=pl.CostEstimate(flops=2000000000, transcendentals=0, bytes_accessed=1000000),

time: 37.2 us -> 37.2 us (level)
  no operation moved by 1% of the time
where the time goes in v23:
time: 37.2 us; the launch traced here: 37 us
  blocking collectives  30.3 us (81%)
  Pallas kernels  5.86 us (16%)
  local copies, waits for them, and re-layouts  0.72 us (2%)
    all_to_all x2, blocking collectives, exchanged(): return lax.all_to_all(blocks, 'tm', split_axis=0, concat_axis=0, tiled=True)  30.3 us
    pallas_call x1, Pallas kernels, per_device(): pl.pallas_call(functools.partial(main_kernel, count, rows, group), out_sh...  2.18 us
    pallas_call x1, Pallas kernels, per_device(): pl.pallas_call(functools.partial(shift_kernel, count, rows), out_shape=[j...  2.1 us
    pallas_call x1, Pallas kernels, per_device(): pl.pallas_call(functools.partial(pack_kernel, group), out_shape=jax.Shape...  1.32 us
  transfers between devices with their start and end apart: 1, of which 0 were waited for; matrix products, arithmetic and copies ran while one was open for 0% of the time, Pallas kernels for 6%

profile of v23, /device:TPU:0, one launch (start us, length us, event | category | flops | bytes accessed | tf_op | source)
XLA Modules:
  0.0 37.0 jit_solution(11413497308058028757)
XLA Ops:
  0.0 0.0 copy-start
  0.0 1.3 %shard_map.73 = bf16[8,80,256]{2,1,0:T(8,128)(2,1)S(1)} custom-call(bf16[2,4,64,256]{3,2,1,0:T(8,128)(2,1)} %video.1), custom_call_target="tpu_custom_call" | custom-call | flops 2000000000 | bytes 1000000 | tf_op jit(solution)/shard_map/pallas_call | solution.py:242
  1.3 18.0 %all_to_all.10.video = bf16[8,80,256]{2,1,0:T(8,128)(2,1)S(1)} all-to-all(bf16[8,80,256]{2,1,0:T(8,128)(2,1)S(1)} %shard_map.73), channel_id=1, replica_groups=mesh['groups'=2,'tm'=8,'height'=2] {'tm'}, dimensions={0} | all-to-all | bytes 655360 | tf_op jit(solution)/shard_map/all_to_all | solution.py:227
  19.3 0.3 shard_map.74
  19.5 0.1 collective-permute-start
  19.6 0.0 copy-done
  19.6 2.1 %shard_map.75 = (f32[8,4,16,256]{3,2,1,0:T(8,128)S(1)}, f32[128,128]{1,0:T(8,128)S(1)}, bf16[256,256]{1,0:T(8,128)(2,1)S(1)}, bf16[256,256]{1,0:T(8,128)(2,1)S(1...) custom-call(bf16[8,80,256]{2,1,0:T(8,128)(2,1)S(1)} %all_to_all.10.video, s32[16]{0:T(128)} %ids_far.1, ...), custom_call_target="tpu_custom_call" | custom-call | tf_op jit(solution)/shard_map/pallas_call | solution.py:276
  21.7 0.0 collective-permute-done.edge
  21.8 2.2 %shard_map.76 = bf16[8,64,256]{2,1,0:T(8,128)(2,1)S(1)} custom-call(bf16[10,16,768]{2,1,0:T(8,128)(2,1)S(1)} %collective-permute-done.edge, f32[8,4,16,256]{3,2,1,0:T(8,128)S(1)} %get-tuple-element.11.given, f32[128,128]{1,0:T(8,128)S(1)} %get-tuple-element.12.bias, bf16[3,3,3,256,256]{4,3,2,1,0:T(8,128)(2,1)S(1)} %copy-done, ...), custom_call_target="tpu_custom_call" | custom-call | tf_op jit(solution)/shard_map/pallas_call | solution.py:294
  23.9 12.4 %all_to_all.11 = bf16[8,64,256]{2,1,0:T(8,128)(2,1)S(1)} all-to-all(bf16[8,64,256]{2,1,0:T(8,128)(2,1)S(1)} %shard_map.76), channel_id=1, replica_groups=mesh['groups'=2,'tm'=8,'height'=2] {'tm'}, dimensions={0} | all-to-all | bytes 524288 | tf_op jit(solution)/shard_map/all_to_all | solution.py:227
  36.3 0.7 %copy.8 = bf16[8,8,8,256]{3,2,1,0:T(8,128)(2,1)} copy(bf16[8,8,8,256]{3,2,0,1:T(8,128)(2,1)S(1)} %bitcast.4) | data formatting | bytes 524288 | tf_op jit(solution)/shard_map/transpose | solution.py:303
Async XLA Ops:
  0.0 19.6 %copy-start = (bf16[3,3,3,256,256]{4,3,2,1,0:T(8,128)(2,1)S(1)}, bf16[3,3,3,256,256]{4,3,2,1,0:T(8,128)(2,1)}, u32[]{:S(2)}) copy-start(bf16[3,3,3,256,256]{4,3,2,1,0:T(8,128)(2,1)} %conv_weight.1) | copy-start | bytes 10616836
  19.5 2.2 %collective-permute-start = (bf16[10,16,768]{2,1,0:T(8,128)(2,1)S(1)}, bf16[10,16,768]{2,1,0:T(8,128)(2,1)S(1)}, u32[]{:S(2)}, u32[]{:S(2)}) collective-permute-start(bf16[10,16,768]{2,1,0:T(8,128)(2,1)S(1)} %shard_map.74), channel_id=1, source_target_pairs={{0,1},{1,0},{2,3},{3,2},{4,5},{5,4},{6,7},{7,6},{8,9},{9,8},{10,11... | collective-permute-start | bytes 737288 | tf_op jit(solution)/shard_map/ppermute | solution.py:273

commit v24 on v21

--- a/solution.py
+++ b/solution.py
@@ -205,15 +205,15 @@
             block = (slice(at, at + area), slice(lane, lane + LANES))
             queries = jnp.concatenate([query[block] * mask for mask in scaled], axis=0)
             scores = lax.dot_general(queries, keys[block], (((1,), (1,)), ((), ())), preferred_element_type=f32)
-            weights, under = [], jnp.zeros((area, LANES), f32)
+            weights = []
             for h in range(len(single)):
                 score = scores[h * area : (h + 1) * area] + bias[...]
-                expo = jnp.exp(score - jnp.max(score, axis=-1, keepdims=True))
-                under = jnp.where(head_of == h, jnp.sum(expo, axis=-1, keepdims=True), under)
-                weights.append(expo.astype(bf16))
-            heads_values = jnp.concatenate([values[block] * mask for mask in single], axis=0)
+                weights.append(jnp.exp(score - jnp.max(score, axis=-1, keepdims=True)).astype(bf16))
+            heads_values = jnp.concatenate(
+                [jnp.concatenate([values[block] * mask, mask], axis=1) for mask in single], axis=0
+            )
             mixed = jnp.dot(jnp.concatenate(weights, axis=1), heads_values, preferred_element_type=f32)
-            attended.append((mixed / under).astype(bf16))
+            attended.append((mixed[:, :LANES] / mixed[:, LANES:]).astype(bf16))
         gone.append(jnp.concatenate(attended, axis=1))
     encoded = hidden + jnp.dot(jnp.concatenate(gone, axis=0), w_output[...], preferred_element_type=f32)
     for w in range(own):

time: 37.2 us -> 37.1 us (level)
  no operation moved by 1% of the time
where the time goes in v24:
time: 37.1 us; the launch traced here: 36.9 us
  blocking collectives  30.3 us (82%)
  Pallas kernels  5.7 us (15%)
  local copies, waits for them, and re-layouts  0.72 us (2%)
    all_to_all x2, blocking collectives, exchanged(): return lax.all_to_all(blocks, 'tm', split_axis=0, concat_axis=0, tiled=True)  30.3 us
    pallas_call x1, Pallas kernels, per_device(): pl.pallas_call(functools.partial(shift_kernel, count, rows), out_shape=[j...  2.1 us
    pallas_call x1, Pallas kernels, per_device(): pl.pallas_call(functools.partial(main_kernel, count, rows, group), out_sh...  2.09 us
    pallas_call x1, Pallas kernels, per_device(): pl.pallas_call(functools.partial(pack_kernel, group), out_shape=jax.Shape...  1.25 us
  transfers between devices with their start and end apart: 1, of which 0 were waited for; matrix products, arithmetic and copies ran while one was open for 0% of the time, Pallas kernels for 6%

profile of v24, /device:TPU:0, one launch (start us, length us, event | category | flops | bytes accessed | tf_op | source)
XLA Modules:
  0.0 36.9 jit_solution(17704266095243427418)
XLA Ops:
  0.0 0.0 copy-start
  0.0 1.3 %shard_map.73 = bf16[8,80,256]{2,1,0:T(8,128)(2,1)S(1)} custom-call(bf16[2,4,64,256]{3,2,1,0:T(8,128)(2,1)} %video.1), custom_call_target="tpu_custom_call" | custom-call | flops 2000000000 | bytes 1000000 | tf_op jit(solution)/shard_map/pallas_call | solution.py:244
  1.3 18.0 %all_to_all.10.video = bf16[8,80,256]{2,1,0:T(8,128)(2,1)S(1)} all-to-all(bf16[8,80,256]{2,1,0:T(8,128)(2,1)S(1)} %shard_map.73), channel_id=1, replica_groups=mesh['groups'=2,'tm'=8,'height'=2] {'tm'}, dimensions={0} | all-to-all | bytes 655360 | tf_op jit(solution)/shard_map/all_to_all | solution.py:229
  19.2 0.3 shard_map.74
  19.5 0.1 collective-permute-start
  19.6 0.0 copy-done
  19.6 2.1 %shard_map.75 = (f32[8,4,16,256]{3,2,1,0:T(8,128)S(1)}, f32[128,128]{1,0:T(8,128)S(1)}, bf16[256,256]{1,0:T(8,128)(2,1)S(1)}, bf16[256,256]{1,0:T(8,128)(2,1)S(1...) custom-call(bf16[8,80,256]{2,1,0:T(8,128)(2,1)S(1)} %all_to_all.10.video, s32[16]{0:T(128)} %ids_far.1, ...), custom_call_target="tpu_custom_call" | custom-call | tf_op jit(solution)/shard_map/pallas_call | solution.py:278
  21.7 0.0 collective-permute-done.edge
  21.7 2.1 %shard_map.76 = bf16[8,64,256]{2,1,0:T(8,128)(2,1)S(1)} custom-call(bf16[10,16,768]{2,1,0:T(8,128)(2,1)S(1)} %collective-permute-done.edge, f32[8,4,16,256]{3,2,1,0:T(8,128)S(1)} %get-tuple-element.11.given, f32[128,128]{1,0:T(8,128)S(1)} %get-tuple-element.12.bias, bf16[3,3,3,256,256]{4,3,2,1,0:T(8,128)(2,1)S(1)} %copy-done, ...), custom_call_target="tpu_custom_call" | custom-call | tf_op jit(solution)/shard_map/pallas_call | solution.py:296
  23.8 12.4 %all_to_all.11 = bf16[8,64,256]{2,1,0:T(8,128)(2,1)S(1)} all-to-all(bf16[8,64,256]{2,1,0:T(8,128)(2,1)S(1)} %shard_map.76), channel_id=1, replica_groups=mesh['groups'=2,'tm'=8,'height'=2] {'tm'}, dimensions={0} | all-to-all | bytes 524288 | tf_op jit(solution)/shard_map/all_to_all | solution.py:229
  36.1 0.7 %copy.8 = bf16[8,8,8,256]{3,2,1,0:T(8,128)(2,1)} copy(bf16[8,8,8,256]{3,2,0,1:T(8,128)(2,1)S(1)} %bitcast.4) | data formatting | bytes 524288 | tf_op jit(solution)/shard_map/transpose | solution.py:305
Async XLA Ops:
  0.0 19.6 %copy-start = (bf16[3,3,3,256,256]{4,3,2,1,0:T(8,128)(2,1)S(1)}, bf16[3,3,3,256,256]{4,3,2,1,0:T(8,128)(2,1)}, u32[]{:S(2)}) copy-start(bf16[3,3,3,256,256]{4,3,2,1,0:T(8,128)(2,1)} %conv_weight.1) | copy-start | bytes 10616836
  19.5 2.2 %collective-permute-start = (bf16[10,16,768]{2,1,0:T(8,128)(2,1)S(1)}, bf16[10,16,768]{2,1,0:T(8,128)(2,1)S(1)}, u32[]{:S(2)}, u32[]{:S(2)}) collective-permute-start(bf16[10,16,768]{2,1,0:T(8,128)(2,1)S(1)} %shard_map.74), channel_id=1, source_target_pairs={{0,1},{1,0},{2,3},{3,2},{4,5},{5,4},{6,7},{7,6},{8,9},{9,8},{10,11... | collective-permute-start | bytes 737288 | tf_op jit(solution)/shard_map/ppermute | solution.py:275

commit v25 on v24

--- a/solution.py
+++ b/solution.py
@@ -48,8 +48,9 @@
     return lax.div(at, jnp.int32(by)), lax.rem(at, jnp.int32(by))
 
 
-def pack_kernel(group, video, *refs):
-    out, local, wide, sems = refs
+def pack_kernel(group, ids_far, video, out, ids, near_ids, local, wide, sems, ids_sem):
+    ids_copy = pltpu.make_async_copy(ids_far, near_ids, ids_sem)
+    ids_copy.start()
     count, rows, cols, chans = video.shape
     lines = count * rows
     stride = cols + 2 * EDGE
@@ -65,6 +66,9 @@
     for at in range(lines):
         fill(wide, at * stride, nothing)
         fill(wide, at * stride + EDGE + cols, nothing)
+    ids_copy.wait()
+    for s in range(ids.shape[0]):
+        ids[s : s + 1, :] = jnp.full((1, LANES), near_ids[s], jnp.int32)
     for at, copy in enumerate(copies):
         copy.wait()
         fill(wide, at * stride + EDGE, local[at // rows, at % rows].astype(f32))
@@ -121,7 +125,7 @@
         frame = source * count + inner
         block = jnp.zeros(at.shape, jnp.int32)
         for s in range(frames):
-            block = jnp.where(frame == s, ids[s], block)
+            block = jnp.where(frame == s, ids[s : s + 1, :area], block)
         return pixel, frame, block
 
     row_p, row_t, row_b = place_of(lax.broadcasted_iota(jnp.int32, (area, area), 0))
@@ -130,20 +134,16 @@
     bias[...] = jnp.where(permit, 0.0, -1e30)
 
 
-def shift_kernel(count, rows, video, ids_far, *refs):
-    conv_weight, far, (total, bias, *near) = refs[0], refs[1:5], refs[5:11]
-    vid, grid, ids, sems, ids_sem = refs[11:]
-    ids_copy = pltpu.make_async_copy(ids_far, ids, ids_sem)
-    ids_copy.start()
+def shift_kernel(count, rows, vid, ids, conv_weight, *refs):
+    far, (total, bias, *near), (grid, sems) = refs[:4], refs[4:10], refs[10:]
     others = [pltpu.make_async_copy(src, dst, sems.at[i]) for i, (src, dst) in enumerate(zip(far, near))]
     for copy in others:
         copy.start()
-    sources, step, chans = video.shape
-    span = step // (count * rows)
-    own = span - 2
-    frames = sources * count
+    own, _, frames, chans = total.shape
+    span = own + 2
+    sources = frames // count
+    step = span * count * rows
     half = own // 2 if own % 2 == 0 else own
-    fill(vid, 0, video[...].reshape(sources * step, chans).astype(f32))
     for w in range(span):
         for r in range(rows):
             now = frames_of(vid, w, r, count, rows, sources, step)
@@ -160,7 +160,6 @@
             part = jnp.dot(window, weight, preferred_element_type=f32)
             some = total.at[w : w + half, low:high]
             some[...] = some[...] + part.reshape(half, high - low, frames, chans)
-    ids_copy.wait()
     fill_bias(bias, ids, frames, count)
     for copy in others:
         copy.wait()
@@ -241,35 +240,42 @@
     in_far = functools.partial(pltpu.with_memory_space_constraint, memory_space=pltpu.HBM)
     weights = [in_far(x) for x in (w_query, w_key, w_value, w_output)]
 
-    blocks = pl.pallas_call(
+    sources = group * (2 if outer > 1 else 1)
+    frames = sources * count
+    ids = block_ids
+    if outer > 1:
+        ids = jnp.concatenate([jnp.full((group * count,), -2, jnp.int32), ids])
+        ids = lax.dynamic_slice(ids, (lax.axis_index("outer") * group * count,), (frames,))
+    blocks, ids = pl.pallas_call(
         functools.partial(pack_kernel, group),
-        out_shape=jax.ShapeDtypeStruct((group, span * lines, chans), bf16),
-        in_specs=[far],
-        out_specs=near,
+        out_shape=[
+            jax.ShapeDtypeStruct((group, span * lines, chans), bf16),
+            jax.ShapeDtypeStruct((frames, LANES), jnp.int32),
+        ],
+        in_specs=[far, far],
+        out_specs=[near, near],
         scratch_shapes=[
+            pltpu.SMEM((frames,), jnp.int32),
             pltpu.VMEM(video.shape, bf16),
             scratch(lines * (cols + 2 * EDGE), chans),
             pltpu.SemaphoreType.DMA((lines,)),
+            pltpu.SemaphoreType.DMA(()),
         ],
         compiler_params=params,
         cost_estimate=pl.CostEstimate(flops=2000000000, transcendentals=0, bytes_accessed=1000000),
-    )(in_far(video))
+    )(in_far(ids), in_far(video))
     piece = exchanged(blocks)
-    ids = block_ids
     if outer > 1:
         before = lax.ppermute(piece, "outer", [(i, i + 1) for i in range(outer - 1)])
         piece = jnp.concatenate([before, piece], axis=0)
-        ids = jnp.concatenate([jnp.full((group * count,), -2, jnp.int32), ids])
-        ids = lax.dynamic_slice(ids, (lax.axis_index("outer") * group * count,), (2 * group * count,))
-    sources = piece.shape[0]
-    frames = sources * count
-    stored = scratch(sources * span * lines, chans)
-    edge = pl.pallas_call(
+    edge, wide = pl.pallas_call(
         functools.partial(edge_kernel, count, rows),
-        out_shape=jax.ShapeDtypeStruct((span, frames, TAPS * chans), bf16),
+        out_shape=[
+            jax.ShapeDtypeStruct((span, frames, TAPS * chans), bf16),
+            jax.ShapeDtypeStruct((chans // LANES, sources * span * lines, LANES), f32),
+        ],
         in_specs=[near],
-        out_specs=near,
-        scratch_shapes=[stored],
+        out_specs=[near, near],
         compiler_params=params,
     )(piece)
     edge = lax.ppermute(edge, "height", [(0, 1), (1, 0)])
@@ -282,17 +288,14 @@
             jax.ShapeDtypeStruct((area, area), f32),
         ]
         + [jax.ShapeDtypeStruct(x.shape, bf16) for x in weights],
-        in_specs=[near, far, near] + [far] * 4,
+        in_specs=[near] * 3 + [far] * 4,
         out_specs=[near] * 6,
         scratch_shapes=[
-            stored,
             pltpu.VMEM((span, rows, frames, TAPS * chans), bf16),
-            pltpu.SMEM((frames,), jnp.int32),
             pltpu.SemaphoreType.DMA((4,)),
-            pltpu.SemaphoreType.DMA(()),
         ],
         compiler_params=params,
-    )(piece, in_far(ids), conv_weight, *weights)
+    )(wide, ids, conv_weight, *weights)
     blocks = pl.pallas_call(
         functools.partial(main_kernel, count, rows, group),
         out_shape=jax.ShapeDtypeStruct((group, own * lines, chans), bf16),

time: 37.1 us -> 37.1 us (level)
  no operation moved by 1% of the time
where the time goes in v25:
time: 37.1 us; the launch traced here: 36.9 us
  blocking collectives  30.3 us (82%)
  Pallas kernels  5.77 us (16%)
  local copies, waits for them, and re-layouts  0.72 us (2%)
    all_to_all x2, blocking collectives, exchanged(): return lax.all_to_all(blocks, 'tm', split_axis=0, concat_axis=0, tiled=True)  30.3 us
    pallas_call x1, Pallas kernels, per_device(): pl.pallas_call(functools.partial(shift_kernel, count, rows), out_shape=[j...  2.16 us
    pallas_call x1, Pallas kernels, per_device(): pl.pallas_call(functools.partial(main_kernel, count, rows, group), out_sh...  2.09 us
    pallas_call x1, Pallas kernels, per_device(): pl.pallas_call(functools.partial(pack_kernel, group), out_shape=[jax.Shap...  1.26 us
  transfers between devices with their start and end apart: 1, of which 0 were waited for; matrix products, arithmetic and copies ran while one was open for 0% of the time, Pallas kernels for 6%

profile of v25, /device:TPU:0, one launch (start us, length us, event | category | flops | bytes accessed | tf_op | source)
XLA Modules:
  0.0 36.9 jit_solution(5816416669930785240)
XLA Ops:
  0.0 0.0 copy-start
  0.0 1.3 %shard_map.73 = (bf16[8,80,256]{2,1,0:T(8,128)(2,1)S(1)}, s32[16,128]{1,0:T(8,128)S(1)}) custom-call(s32[16]{0:T(128)} %ids_far.1, bf16[2,4,64,256]{3,2,1,0:T(8,128)(2,1)} %video.1), custom_call_target="tpu_custom_call" | custom-call | flops 2000000000 | bytes 1000000 | tf_op jit(solution)/shard_map/pallas_call | solution.py:249
  1.3 18.0 %all_to_all.10.video = bf16[8,80,256]{2,1,0:T(8,128)(2,1)S(1)} all-to-all(bf16[8,80,256]{2,1,0:T(8,128)(2,1)S(1)} %get-tuple-element.15), channel_id=1, replica_groups=mesh['groups'=2,'tm'=8,'height'=2] {'tm'}, dimensions={0} | all-to-all | bytes 655360 | tf_op jit(solution)/shard_map/all_to_all | solution.py:228
  19.2 0.3 shard_map.74
  19.5 0.1 collective-permute-start
  19.6 0.0 copy-done
  19.6 2.2 %shard_map.75 = (f32[8,4,16,256]{3,2,1,0:T(8,128)S(1)}, f32[128,128]{1,0:T(8,128)S(1)}, bf16[256,256]{1,0:T(8,128)(2,1)S(1)}, bf16[256,256]{1,0:T(8,128)(2,1)S(1...) custom-call(f32[2,640,128]{2,1,0:T(8,128)S(1)} %get-tuple-element.17.vid, ...), custom_call_target="tpu_custom_call" | custom-call | tf_op jit(solution)/shard_map/pallas_call | solution.py:284
  21.7 0.0 collective-permute-done.edge
  21.8 2.1 %shard_map.76 = bf16[8,64,256]{2,1,0:T(8,128)(2,1)S(1)} custom-call(bf16[10,16,768]{2,1,0:T(8,128)(2,1)S(1)} %collective-permute-done.edge, f32[8,4,16,256]{3,2,1,0:T(8,128)S(1)} %get-tuple-element.19.given, f32[128,128]{1,0:T(8,128)S(1)} %get-tuple-element.20.bias, bf16[3,3,3,256,256]{4,3,2,1,0:T(8,128)(2,1)S(1)} %copy-done, ...), custom_call_target="tpu_custom_call" | custom-call | tf_op jit(solution)/shard_map/pallas_call | solution.py:299
  23.9 12.4 %all_to_all.11 = bf16[8,64,256]{2,1,0:T(8,128)(2,1)S(1)} all-to-all(bf16[8,64,256]{2,1,0:T(8,128)(2,1)S(1)} %shard_map.76), channel_id=1, replica_groups=mesh['groups'=2,'tm'=8,'height'=2] {'tm'}, dimensions={0} | all-to-all | bytes 524288 | tf_op jit(solution)/shard_map/all_to_all | solution.py:228
  36.2 0.7 %copy.8 = bf16[8,8,8,256]{3,2,1,0:T(8,128)(2,1)} copy(bf16[8,8,8,256]{3,2,0,1:T(8,128)(2,1)S(1)} %bitcast.4) | data formatting | bytes 524288 | tf_op jit(solution)/shard_map/transpose | solution.py:308
Async XLA Ops:
  0.0 19.6 %copy-start = (bf16[3,3,3,256,256]{4,3,2,1,0:T(8,128)(2,1)S(1)}, bf16[3,3,3,256,256]{4,3,2,1,0:T(8,128)(2,1)}, u32[]{:S(2)}) copy-start(bf16[3,3,3,256,256]{4,3,2,1,0:T(8,128)(2,1)} %conv_weight.3) | copy-start | bytes 10616836
  19.5 2.3 %collective-permute-start = (bf16[10,16,768]{2,1,0:T(8,128)(2,1)S(1)}, bf16[10,16,768]{2,1,0:T(8,128)(2,1)S(1)}, u32[]{:S(2)}, u32[]{:S(2)}) collective-permute-start(bf16[10,16,768]{2,1,0:T(8,128)(2,1)S(1)} %get-tuple-element.16), channel_id=1, source_target_pairs={{0,1},{1,0},{2,3},{3,2},{4,5},{5,4},{6,7},{7,6},{8,9},{9,8},{10,11... | collective-permute-start | bytes 737288 | tf_op jit(solution)/shard_map/ppermute | solution.py:281

commit v26 on v24

--- a/solution.py
+++ b/solution.py
@@ -195,9 +195,9 @@
         lines_of.append(row[:, None])
     hidden = jnp.concatenate(lines_of, axis=1).reshape(own * rows * frames, chans).astype(bf16).astype(f32)
     normed = rms(hidden).astype(bf16)
-    query, keys, values = (
-        jnp.dot(normed, weight[...], preferred_element_type=f32).astype(bf16) for weight in (w_query, w_key, w_value)
-    )
+    weight = jnp.concatenate([w_query[...], w_key[...], w_value[...]], axis=1)
+    projected = jnp.dot(normed, weight, preferred_element_type=f32).astype(bf16)
+    query, keys, values = (projected[:, i * chans : (i + 1) * chans] for i in range(3))
     gone = []
     for at in range(0, own * rows * frames, area):
         attended = []

time: 37.1 us -> 37.1 us (level)
  no operation moved by 1% of the time
where the time goes in v26:
time: 37.1 us; the launch traced here: 36.9 us
  blocking collectives  30.3 us (82%)
  Pallas kernels  5.7 us (15%)
  local copies, waits for them, and re-layouts  0.72 us (2%)
    all_to_all x2, blocking collectives, exchanged(): return lax.all_to_all(blocks, 'tm', split_axis=0, concat_axis=0, tiled=True)  30.3 us
    pallas_call x1, Pallas kernels, per_device(): pl.pallas_call(functools.partial(shift_kernel, count, rows), out_shape=[j...  2.1 us
    pallas_call x1, Pallas kernels, per_device(): pl.pallas_call(functools.partial(main_kernel, count, rows, group), out_sh...  2.09 us
    pallas_call x1, Pallas kernels, per_device(): pl.pallas_call(functools.partial(pack_kernel, group), out_shape=jax.Shape...  1.25 us
  transfers between devices with their start and end apart: 1, of which 0 were waited for; matrix products, arithmetic and copies ran while one was open for 0% of the time, Pallas kernels for 6%

profile of v26, /device:TPU:0, one launch (start us, length us, event | category | flops | bytes accessed | tf_op | source)
XLA Modules:
  0.0 36.9 jit_solution(17704266095243427418)
XLA Ops:
  0.0 0.0 copy-start
  0.0 1.3 %shard_map.73 = bf16[8,80,256]{2,1,0:T(8,128)(2,1)S(1)} custom-call(bf16[2,4,64,256]{3,2,1,0:T(8,128)(2,1)} %video.1), custom_call_target="tpu_custom_call" | custom-call | flops 2000000000 | bytes 1000000 | tf_op jit(solution)/shard_map/pallas_call | solution.py:244
  1.3 18.0 %all_to_all.10.video = bf16[8,80,256]{2,1,0:T(8,128)(2,1)S(1)} all-to-all(bf16[8,80,256]{2,1,0:T(8,128)(2,1)S(1)} %shard_map.73), channel_id=1, replica_groups=mesh['groups'=2,'tm'=8,'height'=2] {'tm'}, dimensions={0} | all-to-all | bytes 655360 | tf_op jit(solution)/shard_map/all_to_all | solution.py:229
  19.2 0.3 shard_map.74
  19.5 0.1 collective-permute-start
  19.6 0.0 copy-done
  19.6 2.1 %shard_map.75 = (f32[8,4,16,256]{3,2,1,0:T(8,128)S(1)}, f32[128,128]{1,0:T(8,128)S(1)}, bf16[256,256]{1,0:T(8,128)(2,1)S(1)}, bf16[256,256]{1,0:T(8,128)(2,1)S(1...) custom-call(bf16[8,80,256]{2,1,0:T(8,128)(2,1)S(1)} %all_to_all.10.video, s32[16]{0:T(128)} %ids_far.1, ...), custom_call_target="tpu_custom_call" | custom-call | tf_op jit(solution)/shard_map/pallas_call | solution.py:278
  21.7 0.0 collective-permute-done.edge
  21.7 2.1 %shard_map.76 = bf16[8,64,256]{2,1,0:T(8,128)(2,1)S(1)} custom-call(bf16[10,16,768]{2,1,0:T(8,128)(2,1)S(1)} %collective-permute-done.edge, f32[8,4,16,256]{3,2,1,0:T(8,128)S(1)} %get-tuple-element.11.given, f32[128,128]{1,0:T(8,128)S(1)} %get-tuple-element.12.bias, bf16[3,3,3,256,256]{4,3,2,1,0:T(8,128)(2,1)S(1)} %copy-done, ...), custom_call_target="tpu_custom_call" | custom-call | tf_op jit(solution)/shard_map/pallas_call | solution.py:296
  23.8 12.4 %all_to_all.11 = bf16[8,64,256]{2,1,0:T(8,128)(2,1)S(1)} all-to-all(bf16[8,64,256]{2,1,0:T(8,128)(2,1)S(1)} %shard_map.76), channel_id=1, replica_groups=mesh['groups'=2,'tm'=8,'height'=2] {'tm'}, dimensions={0} | all-to-all | bytes 524288 | tf_op jit(solution)/shard_map/all_to_all | solution.py:229
  36.1 0.7 %copy.8 = bf16[8,8,8,256]{3,2,1,0:T(8,128)(2,1)} copy(bf16[8,8,8,256]{3,2,0,1:T(8,128)(2,1)S(1)} %bitcast.4) | data formatting | bytes 524288 | tf_op jit(solution)/shard_map/transpose | solution.py:305
Async XLA Ops:
  0.0 19.6 %copy-start = (bf16[3,3,3,256,256]{4,3,2,1,0:T(8,128)(2,1)S(1)}, bf16[3,3,3,256,256]{4,3,2,1,0:T(8,128)(2,1)}, u32[]{:S(2)}) copy-start(bf16[3,3,3,256,256]{4,3,2,1,0:T(8,128)(2,1)} %conv_weight.1) | copy-start | bytes 10616836
  19.5 2.2 %collective-permute-start = (bf16[10,16,768]{2,1,0:T(8,128)(2,1)S(1)}, bf16[10,16,768]{2,1,0:T(8,128)(2,1)S(1)}, u32[]{:S(2)}, u32[]{:S(2)}) collective-permute-start(bf16[10,16,768]{2,1,0:T(8,128)(2,1)S(1)} %shard_map.74), channel_id=1, source_target_pairs={{0,1},{1,0},{2,3},{3,2},{4,5},{5,4},{6,7},{7,6},{8,9},{9,8},{10,11... | collective-permute-start | bytes 737288 | tf_op jit(solution)/shard_map/ppermute | solution.py:275

commit v27 on v26

--- a/solution.py
+++ b/solution.py
@@ -106,9 +106,10 @@
     sources, step, chans = video.shape
     span = step // (count * rows)
     fill(vid, 0, video[...].reshape(sources * step, chans).astype(f32))
-    row = (rows - 1) * (1 - lax.axis_index("height"))
+    lower = lax.axis_index("height") == 1
     for w in range(span):
-        edge[w] = shifted([activated(x) for x in frames_of(vid, w, row, count, rows, sources, step)])
+        first, last = (frames_of(vid, w, r, count, rows, sources, step) for r in (0, rows - 1))
+        edge[w] = shifted([activated(jnp.where(lower, x, y)) for x, y in zip(first, last)])
 
 
 def fill_bias(bias, ids, frames, count):

time: 37.1 us -> 37 us (level)
  no operation moved by 1% of the time
where the time goes in v27:
time: 37 us; the launch traced here: 36.8 us
  blocking collectives  30.3 us (82%)
  Pallas kernels  5.67 us (15%)
  local copies, waits for them, and re-layouts  0.72 us (2%)
    all_to_all x2, blocking collectives, exchanged(): return lax.all_to_all(blocks, 'tm', split_axis=0, concat_axis=0, tiled=True)  30.3 us
    pallas_call x1, Pallas kernels, per_device(): pl.pallas_call(functools.partial(shift_kernel, count, rows), out_shape=[j...  2.1 us
    pallas_call x1, Pallas kernels, per_device(): pl.pallas_call(functools.partial(main_kernel, count, rows, group), out_sh...  2.09 us
    pallas_call x1, Pallas kernels, per_device(): pl.pallas_call(functools.partial(pack_kernel, group), out_shape=jax.Shape...  1.25 us
  transfers between devices with their start and end apart: 1, of which 0 were waited for; matrix products, arithmetic and copies ran while one was open for 0% of the time, Pallas kernels for 6%

profile of v27, /device:TPU:0, one launch (start us, length us, event | category | flops | bytes accessed | tf_op | source)
XLA Modules:
  0.0 36.8 jit_solution(15765939387614869063)
XLA Ops:
  0.0 0.0 copy-start
  0.0 1.3 %shard_map.73 = bf16[8,80,256]{2,1,0:T(8,128)(2,1)S(1)} custom-call(bf16[2,4,64,256]{3,2,1,0:T(8,128)(2,1)} %video.1), custom_call_target="tpu_custom_call" | custom-call | flops 2000000000 | bytes 1000000 | tf_op jit(solution)/shard_map/pallas_call | solution.py:245
  1.3 18.0 %all_to_all.10.video = bf16[8,80,256]{2,1,0:T(8,128)(2,1)S(1)} all-to-all(bf16[8,80,256]{2,1,0:T(8,128)(2,1)S(1)} %shard_map.73), channel_id=1, replica_groups=mesh['groups'=2,'tm'=8,'height'=2] {'tm'}, dimensions={0} | all-to-all | bytes 655360 | tf_op jit(solution)/shard_map/all_to_all | solution.py:230
  19.2 0.2 shard_map.74
  19.5 0.1 collective-permute-start
  19.5 0.0 copy-done
  19.5 2.1 %shard_map.75 = (f32[8,4,16,256]{3,2,1,0:T(8,128)S(1)}, f32[128,128]{1,0:T(8,128)S(1)}, bf16[256,256]{1,0:T(8,128)(2,1)S(1)}, bf16[256,256]{1,0:T(8,128)(2,1)S(1...) custom-call(bf16[8,80,256]{2,1,0:T(8,128)(2,1)S(1)} %all_to_all.10.video, s32[16]{0:T(128)} %ids_far.1, ...), custom_call_target="tpu_custom_call" | custom-call | tf_op jit(solution)/shard_map/pallas_call | solution.py:279
  21.7 0.0 collective-permute-done.edge
  21.7 2.1 %shard_map.76 = bf16[8,64,256]{2,1,0:T(8,128)(2,1)S(1)} custom-call(bf16[10,16,768]{2,1,0:T(8,128)(2,1)S(1)} %collective-permute-done.edge, f32[8,4,16,256]{3,2,1,0:T(8,128)S(1)} %get-tuple-element.11.given, f32[128,128]{1,0:T(8,128)S(1)} %get-tuple-element.12.bias, bf16[3,3,3,256,256]{4,3,2,1,0:T(8,128)(2,1)S(1)} %copy-done, ...), custom_call_target="tpu_custom_call" | custom-call | tf_op jit(solution)/shard_map/pallas_call | solution.py:297
  23.8 12.4 %all_to_all.11 = bf16[8,64,256]{2,1,0:T(8,128)(2,1)S(1)} all-to-all(bf16[8,64,256]{2,1,0:T(8,128)(2,1)S(1)} %shard_map.76), channel_id=1, replica_groups=mesh['groups'=2,'tm'=8,'height'=2] {'tm'}, dimensions={0} | all-to-all | bytes 524288 | tf_op jit(solution)/shard_map/all_to_all | solution.py:230
  36.1 0.7 %copy.8 = bf16[8,8,8,256]{3,2,1,0:T(8,128)(2,1)} copy(bf16[8,8,8,256]{3,2,0,1:T(8,128)(2,1)S(1)} %bitcast.4) | data formatting | bytes 524288 | tf_op jit(solution)/shard_map/transpose | solution.py:306
Async XLA Ops:
  0.0 19.5 %copy-start = (bf16[3,3,3,256,256]{4,3,2,1,0:T(8,128)(2,1)S(1)}, bf16[3,3,3,256,256]{4,3,2,1,0:T(8,128)(2,1)}, u32[]{:S(2)}) copy-start(bf16[3,3,3,256,256]{4,3,2,1,0:T(8,128)(2,1)} %conv_weight.1) | copy-start | bytes 10616836
  19.5 2.2 %collective-permute-start = (bf16[10,16,768]{2,1,0:T(8,128)(2,1)S(1)}, bf16[10,16,768]{2,1,0:T(8,128)(2,1)S(1)}, u32[]{:S(2)}, u32[]{:S(2)}) collective-permute-start(bf16[10,16,768]{2,1,0:T(8,128)(2,1)S(1)} %shard_map.74), channel_id=1, source_target_pairs={{0,1},{1,0},{2,3},{3,2},{4,5},{5,4},{6,7},{7,6},{8,9},{9,8},{10,11... | collective-permute-start | bytes 737288 | tf_op jit(solution)/shard_map/ppermute | solution.py:276

commit v28 on v27

--- a/solution.py
+++ b/solution.py
@@ -149,10 +149,8 @@
         for r in range(rows):
             now = frames_of(vid, w, r, count, rows, sources, step)
             grid[w, r] = shifted([activated(x) for x in now])
-            if 1 <= w <= own:
-                total[w - 1, r] = jnp.concatenate(now, 0)
-
-    for b in range(TAPS):
+
+    for b in (1, 0, 2):
         low, high = max(0, 1 - b), min(rows, rows + 1 - b)
         weight = jnp.concatenate([conv_weight[a, b, e] for e in range(TAPS) for a in range(TAPS)], axis=0)
         for w in range(0, own, half):
@@ -160,7 +158,14 @@
             window = window.reshape(half * (high - low) * frames, TAPS * TAPS * chans)
             part = jnp.dot(window, weight, preferred_element_type=f32)
             some = total.at[w : w + half, low:high]
-            some[...] = some[...] + part.reshape(half, high - low, frames, chans)
+            part = part.reshape(half, high - low, frames, chans)
+            if b == 1:
+                for i in range(half):
+                    for r in range(rows):
+                        now = frames_of(vid, w + i + 1, r, count, rows, sources, step)
+                        total[w + i, r] = jnp.concatenate(now, 0) + part[i, r]
+            else:
+                some[...] = some[...] + part
     ids_copy.wait()
     fill_bias(bias, ids, frames, count)
     for copy in others:

time: 37 us -> 37.2 us (level)
  no operation moved by 1% of the time
where the time goes in v28:
time: 37.2 us; the launch traced here: 37 us
  blocking collectives  30.3 us (81%)
  Pallas kernels  5.78 us (16%)
  local copies, waits for them, and re-layouts  0.72 us (2%)
    all_to_all x2, blocking collectives, exchanged(): return lax.all_to_all(blocks, 'tm', split_axis=0, concat_axis=0, tiled=True)  30.3 us
    pallas_call x1, Pallas kernels, per_device(): pl.pallas_call(functools.partial(shift_kernel, count, rows), out_shape=[j...  2.22 us
    pallas_call x1, Pallas kernels, per_device(): pl.pallas_call(functools.partial(main_kernel, count, rows, group), out_sh...  2.09 us
    pallas_call x1, Pallas kernels, per_device(): pl.pallas_call(functools.partial(pack_kernel, group), out_shape=jax.Shape...  1.25 us
  transfers between devices with their start and end apart: 1, of which 0 were waited for; matrix products, arithmetic and copies ran while one was open for 0% of the time, Pallas kernels for 6%

profile of v28, /device:TPU:0, one launch (start us, length us, event | category | flops | bytes accessed | tf_op | source)
XLA Modules:
  0.0 37.0 jit_solution(11557088540723468058)
XLA Ops:
  0.0 0.0 copy-start
  0.0 1.3 %shard_map.73 = bf16[8,80,256]{2,1,0:T(8,128)(2,1)S(1)} custom-call(bf16[2,4,64,256]{3,2,1,0:T(8,128)(2,1)} %video.1), custom_call_target="tpu_custom_call" | custom-call | flops 2000000000 | bytes 1000000 | tf_op jit(solution)/shard_map/pallas_call | solution.py:250
  1.3 18.0 %all_to_all.10.video = bf16[8,80,256]{2,1,0:T(8,128)(2,1)S(1)} all-to-all(bf16[8,80,256]{2,1,0:T(8,128)(2,1)S(1)} %shard_map.73), channel_id=1, replica_groups=mesh['groups'=2,'tm'=8,'height'=2] {'tm'}, dimensions={0} | all-to-all | bytes 655360 | tf_op jit(solution)/shard_map/all_to_all | solution.py:235
  19.2 0.2 shard_map.74
  19.5 0.1 collective-permute-start
  19.5 0.0 copy-done
  19.5 2.2 %shard_map.75 = (f32[8,4,16,256]{3,2,1,0:T(8,128)S(1)}, f32[128,128]{1,0:T(8,128)S(1)}, bf16[256,256]{1,0:T(8,128)(2,1)S(1)}, bf16[256,256]{1,0:T(8,128)(2,1)S(1...) custom-call(bf16[8,80,256]{2,1,0:T(8,128)(2,1)S(1)} %all_to_all.10.video, s32[16]{0:T(128)} %ids_far.1, ...), custom_call_target="tpu_custom_call" | custom-call | tf_op jit(solution)/shard_map/pallas_call | solution.py:284
  21.8 0.0 collective-permute-done.edge
  21.8 2.1 %shard_map.76 = bf16[8,64,256]{2,1,0:T(8,128)(2,1)S(1)} custom-call(bf16[10,16,768]{2,1,0:T(8,128)(2,1)S(1)} %collective-permute-done.edge, f32[8,4,16,256]{3,2,1,0:T(8,128)S(1)} %get-tuple-element.11.given, f32[128,128]{1,0:T(8,128)S(1)} %get-tuple-element.12.bias, bf16[3,3,3,256,256]{4,3,2,1,0:T(8,128)(2,1)S(1)} %copy-done, ...), custom_call_target="tpu_custom_call" | custom-call | tf_op jit(solution)/shard_map/pallas_call | solution.py:302
  23.9 12.4 %all_to_all.11 = bf16[8,64,256]{2,1,0:T(8,128)(2,1)S(1)} all-to-all(bf16[8,64,256]{2,1,0:T(8,128)(2,1)S(1)} %shard_map.76), channel_id=1, replica_groups=mesh['groups'=2,'tm'=8,'height'=2] {'tm'}, dimensions={0} | all-to-all | bytes 524288 | tf_op jit(solution)/shard_map/all_to_all | solution.py:235
  36.2 0.7 %copy.8 = bf16[8,8,8,256]{3,2,1,0:T(8,128)(2,1)} copy(bf16[8,8,8,256]{3,2,0,1:T(8,128)(2,1)S(1)} %bitcast.4) | data formatting | bytes 524288 | tf_op jit(solution)/shard_map/transpose | solution.py:311
Async XLA Ops:
  0.0 19.5 %copy-start = (bf16[3,3,3,256,256]{4,3,2,1,0:T(8,128)(2,1)S(1)}, bf16[3,3,3,256,256]{4,3,2,1,0:T(8,128)(2,1)}, u32[]{:S(2)}) copy-start(bf16[3,3,3,256,256]{4,3,2,1,0:T(8,128)(2,1)} %conv_weight.1) | copy-start | bytes 10616836
  19.5 2.3 %collective-permute-start = (bf16[10,16,768]{2,1,0:T(8,128)(2,1)S(1)}, bf16[10,16,768]{2,1,0:T(8,128)(2,1)S(1)}, u32[]{:S(2)}, u32[]{:S(2)}) collective-permute-start(bf16[10,16,768]{2,1,0:T(8,128)(2,1)S(1)} %shard_map.74), channel_id=1, source_target_pairs={{0,1},{1,0},{2,3},{3,2},{4,5},{5,4},{6,7},{7,6},{8,9},{9,8},{10,11... | collective-permute-start | bytes 737288 | tf_op jit(solution)/shard_map/ppermute | solution.py:281

commit v29 on v27

--- a/solution.py
+++ b/solution.py
@@ -56,8 +56,8 @@
     own = cols // group
     span = own + 2
     copies = []
-    for at in range(lines):
-        place = (at // rows, at % rows)
+    for at in range(2 * lines):
+        place = (at // 2 // rows, at // 2 % rows, pl.ds(at % 2 * (cols // 2), cols // 2))
         copy = pltpu.make_async_copy(video.at[place], local.at[place], sems.at[at])
         copy.start()
         copies.append(copy)
@@ -65,8 +65,9 @@
     for at in range(lines):
         fill(wide, at * stride, nothing)
         fill(wide, at * stride + EDGE + cols, nothing)
-    for at, copy in enumerate(copies):
-        copy.wait()
+    for at in range(lines):
+        copies[2 * at].wait()
+        copies[2 * at + 1].wait()
         fill(wide, at * stride + EDGE, local[at // rows, at % rows].astype(f32))
     together = 16 // lines
     for k in range(group):
@@ -250,7 +251,7 @@
         scratch_shapes=[
             pltpu.VMEM(video.shape, bf16),
             scratch(lines * (cols + 2 * EDGE), chans),
-            pltpu.SemaphoreType.DMA((lines,)),
+            pltpu.SemaphoreType.DMA((2 * lines,)),
         ],
         compiler_params=params,
         cost_estimate=pl.CostEstimate(flops=2000000000, transcendentals=0, bytes_accessed=1000000),

time: 37 us -> 37.2 us (level)
  no operation moved by 1% of the time
where the time goes in v29:
time: 37.2 us; the launch traced here: 36.9 us
  blocking collectives  30.3 us (81%)
  Pallas kernels  5.74 us (15%)
  local copies, waits for them, and re-layouts  0.72 us (2%)
    all_to_all x2, blocking collectives, exchanged(): return lax.all_to_all(blocks, 'tm', split_axis=0, concat_axis=0, tiled=True)  30.3 us
    pallas_call x1, Pallas kernels, per_device(): pl.pallas_call(functools.partial(shift_kernel, count, rows), out_shape=[j...  2.1 us
    pallas_call x1, Pallas kernels, per_device(): pl.pallas_call(functools.partial(main_kernel, count, rows, group), out_sh...  2.09 us
    pallas_call x1, Pallas kernels, per_device(): pl.pallas_call(functools.partial(pack_kernel, group), out_shape=jax.Shape...  1.32 us
  transfers between devices with their start and end apart: 1, of which 0 were waited for; matrix products, arithmetic and copies ran while one was open for 0% of the time, Pallas kernels for 6%

profile of v29, /device:TPU:0, one launch (start us, length us, event | category | flops | bytes accessed | tf_op | source)
XLA Modules:
  0.0 36.9 jit_solution(1637264381592914083)
XLA Ops:
  0.0 0.0 copy-start
  0.0 1.3 %shard_map.73 = bf16[8,80,256]{2,1,0:T(8,128)(2,1)S(1)} custom-call(bf16[2,4,64,256]{3,2,1,0:T(8,128)(2,1)} %video.1), custom_call_target="tpu_custom_call" | custom-call | flops 2000000000 | bytes 1000000 | tf_op jit(solution)/shard_map/pallas_call | solution.py:246
  1.3 18.0 %all_to_all.10.video = bf16[8,80,256]{2,1,0:T(8,128)(2,1)S(1)} all-to-all(bf16[8,80,256]{2,1,0:T(8,128)(2,1)S(1)} %shard_map.73), channel_id=1, replica_groups=mesh['groups'=2,'tm'=8,'height'=2] {'tm'}, dimensions={0} | all-to-all | bytes 655360 | tf_op jit(solution)/shard_map/all_to_all | solution.py:231
  19.3 0.2 shard_map.74
  19.5 0.1 collective-permute-start
  19.6 0.0 copy-done
  19.6 2.1 %shard_map.75 = (f32[8,4,16,256]{3,2,1,0:T(8,128)S(1)}, f32[128,128]{1,0:T(8,128)S(1)}, bf16[256,256]{1,0:T(8,128)(2,1)S(1)}, bf16[256,256]{1,0:T(8,128)(2,1)S(1...) custom-call(bf16[8,80,256]{2,1,0:T(8,128)(2,1)S(1)} %all_to_all.10.video, s32[16]{0:T(128)} %ids_far.1, ...), custom_call_target="tpu_custom_call" | custom-call | tf_op jit(solution)/shard_map/pallas_call | solution.py:280
  21.7 0.0 collective-permute-done.edge
  21.7 2.1 %shard_map.76 = bf16[8,64,256]{2,1,0:T(8,128)(2,1)S(1)} custom-call(bf16[10,16,768]{2,1,0:T(8,128)(2,1)S(1)} %collective-permute-done.edge, f32[8,4,16,256]{3,2,1,0:T(8,128)S(1)} %get-tuple-element.11.given, f32[128,128]{1,0:T(8,128)S(1)} %get-tuple-element.12.bias, bf16[3,3,3,256,256]{4,3,2,1,0:T(8,128)(2,1)S(1)} %copy-done, ...), custom_call_target="tpu_custom_call" | custom-call | tf_op jit(solution)/shard_map/pallas_call | solution.py:298
  23.8 12.4 %all_to_all.11 = bf16[8,64,256]{2,1,0:T(8,128)(2,1)S(1)} all-to-all(bf16[8,64,256]{2,1,0:T(8,128)(2,1)S(1)} %shard_map.76), channel_id=1, replica_groups=mesh['groups'=2,'tm'=8,'height'=2] {'tm'}, dimensions={0} | all-to-all | bytes 524288 | tf_op jit(solution)/shard_map/all_to_all | solution.py:231
  36.2 0.7 %copy.8 = bf16[8,8,8,256]{3,2,1,0:T(8,128)(2,1)} copy(bf16[8,8,8,256]{3,2,0,1:T(8,128)(2,1)S(1)} %bitcast.4) | data formatting | bytes 524288 | tf_op jit(solution)/shard_map/transpose | solution.py:307
Async XLA Ops:
  0.0 19.6 %copy-start = (bf16[3,3,3,256,256]{4,3,2,1,0:T(8,128)(2,1)S(1)}, bf16[3,3,3,256,256]{4,3,2,1,0:T(8,128)(2,1)}, u32[]{:S(2)}) copy-start(bf16[3,3,3,256,256]{4,3,2,1,0:T(8,128)(2,1)} %conv_weight.1) | copy-start | bytes 10616836
  19.5 2.2 %collective-permute-start = (bf16[10,16,768]{2,1,0:T(8,128)(2,1)S(1)}, bf16[10,16,768]{2,1,0:T(8,128)(2,1)S(1)}, u32[]{:S(2)}, u32[]{:S(2)}) collective-permute-start(bf16[10,16,768]{2,1,0:T(8,128)(2,1)S(1)} %shard_map.74), channel_id=1, source_target_pairs={{0,1},{1,0},{2,3},{3,2},{4,5},{5,4},{6,7},{7,6},{8,9},{9,8},{10,11... | collective-permute-start | bytes 737288 | tf_op jit(solution)/shard_map/ppermute | solution.py:277

commit v30 on v27

--- a/solution.py
+++ b/solution.py
@@ -192,7 +192,9 @@
 
     lines_of = []
     for r in range(rows):
-        row = given[:, r] + jnp.where(r == (rows - 1) * (1 - lower), part, 0.0)
+        row = given[:, r]
+        if r in (0, rows - 1):
+            row = row + jnp.where(r == (rows - 1) * (1 - lower), part, 0.0)
         lines_of.append(row[:, None])
     hidden = jnp.concatenate(lines_of, axis=1).reshape(own * rows * frames, chans).astype(bf16).astype(f32)
     normed = rms(hidden).astype(bf16)

time: 37 us -> 37 us (level)
  no operation moved by 1% of the time
where the time goes in v30:
time: 37 us; the launch traced here: 36.8 us
  blocking collectives  30.3 us (82%)
  Pallas kernels  5.65 us (15%)
  local copies, waits for them, and re-layouts  0.72 us (2%)
    all_to_all x2, blocking collectives, exchanged(): return lax.all_to_all(blocks, 'tm', split_axis=0, concat_axis=0, tiled=True)  30.3 us
    pallas_call x1, Pallas kernels, per_device(): pl.pallas_call(functools.partial(shift_kernel, count, rows), out_shape=[j...  2.1 us
    pallas_call x1, Pallas kernels, per_device(): pl.pallas_call(functools.partial(main_kernel, count, rows, group), out_sh...  2.08 us
    pallas_call x1, Pallas kernels, per_device(): pl.pallas_call(functools.partial(pack_kernel, group), out_shape=jax.Shape...  1.25 us
  transfers between devices with their start and end apart: 1, of which 0 were waited for; matrix products, arithmetic and copies ran while one was open for 0% of the time, Pallas kernels for 6%

profile of v30, /device:TPU:0, one launch (start us, length us, event | category | flops | bytes accessed | tf_op | source)
XLA Modules:
  0.0 36.8 jit_solution(5892422396564910224)
XLA Ops:
  0.0 0.0 copy-start
  0.0 1.3 %shard_map.73 = bf16[8,80,256]{2,1,0:T(8,128)(2,1)S(1)} custom-call(bf16[2,4,64,256]{3,2,1,0:T(8,128)(2,1)} %video.1), custom_call_target="tpu_custom_call" | custom-call | flops 2000000000 | bytes 1000000 | tf_op jit(solution)/shard_map/pallas_call | solution.py:247
  1.3 18.0 %all_to_all.10.video = bf16[8,80,256]{2,1,0:T(8,128)(2,1)S(1)} all-to-all(bf16[8,80,256]{2,1,0:T(8,128)(2,1)S(1)} %shard_map.73), channel_id=1, replica_groups=mesh['groups'=2,'tm'=8,'height'=2] {'tm'}, dimensions={0} | all-to-all | bytes 655360 | tf_op jit(solution)/shard_map/all_to_all | solution.py:232
  19.2 0.2 shard_map.74
  19.5 0.1 collective-permute-start
  19.5 0.0 copy-done
  19.5 2.1 %shard_map.75 = (f32[8,4,16,256]{3,2,1,0:T(8,128)S(1)}, f32[128,128]{1,0:T(8,128)S(1)}, bf16[256,256]{1,0:T(8,128)(2,1)S(1)}, bf16[256,256]{1,0:T(8,128)(2,1)S(1...) custom-call(bf16[8,80,256]{2,1,0:T(8,128)(2,1)S(1)} %all_to_all.10.video, s32[16]{0:T(128)} %ids_far.1, ...), custom_call_target="tpu_custom_call" | custom-call | tf_op jit(solution)/shard_map/pallas_call | solution.py:281
  21.7 0.0 collective-permute-done.edge
  21.7 2.1 %shard_map.76 = bf16[8,64,256]{2,1,0:T(8,128)(2,1)S(1)} custom-call(bf16[10,16,768]{2,1,0:T(8,128)(2,1)S(1)} %collective-permute-done.edge, f32[8,4,16,256]{3,2,1,0:T(8,128)S(1)} %get-tuple-element.11.given, f32[128,128]{1,0:T(8,128)S(1)} %get-tuple-element.12.bias, bf16[3,3,3,256,256]{4,3,2,1,0:T(8,128)(2,1)S(1)} %copy-done, ...), custom_call_target="tpu_custom_call" | custom-call | tf_op jit(solution)/shard_map/pallas_call | solution.py:299
  23.7 12.4 %all_to_all.11 = bf16[8,64,256]{2,1,0:T(8,128)(2,1)S(1)} all-to-all(bf16[8,64,256]{2,1,0:T(8,128)(2,1)S(1)} %shard_map.76), channel_id=1, replica_groups=mesh['groups'=2,'tm'=8,'height'=2] {'tm'}, dimensions={0} | all-to-all | bytes 524288 | tf_op jit(solution)/shard_map/all_to_all | solution.py:232
  36.1 0.7 %copy.8 = bf16[8,8,8,256]{3,2,1,0:T(8,128)(2,1)} copy(bf16[8,8,8,256]{3,2,0,1:T(8,128)(2,1)S(1)} %bitcast.4) | data formatting | bytes 524288 | tf_op jit(solution)/shard_map/transpose | solution.py:308
Async XLA Ops:
  0.0 19.5 %copy-start = (bf16[3,3,3,256,256]{4,3,2,1,0:T(8,128)(2,1)S(1)}, bf16[3,3,3,256,256]{4,3,2,1,0:T(8,128)(2,1)}, u32[]{:S(2)}) copy-start(bf16[3,3,3,256,256]{4,3,2,1,0:T(8,128)(2,1)} %conv_weight.1) | copy-start | bytes 10616836
  19.5 2.2 %collective-permute-start = (bf16[10,16,768]{2,1,0:T(8,128)(2,1)S(1)}, bf16[10,16,768]{2,1,0:T(8,128)(2,1)S(1)}, u32[]{:S(2)}, u32[]{:S(2)}) collective-permute-start(bf16[10,16,768]{2,1,0:T(8,128)(2,1)S(1)} %shard_map.74), channel_id=1, source_target_pairs={{0,1},{1,0},{2,3},{3,2},{4,5},{5,4},{6,7},{7,6},{8,9},{9,8},{10,11... | collective-permute-start | bytes 737288 | tf_op jit(solution)/shard_map/ppermute | solution.py:278
